TPU v7x, 32 devices: a whole 2x2x4 slice. The times are simulated.
32 devices in a mesh: energy: 4 (over y, x), momentum: 2 (over core), phonon: 4 (over z).
Axes of the slice: x: 2, y: 2, z: 4, core: 2. Of those that a mesh axis runs over, the one named last changes fastest.
Arguments:
- g_less: bfloat16 [8, 2, 2, 144, 2176], P('energy', 'momentum', None, None, 'phonon'), may hold values from -6 to 6
- g_great: bfloat16 [8, 2, 2, 144, 2176], P('energy', 'momentum', None, None, 'phonon'), may hold values from -6 to 6
- d_less: float32 [64, 2, 9, 17, 128], P(('energy', 'momentum', 'phonon')), may hold values from -2 to 2
- d_ret: bfloat16 [64, 2, 384, 384], P(('energy', 'momentum', 'phonon')), may hold values from -0.21875 to 0.21875
- neighbours: int32 [17, 128], replicated, may hold values from 0 to 127
- bond_dirs: float32 [3, 17, 128], replicated, may hold values from -4 to 4
- energy_offset: int32 [64], replicated, may hold values from 1 to 4
- momentum_offset: int32 [64], replicated, may hold values from 0 to 1
- absorb: float32 [64], replicated, may hold values from 0.1 to 0.9
Outputs:
- self_energy: bfloat16 [8, 2, 2, 144, 2176], P('energy', 'momentum', None, None, 'phonon')
- d_next: bfloat16 [64, 2, 384, 384], P(('energy', 'momentum', 'phonon'))
Inputs may be any that keep to these rules, and one draw needn't show every extreme that they name: `neighbours`: atoms of the window.
All inputs are finite; a program needn't handle non-finite values.
Results may differ from a plain program's by a relative error of at most 0.008.
Values may be sent and summed in bfloat16 or wider, within the bound.
No kernel may reach another device: no remote copies, remote signals or barrier semaphores. Data moves between devices by JAX's collectives and lax.ppermute only.
A program may use at most 128 MiB of HBM per device.

v0:
```python
import jax
import jax.numpy as jnp
from jax import lax
from jax.sharding import PartitionSpec as P

ORB = 12
REACH = 4


HIGH = lax.Precision.HIGHEST


def shifted_2(block, axis, distance):
    devices = range(lax.axis_size(axis))
    route = [(i - distance, i) for i in devices if i - distance in devices]
    return lax.ppermute(block, axis, route)


def scaled_blocks(weights, blocks):
    real_w = weights[None, :, :, 0, None, :]
    imag_w = weights[None, :, :, 1, None, :]
    real_b = blocks[:, None, :, 0].astype(jnp.float32)
    imag_b = blocks[:, None, :, 1].astype(jnp.float32)
    real_part = jnp.sum(real_w * real_b - imag_w * imag_b, axis=2)
    imag_part = jnp.sum(real_w * imag_b + imag_w * real_b, axis=2)
    return jnp.stack([real_part, imag_part], axis=2)


def inner_sums(local_blocks, shifted):
    local_real = local_blocks[:, :, 0].astype(jnp.float32)[:, :, None]
    local_imag = local_blocks[:, :, 1].astype(jnp.float32)[:, :, None]
    other_real = shifted[:, :, 0].astype(jnp.float32)[:, None]
    other_imag = shifted[:, :, 1].astype(jnp.float32)[:, None]
    real_sum = jnp.sum(local_real * other_real + local_imag * other_imag, axis=(0, 3))
    imag_sum = jnp.sum(local_imag * other_real - local_real * other_imag, axis=(0, 3))
    return jnp.stack([real_sum, imag_sum], axis=2)


def times_adjoint(left, right):
    return jnp.einsum("mab,mcb->mac", left, right, preferred_element_type=jnp.float32)


def times_plain(left, right):
    return jnp.einsum("mab,mbc->mac", left, right, preferred_element_type=jnp.float32)


def local(
    g_less, g_great, d_less, d_ret, neighbours, bond_dirs, energy_offset, momentum_offset, absorb
):
    energies = g_less.shape[0]
    momenta_here = g_less.shape[1]
    local_width = g_less.shape[4]
    bonds = d_less.shape[3]
    whole_atoms = d_less.shape[4]
    atom_share = local_width // bonds
    all_momenta = momenta_here * lax.axis_size("momentum")
    all_energies = energies * lax.axis_size("energy")
    modes_here = d_less.shape[0]
    order = d_ret.shape[2]
    classes = REACH * all_momenta
    energy_rank = lax.axis_index("energy")
    momentum_rank = lax.axis_index("momentum")
    phonon_rank = lax.axis_index("phonon")
    span = -(-REACH // energies)
    lower_steps = list(range(span, 0, -1))
    both_steps = lower_steps + list(range(-1, -span - 1, -1))
    label = (energy_offset - 1) * all_momenta + momentum_offset
    table = (label[:, None] == jnp.arange(classes, dtype=jnp.int32)[None, :]).astype(jnp.float32)
    soaked = table * absorb[:, None]
    pair_cube = bond_dirs[:, None] * bond_dirs[None, :]
    pair = pair_cube.reshape((9,) + bond_dirs.shape[1:])
    coupling = jnp.sum(d_less * pair[None, None], axis=2)
    first_mode = (
        (energy_rank * lax.axis_size("momentum") + momentum_rank) * lax.axis_size("phonon")
        + phonon_rank
    ) * modes_here
    own_table = lax.dynamic_slice_in_dim(table, first_mode, modes_here, 0)
    spread = lax.all_to_all(
        coupling.astype(jnp.bfloat16), "phonon", split_axis=3, concat_axis=0, tiled=True
    ).astype(coupling.dtype)
    blank = jnp.zeros((classes, 2 * bonds * atom_share), jnp.float32)
    piece = lax.all_gather(
        spread.astype(jnp.bfloat16), ("energy", "momentum"), axis=0, tiled=True
    ).astype(jnp.float32)
    rows = piece.shape[0]
    flat_piece = piece.reshape(rows, -1)
    emitted = blank + jnp.einsum("mc,mx->cx", table, flat_piece, precision=HIGH)
    absorbed = blank + jnp.einsum("mc,mx->cx", soaked, flat_piece, precision=HIGH)
    emitted = emitted.reshape(classes, 2, bonds, atom_share)
    absorbed = absorbed.reshape(classes, 2, bonds, atom_share)
    emit_table = emitted.transpose(0, 1, 3, 2).reshape(REACH, all_momenta, 2, local_width)
    soak_table = absorbed.transpose(0, 1, 3, 2).reshape(REACH, all_momenta, 2, local_width)
    moved = [shifted_2(g_less, "energy", step) for step in both_steps]
    lower = jnp.concatenate(moved[:span], axis=0)
    upper = jnp.concatenate(moved[span:], axis=0)
    lesser_rimmed = jnp.concatenate([lower, g_less, upper], axis=0)
    greater_moved = [shifted_2(g_great, "energy", step) for step in lower_steps]
    greater_rim = jnp.concatenate(greater_moved, axis=0)
    greater_rimmed = jnp.concatenate([greater_rim, g_great], axis=0)
    lesser_wide, greater_wide = (
        lax.all_gather(lesser_rimmed, "momentum", axis=1, tiled=True),
        lax.all_gather(greater_rimmed, "momentum", axis=1, tiled=True),
    )
    here_moment = momentum_rank * momenta_here + jnp.arange(momenta_here, dtype=jnp.int32)
    every_moment = jnp.arange(all_momenta, dtype=jnp.int32)
    behind = (here_moment[:, None] - every_moment[None, :]) % all_momenta
    ahead = (every_moment[None, :] - here_moment[:, None]) % all_momenta
    pick_behind = (behind[:, :, None] == every_moment[None, None, :]).astype(jnp.float32)
    pick_ahead = (ahead[:, :, None] == every_moment[None, None, :]).astype(jnp.float32)
    total = jnp.zeros(g_less.shape, jnp.float32)
    polar_parts = []
    for energy_step in range(1, REACH + 1):
        below = lesser_wide[REACH - energy_step : REACH - energy_step + energies]
        above = lesser_wide[REACH + energy_step : REACH + energy_step + energies]
        weight_below = jnp.einsum(
            "lkq,qzx->lkzx", pick_behind, emit_table[energy_step - 1], precision=HIGH
        )
        weight_above = jnp.einsum(
            "lkq,qzx->lkzx", pick_ahead, soak_table[energy_step - 1], precision=HIGH
        )
        total = total + scaled_blocks(weight_below, below) + scaled_blocks(weight_above, above)
        earlier = greater_wide[REACH - energy_step : REACH - energy_step + energies]
        pairs = inner_sums(g_less, earlier)
        polar_parts.append(jnp.einsum("lkq,lkzx->qzx", pick_behind, pairs, precision=HIGH))
    self_energy = total.astype(jnp.bfloat16)
    scale = float(all_energies * all_momenta * ORB * ORB) ** (-0.5)
    polar_local = jnp.stack(polar_parts).reshape(classes, 2, local_width) * scale
    polar_summed = lax.psum(polar_local, ("energy", "momentum"))
    polar_full = lax.all_gather(polar_summed, "phonon", axis=2, tiled=True)
    own_polar = jnp.einsum("mc,czx->mzx", own_table, polar_full, precision=HIGH)
    own_polar = own_polar.reshape(modes_here, 2, whole_atoms, bonds).transpose(0, 1, 3, 2)
    link = (
        neighbours[:, :, None] == jnp.arange(whole_atoms, dtype=jnp.int32)[None, None, :]
    ).astype(jnp.float32)
    weighted = pair_cube[None, None] * own_polar[:, :, None, None]
    dense = jnp.einsum("mzijna,nab->mziajb", weighted, link, precision=HIGH)
    dense = dense.reshape(modes_here, 2, order, order).astype(jnp.bfloat16)
    dense_re, dense_im = (dense[:, 0], dense[:, 1])
    ret_re, ret_im = (d_ret[:, 0], d_ret[:, 1])
    half_re = (times_adjoint(dense_re, ret_re) + times_adjoint(dense_im, ret_im)).astype(
        jnp.bfloat16
    )
    half_im = (times_adjoint(dense_im, ret_re) - times_adjoint(dense_re, ret_im)).astype(
        jnp.bfloat16
    )
    next_re = times_plain(ret_re, half_re) - times_plain(ret_im, half_im)
    next_im = times_plain(ret_re, half_im) + times_plain(ret_im, half_re)
    d_next = jnp.stack([next_re, next_im], axis=1).astype(jnp.bfloat16)
    return (self_energy, d_next)


def solution(mesh):
    in_specs = (
        P("energy", "momentum", None, None, "phonon"),
        P("energy", "momentum", None, None, "phonon"),
        P(("energy", "momentum", "phonon"), None, None, None, None),
        P(("energy", "momentum", "phonon"), None, None, None),
        P(),
        P(),
        P(),
        P(),
        P(),
    )
    out_specs = (
        P("energy", "momentum", None, None, "phonon"),
        P(("energy", "momentum", "phonon"), None, None, None),
    )
    return jax.shard_map(local, mesh=mesh, in_specs=in_specs, out_specs=out_specs, check_vma=False)
```

profile of v0, /device:TPU:0, one launch (start us, length us, event | category | flops | bytes accessed | tf_op | source)
XLA Modules:
  0.0 220.1 jit_solution(10038464538915616396)
XLA Ops:
  7.2 4.9 %collective-permute-start.5 = (bf16[2,1,2,144,544]{4,3,2,1,0:T(8,128)(2,1)}, bf16[2,1,2,144,544]{4,3,2,1,0:T(8,128)(2,1)S(1)}, u32[]{:S(2)}, u32[]{:S(2)}) collective-permute-start(bf16[2,1,2,144,544]{4,3,2,1,0:T(8,128)(2,1)} %param.10), channel_id=1, source_target_pairs={{0,8},{8,16},{16,24},{1,9},{9,17},{17,25},{2,10},{10,18},{18,26},{... | collective-permute-start | bytes 1880072 | tf_op jit(solution)/shard_map/ppermute | solution.py:16
  12.1 3.4 %collective-permute-start.4 = (bf16[2,1,2,144,544]{4,3,2,1,0:T(8,128)(2,1)}, bf16[2,1,2,144,544]{4,3,2,1,0:T(8,128)(2,1)S(1)}, u32[]{:S(2)}, u32[]{:S(2)}) collective-permute-start(bf16[2,1,2,144,544]{4,3,2,1,0:T(8,128)(2,1)} %param.10), channel_id=1, source_target_pairs={{0,16},{8,24},{1,17},{9,25},{2,18},{10,26},{3,19},{11,27},{4,20},{... | collective-permute-start | bytes 1880072 | tf_op jit(solution)/shard_map/ppermute | solution.py:16
  15.5 12.6 %collective-permute-done.5 = bf16[2,1,2,144,544]{4,3,2,1,0:T(8,128)(2,1)S(1)} collective-permute-done((bf16[2,1,2,144,544]{4,3,2,1,0:T(8,128)(2,1)}, bf16[2,1,2,144,544]{4,3,2,1,0:T(8,128)(2,1)S(1)}, u32[]{:S(2)}, u32[]{:S(2)}) %collective-permute-start.5) | collective-permute-done | bytes 626720 | tf_op jit(solution)/shard_map/ppermute | solution.py:16
  28.1 16.7 %collective-permute-done.4 = bf16[2,1,2,144,544]{4,3,2,1,0:T(8,128)(2,1)S(1)} collective-permute-done((bf16[2,1,2,144,544]{4,3,2,1,0:T(8,128)(2,1)}, bf16[2,1,2,144,544]{4,3,2,1,0:T(8,128)(2,1)S(1)}, u32[]{:S(2)}, u32[]{:S(2)}) %collective-permute-start.4) | collective-permute-done | bytes 626720 | tf_op jit(solution)/shard_map/ppermute | solution.py:16
  44.8 2.8 %pad_maximum_fusion = bf16[6,1,2,144,544]{4,3,2,1,0:T(8,128)(2,1)} fusion(bf16[2,1,2,144,544]{4,3,2,1,0:T(8,128)(2,1)} %param.10, bf16[2,1,2,144,544]{4,3,2,1,0:T(8,128)(2,1)S(1)} %collective-permute-done.5, bf16[2,1,2,144,544]{4,3,2,1,0:T(8,128)(2,1)S(1)} %collective-permute-done.4), kind=kLoop, calls=%fused_computation.4 | loop fusion | flops 1880064 | bytes 3760128 | tf_op jit(solution)/shard_map/concatenate | solution.py:99
  47.7 1.1 copy-done.1
  48.8 5.3 %collective-permute-start = (bf16[2,1,2,144,544]{4,3,2,1,0:T(8,128)(2,1)S(1)}, bf16[2,1,2,144,544]{4,3,2,1,0:T(8,128)(2,1)}, u32[]{:S(2)}, u32[]{:S(2)}) collective-permute-start(bf16[2,1,2,144,544]{4,3,2,1,0:T(8,128)(2,1)S(1)} %copy-done.1), channel_id=1, source_target_pairs={{0,16},{8,24},{1,17},{9,25},{2,18},{10,26},{3,19},{11,27},{4,20},{... | collective-permute-start | bytes 1880072 | tf_op jit(solution)/shard_map/ppermute | solution.py:16
  54.1 2.2 collective-permute-start.1
  56.2 1.3 collective-permute-start.2
  57.5 1.3 collective-permute-start.3
  58.8 0.2 copy.276
  59.0 0.2 broadcast_multiply_fusion
  59.2 0.3 copy.278
  59.7 0.1 copy.279
  59.8 0.8 reshape.1546
  60.6 4.9 %all-to-all-start = ((bf16[4,2,1088]{2,1,0:T(2,128)(2,1)}), bf16[4,2,1088]{2,1,0:T(2,128)(2,1)S(1)}, u32[]{:S(2)}, u32[]{:S(2)}) async-start(bf16[4,2,1088]{2,1,0:T(2,128)(2,1)} %reshape.1546), calls=%async_computation | async-start | bytes 36864 | tf_op jit(solution)/shard_map/all_to_all | solution.py:78
  65.9 5.3 %all-to-all-done = bf16[4,2,1088]{2,1,0:T(2,128)(2,1)S(1)} async-done(((bf16[4,2,1088]{2,1,0:T(2,128)(2,1)}), bf16[4,2,1088]{2,1,0:T(2,128)(2,1)S(1)}, u32[]{:S(2)}, u32[]{:S(2)}) %all-to-all-start) | async-done | bytes 17440 | tf_op jit(solution)/shard_map/all_to_all | solution.py:78
  71.1 0.3 reshape.1547
  71.4 0.2 copy.352
  71.6 29.6 %all_gather.12 = bf16[64,2,17,32]{3,0,2,1:T(8,128)(2,1)} all-gather(bf16[8,2,17,32]{3,0,2,1:T(8,128)(2,1)S(1)} %bitcast.476), channel_id=1, replica_groups=mesh['energy'=4,'momentum'=2,'phonon'=4] {'energy','momentum'}, dimensions={0}, use_global_device_ids=true | all-gather | bytes 156672 | tf_op jit(solution)/shard_map/all_gather | solution.py:82
  101.3 1.3 copy.282
  102.6 1.3 convolution_bitcast_fusion.1
  103.9 0.6 convolution_bitcast_fusion
  105.0 0.2 convolution_bitcast_fusion.13
  105.2 0.2 convolution_bitcast_fusion.9
  106.7 0.2 convolution_bitcast_fusion.12
  106.9 0.2 convolution_bitcast_fusion.10
  107.2 2.1 constant_dynamic-update-slice_fusion.4
  109.2 2.1 constant_dynamic-update-slice_fusion.3
  111.3 1.0 constant_dynamic-update-slice_fusion.2
  112.2 2.0 constant_dynamic-update-slice_fusion.1
  114.3 2.1 constant_dynamic-update-slice_fusion
  116.4 0.2 convolution_bitcast_fusion.11
  116.6 0.2 convolution_bitcast_fusion.6
  116.8 0.2 convolution_bitcast_fusion.7
  117.0 0.2 convolution_bitcast_fusion.8
  117.4 4.0 %fusion.49 = (f32[2,544]{1,0:T(2,128)S(1)}, f32[2,544]{1,0:T(2,128)S(1)}, f32[2,544]{1,0:T(2,128)S(1)}, f32[2,544]{1,0:T(2,128)S(1)}, f32[2,544]{1,0:T(2,128)S(1...) fusion(f32[2,144,544]{2,1,0:T(8,128)S(1)} %get-tuple-element.49, ...), kind=kLoop, calls=%fused_computation.92 | loop fusion | flops 12525056 | bytes 6301696 | tf_op jit(solution)/shard_map/reduce_sum | solution.py:34
  121.3 0.3 convolution_bitcast_fusion.2
  121.6 0.3 convolution_bitcast_fusion.3
  121.9 0.3 convolution_bitcast_fusion.4
  122.2 0.3 convolution_bitcast_fusion.5
  122.6 24.0 %psum.7 = f32[8,2,544]{2,1,0:T(2,128)S(1)} all-reduce(f32[8,2,544]{2,1,0:T(2,128)S(1)} %bitcast.478), channel_id=1, replica_groups=mesh['energy'=4,'momentum'=2,'phonon'=4] {'energy','momentum'}, use_global_device_ids=true, to_apply=%region_25.26 | all-reduce | flops 8704 | bytes 69632 | tf_op jit(solution)/shard_map/psum | solution.py:128
  146.6 0.3 copy.326
  146.9 38.0 %all_gather.15 = f32[8,2,2176]{0,1,2:T(2,128)S(1)} all-gather(f32[8,2,544]{0,1,2:T(2,128)S(1)} %copy.326), channel_id=1, replica_groups=mesh['energy'=4,'momentum'=2,'phonon'=4] {'phonon'}, dimensions={2}, use_global_device_ids=true | all-gather | bytes 174080 | tf_op jit(solution)/shard_map/all_gather | solution.py:129
  184.8 1.2 fusion.2
  186.1 0.2 reshape.1500
  186.3 0.2 copy.329
  186.5 4.0 %fusion.11 = bf16[2,2,3,128,3,128]{5,4,2,1,0,3:T(4,128)(2,1)S(1)} fusion(f32[2,2,17,128]{2,1,0,3:T(2,128)S(1)} %copy.329, f32[3,3,17,128]{2,1,0,3:T(4,128)S(1)} %broadcast_multiply_fusion, s32[17,128]{0,1:T(8,128)S(1)} %copy.309), kind=kOutput, calls=%fused_computation.58 | convolution fusion | flops 121270784 | bytes 1301504 | tf_op jit(solution)/shard_map/mzijna,nab->mziajb/dot_general | solution.py:136
  190.5 2.0 copy.378
  192.5 3.5 %reshape.1545 = bf16[2,2,384,384]{3,2,0,1:T(8,128)(2,1)S(1)} reshape(bf16[2,2,3,128,3,128]{5,4,3,2,0,1:T(4,128)(2,1)} %copy.378) | data formatting | bytes 2359296 | tf_op jit(solution)/shard_map/convert_element_type | solution.py:137
  196.0 0.5 fusion.84
  196.5 0.5 fusion.88
  197.1 0.5 fusion.72
  197.6 0.6 fusion.82
  198.2 0.5 fusion.71
  198.8 0.6 fusion.75
  199.4 0.6 fusion.86
  200.0 0.6 fusion.76
  200.7 0.1 pad_maximum_fusion.1
  200.8 1.5 copy.339
  202.3 3.4 %fusion.21 = (f32[2,144,544]{2,1,0:T(8,128)S(1)}, f32[2,144,544]{2,1,0:T(8,128)S(1)}, f32[2,144,544]{2,1,0:T(8,128)S(1)}, f32[2,144,544]{2,1,0:T(8,128)S(1)}) fusion(f32[2,544]{1,0:T(2,128)S(1)} %get-tuple-element.73, f32[2,544]{1,0:T(2,128)S(1)} %get-tuple-element.72, bf16[10,2,2,144,544]{4,3,2,1,0:T(8,128)(2,1)} %all-gather.3.cloned.1.call-done, ...), kind=kLoop, calls=%fused_computation.64 | loop fusion | flops 5640192 | bytes 5030912 | tf_op jit(solution)/shard_map/reduce_sum | solution.py:24
  205.6 4.6 %fusion.33 = (f32[2,144,544]{2,1,0:T(8,128)S(1)}, f32[2,144,544]{2,1,0:T(8,128)S(1)}, f32[2,144,544]{2,1,0:T(8,128)S(1)}, f32[2,144,544]{2,1,0:T(8,128)S(1)}, f3...) fusion(f32[2,544]{1,0:T(2,128)S(1)} %get-tuple-element.69, f32[2,544]{1,0:T(2,128)S(1)} %get-tuple-element.68, ...), kind=kLoop, calls=%fused_computation.76 | loop fusion | flops 8460288 | bytes 7546368 | tf_op jit(solution)/shard_map/reduce_sum | solution.py:24
  210.3 1.5 fusion.45
  211.9 1.4 fusion.70
  (70 shorter events, 2.7 us)
Async XLA Ops:
  7.2 110.2 %all-gather.5.cloned.1.call-start = ((), (), s32[]{:S(2)}) async-start(), calls=%async_computation.2 | async-start | bytes 6635520 | tf_op jit(solution)/shard_map/all_gather | solution.py:102
  7.2 20.9 %collective-permute-start.5 = (bf16[2,1,2,144,544]{4,3,2,1,0:T(8,128)(2,1)}, bf16[2,1,2,144,544]{4,3,2,1,0:T(8,128)(2,1)S(1)}, u32[]{:S(2)}, u32[]{:S(2)}) collective-permute-start(bf16[2,1,2,144,544]{4,3,2,1,0:T(8,128)(2,1)} %param.10), channel_id=1, source_target_pairs={{0,8},{8,16},{16,24},{1,9},{9,17},{17,25},{2,10},{10,18},{18,26},{... | collective-permute-start | bytes 1880072 | tf_op jit(solution)/shard_map/ppermute | solution.py:16
  12.1 32.7 %collective-permute-start.4 = (bf16[2,1,2,144,544]{4,3,2,1,0:T(8,128)(2,1)}, bf16[2,1,2,144,544]{4,3,2,1,0:T(8,128)(2,1)S(1)}, u32[]{:S(2)}, u32[]{:S(2)}) collective-permute-start(bf16[2,1,2,144,544]{4,3,2,1,0:T(8,128)(2,1)} %param.10), channel_id=1, source_target_pairs={{0,16},{8,24},{1,17},{9,25},{2,18},{10,26},{3,19},{11,27},{4,20},{... | collective-permute-start | bytes 1880072 | tf_op jit(solution)/shard_map/ppermute | solution.py:16
  47.6 1.1 copy-start.1
  47.6 11.2 %copy-start.3 = (f32[3,17,128]{2,0,1:T(4,128)S(1)}, f32[3,17,128]{2,0,1:T(4,128)}, u32[]{:S(2)}) copy-start(f32[3,17,128]{2,0,1:T(4,128)} %param.14) | copy-start | bytes 78340
  48.8 10.8 %copy-start.2 = (f32[2,2,9,17,128]{4,1,3,2,0:T(2,128)S(1)}, f32[2,2,9,17,128]{4,1,3,2,0:T(2,128)}, u32[]{:S(2)}) copy-start(f32[2,2,9,17,128]{4,1,3,2,0:T(2,128)} %param.11) | copy-start | bytes 940036
  48.8 58.4 %collective-permute-start = (bf16[2,1,2,144,544]{4,3,2,1,0:T(8,128)(2,1)S(1)}, bf16[2,1,2,144,544]{4,3,2,1,0:T(8,128)(2,1)}, u32[]{:S(2)}, u32[]{:S(2)}) collective-permute-start(bf16[2,1,2,144,544]{4,3,2,1,0:T(8,128)(2,1)S(1)} %copy-done.1), channel_id=1, source_target_pairs={{0,16},{8,24},{1,17},{9,25},{2,18},{10,26},{3,19},{11,27},{4,20},{... | collective-permute-start | bytes 1880072 | tf_op jit(solution)/shard_map/ppermute | solution.py:16
  54.1 55.1 %collective-permute-start.1 = (bf16[2,1,2,144,544]{4,3,2,1,0:T(8,128)(2,1)S(1)}, bf16[2,1,2,144,544]{4,3,2,1,0:T(8,128)(2,1)}, u32[]{:S(2)}, u32[]{:S(2)}) collective-permute-start(bf16[2,1,2,144,544]{4,3,2,1,0:T(8,128)(2,1)S(1)} %copy-done.1), channel_id=1, source_target_pairs={{0,8},{8,16},{16,24},{1,9},{9,17},{17,25},{2,10},{10,18},{18,26},{... | collective-permute-start | bytes 1880072 | tf_op jit(solution)/shard_map/ppermute | solution.py:16
  56.2 56.0 %collective-permute-start.2 = (bf16[2,1,2,144,544]{4,3,2,1,0:T(8,128)(2,1)S(1)}, bf16[2,1,2,144,544]{4,3,2,1,0:T(8,128)(2,1)}, u32[]{:S(2)}, u32[]{:S(2)}) collective-permute-start(bf16[2,1,2,144,544]{4,3,2,1,0:T(8,128)(2,1)S(1)} %copy-done.1), channel_id=1, source_target_pairs={{8,0},{16,8},{24,16},{9,1},{17,9},{25,17},{10,2},{18,10},{26,18},{... | collective-permute-start | bytes 1880072 | tf_op jit(solution)/shard_map/ppermute | solution.py:16
  57.5 56.8 %collective-permute-start.3 = (bf16[2,1,2,144,544]{4,3,2,1,0:T(8,128)(2,1)S(1)}, bf16[2,1,2,144,544]{4,3,2,1,0:T(8,128)(2,1)}, u32[]{:S(2)}, u32[]{:S(2)}) collective-permute-start(bf16[2,1,2,144,544]{4,3,2,1,0:T(8,128)(2,1)S(1)} %copy-done.1), channel_id=1, source_target_pairs={{16,0},{24,8},{17,1},{25,9},{18,2},{26,10},{19,3},{27,11},{20,4},{... | collective-permute-start | bytes 1880072 | tf_op jit(solution)/shard_map/ppermute | solution.py:16
  59.0 6.5 %copy-start.6 = (s32[64]{0:T(128)S(1)}, s32[64]{0:T(128)}, u32[]{:S(2)}) copy-start(s32[64]{0:T(128)} %param.16) | copy-start | bytes 772
  59.0 6.5 %copy-start.7 = (s32[64]{0:T(128)S(1)}, s32[64]{0:T(128)}, u32[]{:S(2)}) copy-start(s32[64]{0:T(128)} %param.15) | copy-start | bytes 772
  59.5 6.2 %copy-start.4 = (s32[17,128]{1,0:T(8,128)S(1)}, s32[17,128]{1,0:T(8,128)}, u32[]{:S(2)}) copy-start(s32[17,128]{1,0:T(8,128)} %param.13) | copy-start | bytes 26116
  60.6 10.5 %all-to-all-start = ((bf16[4,2,1088]{2,1,0:T(2,128)(2,1)}), bf16[4,2,1088]{2,1,0:T(2,128)(2,1)S(1)}, u32[]{:S(2)}, u32[]{:S(2)}) async-start(bf16[4,2,1088]{2,1,0:T(2,128)(2,1)} %reshape.1546), calls=%async_computation | async-start | bytes 36864 | tf_op jit(solution)/shard_map/all_to_all | solution.py:78
  65.5 136.7 %all-gather.3.cloned.1.call-start = ((), (), s32[]{:S(2)}) async-start(), calls=%async_computation.1 | async-start | bytes 11059200 | tf_op jit(solution)/shard_map/all_gather | solution.py:101
  65.7 36.8 %copy-start.5 = (f32[64]{0:T(128)S(1)}, f32[64]{0:T(128)}, u32[]{:S(2)}) copy-start(f32[64]{0:T(128)} %param.17) | copy-start | bytes 772
  192.5 3.5 %copy-start = (bf16[2,2,384,384]{3,2,1,0:T(8,128)(2,1)S(1)}, bf16[2,2,384,384]{3,2,1,0:T(8,128)(2,1)}, u32[]{:S(2)}) copy-start(bf16[2,2,384,384]{3,2,1,0:T(8,128)(2,1)} %param.12) | copy-start | bytes 3538948
  202.3 8.0 %slice-start = ((s8[7372800]{0:T(1024)(128)(4,1)}), s8[4194304]{0:T(1024)(128)(4,1)S(1)}, s32[]{:S(2)}) async-start(s8[7372800]{0:T(1024)(128)(4,1)} %bitcast.454), calls=%async_computation.3 | async-start | bytes 8388608
  205.6 4.7 %slice-start.1 = ((s8[7372800]{0:T(1024)(128)(4,1)}), s8[3178496]{0:T(1024)(128)(4,1)S(1)}, s32[]{:S(2)}) async-start(s8[7372800]{0:T(1024)(128)(4,1)} %bitcast.454), calls=%async_computation.4 | async-start | bytes 6356992
Sparse Core Ops, SparseCore 0:
  47.8 15.1 all-gather.4
  116.5 18.9 all-gather.2
where the time goes:
time: 221 us; the launch traced here: 220 us
  blocking collectives  91.6 us (41%)
  waiting for transfers between devices  34.6 us (16%)
  starting transfers between devices  23.3 us (11%)
  local copies, waits for them, and re-layouts  23.2 us (10%)
  other arithmetic  18.4 us (8%)
  between operations  14.6 us (7%)
  matrix products  14.5 us (7%)
    all_gather x1, blocking collectives, local(): polar_full = lax.all_gather(polar_summed, 'phonon', axis=2, tiled=True)  38 us
    all_gather x1, blocking collectives, local(): lax.all_gather(spread.astype(jnp.bfloat16), ('energy', 'momentum'), axis=...  29.6 us
    ppermute x6, waiting for transfers between devices, shifted_2(): return lax.ppermute(block, axis, route)  29.3 us
    psum x1, blocking collectives, local(): polar_summed = lax.psum(polar_local, ('energy', 'momentum'))  24 us
    ppermute x6, starting transfers between devices, shifted_2(): return lax.ppermute(block, axis, route)  18.4 us
    unnamed x29, local copies, waits for them, and re-layouts  11.1 us
    reduce_sum x3, other arithmetic, scaled_blocks(): real_part = jnp.sum(real_w * real_b - imag_w * imag_b, axis=2)  9.54 us
    convert_element_type x2, local copies, waits for them, and re-layouts, local(): dense = dense.reshape(modes_here, 2, order, order).astype(jnp.bfloat16)  5.41 us
  transfers between devices with their start and end apart: 9, of which 3 were waited for; matrix products, arithmetic and copies ran while one was open for 19% of the time, Pallas kernels for 0%

commit v1 on v0

--- a/solution.py
+++ b/solution.py
@@ -1,10 +1,16 @@
+import functools
+
 import jax
 import jax.numpy as jnp
+import numpy as np
 from jax import lax
+from jax.experimental import pallas as pl
+from jax.experimental.pallas import tpu as pltpu
 from jax.sharding import PartitionSpec as P
 
 ORB = 12
 REACH = 4
+LANES = 128
 
 
 HIGH = lax.Precision.HIGHEST
@@ -44,7 +50,7 @@
     return jnp.einsum("mab,mbc->mac", left, right, preferred_element_type=jnp.float32)
 
 
-def local(
+def general(
     g_less, g_great, d_less, d_ret, neighbours, bond_dirs, energy_offset, momentum_offset, absorb
 ):
     energies = g_less.shape[0]
@@ -149,6 +155,456 @@
     return (self_energy, d_next)
 
 
+GROUP = ("energy", "momentum")
+EVERY = ("energy", "momentum", "phonon")
+F32 = jnp.float32
+BF16 = jnp.bfloat16
+
+
+class Plan:
+    def __init__(self, g_shape, d_shape, ret_shape, n_energy, n_momentum, n_phonon):
+        self.energies, self.momenta, _, self.entries, self.width = g_shape
+        self.modes, _, _, self.bonds, self.atoms = d_shape
+        self.order = ret_shape[2]
+        self.n_momentum = n_momentum
+        self.n_phonon = n_phonon
+        self.group = n_energy * n_momentum
+        self.devices = self.group * n_phonon
+        self.all_energies = self.energies * n_energy
+        self.all_momenta = self.momenta * n_momentum
+        self.classes = REACH * self.all_momenta
+        self.slabs = 2 * self.energies
+        self.tiles = self.width // LANES
+        self.rest = self.width % LANES
+        self.halves = self.group // max(self.tiles, 1)
+        self.rows = self.entries // max(self.halves, 1)
+        self.rest_rows = self.entries // self.group
+        self.main_rows = self.slabs * self.rows
+        self.rest_pad = -(-self.rest_rows // 8) * 8
+        self.message = -(-(self.main_rows + self.rest_pad) // 16) * 16
+        self.tail = self.message - self.main_rows
+        self.held = self.rows + self.rest_pad
+        self.columns = self.width * n_phonon
+
+    def fits(self):
+        return (
+            self.momenta == 1
+            and self.group & (self.group - 1) == 0
+            and self.tiles > 0
+            and self.halves * self.tiles == self.group
+            and self.entries % (8 * self.halves) == 0
+            and self.entries % 16 == 0
+            and self.entries % self.group == 0
+            and self.rest > 0
+            and self.slabs * self.rest == LANES
+            and self.tail >= self.rest_pad
+            and self.modes * 4 <= 8
+            and self.atoms == LANES
+            and self.order == 3 * self.atoms
+            and self.all_energies <= 8
+            and self.all_momenta <= 2
+        )
+
+
+def call(kernel, out_shape, *operands, scratch=(), scalars=0, flops=0, moved=0):
+    smem = pl.BlockSpec(memory_space=pltpu.SMEM)
+    vmem = pl.BlockSpec(memory_space=pltpu.VMEM)
+    specs = [smem] * scalars + [vmem] * (len(operands) - scalars)
+    many = isinstance(out_shape, (list, tuple))
+    return pl.pallas_call(
+        kernel,
+        out_shape=out_shape,
+        in_specs=specs,
+        out_specs=[vmem] * len(out_shape) if many else vmem,
+        scratch_shapes=list(scratch),
+        compiler_params=pltpu.CompilerParams(vmem_limit_bytes=48 * 2**20),
+        cost_estimate=pl.CostEstimate(flops=flops, bytes_accessed=moved, transcendentals=0),
+    )(*operands)
+
+
+def deal_kernel(plan, rank_ref, less_ref, great_ref, *refs):
+    outs, rest_ref = refs[: plan.group], refs[plan.group]
+    rank = rank_ref[0]
+    sources = (less_ref, great_ref)
+    for which, source in enumerate(sources):
+        pieces = [
+            source[e, 0, z, :, plan.tiles * LANES :].astype(F32)
+            for e in range(plan.energies)
+            for z in range(2)
+        ]
+        rest_ref[which, : plan.entries] = jnp.concatenate(pieces, axis=1)
+        rest_ref[which, plan.entries :] = jnp.zeros((plan.tail, LANES), F32)
+    for k in range(plan.group):
+        target = rank ^ k
+        tile = target // plan.halves
+        half = target % plan.halves
+        lanes = pl.ds(pl.multiple_of(tile * LANES, LANES), LANES)
+        for which, source in enumerate(sources):
+            parts = []
+            for e in range(plan.energies):
+                for z in range(2):
+                    whole = source[e, 0, z, :, lanes].astype(F32)
+                    part = whole[: plan.rows]
+                    for other in range(1, plan.halves):
+                        piece = whole[other * plan.rows : (other + 1) * plan.rows]
+                        part = jnp.where(half == other, piece, part)
+                    parts.append(part)
+            parts.append(rest_ref[which, pl.ds(target * plan.rest_rows, plan.tail), :])
+            outs[k][which] = jnp.concatenate(parts, axis=0).astype(BF16)
+
+
+def couple_kernel(plan, less_ref, dirs_ref, mod_ref, out_ref):
+    bonds, width = plan.bonds, plan.width
+    padded = -(-bonds // 8) * 8
+    dirs = dirs_ref[...]
+    rows = []
+    for m in range(plan.modes):
+        for z in range(2):
+            total = jnp.zeros((bonds, plan.atoms), F32)
+            for i in range(3):
+                for j in range(3):
+                    total = total + less_ref[m, z, 3 * i + j] * (dirs[i] * dirs[j])
+            rows.append(jnp.pad(total, ((0, padded - bonds), (0, 0))))
+    stacked = jnp.concatenate(rows, axis=0).astype(BF16)
+    atom = lax.broadcasted_iota(jnp.int32, (plan.atoms, plan.columns), 0)
+    column = lax.broadcasted_iota(jnp.int32, (plan.atoms, plan.columns), 1)
+    inside = column - atom * bonds
+    chosen = jnp.where((inside >= 0) & (inside < bonds), 1.0, 0.0).astype(BF16)
+    spread = jnp.dot(stacked, chosen, preferred_element_type=F32)
+    bond = lax.broadcasted_iota(jnp.int32, (padded, plan.columns), 0)
+    keep = bond == mod_ref[...]
+    lines = []
+    for row in range(2 * plan.modes):
+        piece = spread[row * padded : (row + 1) * padded]
+        lines.append(jnp.sum(jnp.where(keep, piece, 0.0), axis=0, keepdims=True))
+    while len(lines) < 4:
+        lines.append(jnp.zeros((1, plan.columns), F32))
+    flat = jnp.concatenate(lines, axis=0)
+    for p in range(plan.n_phonon):
+        start = p * width
+        rest = flat[:, start + plan.tiles * LANES : start + width]
+        rest = jnp.concatenate([rest, jnp.zeros((4, LANES - plan.rest), F32)], axis=1)
+        for tile in range(plan.tiles):
+            main = flat[:, start + tile * LANES : start + (tile + 1) * LANES]
+            block = jnp.concatenate([main, rest], axis=0)
+            for half in range(plan.halves):
+                out_ref[(tile * plan.halves + half) * plan.n_phonon + p] = block
+
+
+def place_of(plan, source, e, z):
+    energy = plan.energies * (source // plan.n_momentum) + e
+    return (energy * plan.all_momenta + source % plan.n_momentum) * 2 + z
+
+
+def stage_blocks(plan, rank, which, messages, held_ref):
+    row = lax.broadcasted_iota(jnp.int32, (plan.rest_pad, LANES), 0)
+    for k, message in enumerate(messages):
+        source = rank ^ k
+        values = message[which].astype(F32)
+        tail = values[plan.main_rows : plan.main_rows + plan.rest_pad]
+        tail = jnp.where(row < plan.rest_rows, tail, 0.0)
+        for e in range(plan.energies):
+            for z in range(2):
+                slab = 2 * e + z
+                place = place_of(plan, source, e, z)
+                held_ref[place, : plan.rows] = values[slab * plan.rows : (slab + 1) * plan.rows]
+                turned = tail if slab == 0 else pltpu.roll(tail, LANES - slab * plan.rest, 1)
+                held_ref[place, plan.rows :] = turned
+
+
+def polar_kernel(plan, rank_ref, pick_ref, *refs):
+    messages = refs[: plan.group]
+    out_ref, low_ref, high_ref = refs[plan.group :]
+    rank = rank_ref[0]
+    stage_blocks(plan, rank, 0, messages, low_ref)
+    stage_blocks(plan, rank, 1, messages, high_ref)
+    count, momenta = plan.all_energies, plan.all_momenta
+
+    def step(chunk, sums):
+        rows = pl.ds(pl.multiple_of(chunk * 8, 8), 8)
+        sums = list(sums)
+        for energy_step in range(1, REACH + 1):
+            for q in range(momenta):
+                index = ((energy_step - 1) * momenta + q) * 2
+                for energy in range(energy_step, count):
+                    for k in range(momenta):
+                        low = (energy * momenta + k) * 2
+                        high = ((energy - energy_step) * momenta + (k - q) % momenta) * 2
+                        low_re, low_im = low_ref[low, rows], low_ref[low + 1, rows]
+                        high_re, high_im = high_ref[high, rows], high_ref[high + 1, rows]
+                        sums[index] = sums[index] + (low_re * high_re + low_im * high_im)
+                        sums[index + 1] = sums[index + 1] + (low_im * high_re - low_re * high_im)
+        return tuple(sums)
+
+    none = tuple(jnp.zeros((8, LANES), F32) for _ in range(2 * plan.classes))
+    main = lax.fori_loop(0, plan.rows // 8, step, none)
+    rest = lax.fori_loop(plan.rows // 8, plan.held // 8, step, none)
+    scale = float(count * momenta * plan.entries) ** (-0.5)
+    lines = [jnp.sum(part, axis=0, keepdims=True) * scale for part in main + rest]
+    table = jnp.concatenate(lines, axis=0)
+    picked = lax.dot_general(
+        pick_ref[...], table, (((0,), (0,)), ((), ())), precision=HIGH, preferred_element_type=F32
+    )
+    out_ref[...] = picked.reshape(out_ref.shape)
+
+
+def energy_kernel(plan, rank_ref, weigh_ref, coupling_ref, *refs):
+    messages = refs[: plan.group]
+    outs = refs[plan.group : 2 * plan.group]
+    low_ref, sum_ref, weight_ref = refs[2 * plan.group :]
+    rank = rank_ref[0]
+    flat = coupling_ref[...].reshape(plan.devices * 8, LANES)
+    weight_ref[...] = jnp.dot(weigh_ref[...], flat, precision=HIGH, preferred_element_type=F32)
+    stage_blocks(plan, rank, 0, messages, low_ref)
+    count, momenta = plan.all_energies, plan.all_momenta
+
+    def run(base):
+        def step(chunk, carry):
+            rows = pl.ds(pl.multiple_of(chunk * 8, 8), 8)
+            re = [None] * (count * momenta)
+            im = [None] * (count * momenta)
+            for energy_step in range(1, REACH + 1):
+                for q in range(momenta):
+                    index = base + ((energy_step - 1) * momenta + q) * 2
+                    pairs = []
+                    for part, sign in ((0, -1), (1, 1)):
+                        at = index + part * 2 * plan.classes
+                        w_re = jnp.broadcast_to(weight_ref[at : at + 1], (8, LANES))
+                        w_im = jnp.broadcast_to(weight_ref[at + 1 : at + 2], (8, LANES))
+                        pairs.append((sign, w_re, w_im))
+                    for energy in range(count):
+                        for k in range(momenta):
+                            slot = energy * momenta + k
+                            for sign, w_re, w_im in pairs:
+                                other = energy + sign * energy_step
+                                if other < 0 or other >= count:
+                                    continue
+                                at = (other * momenta + (k + sign * q) % momenta) * 2
+                                b_re, b_im = low_ref[at, rows], low_ref[at + 1, rows]
+                                t_re = w_re * b_re - w_im * b_im
+                                t_im = w_re * b_im + w_im * b_re
+                                re[slot] = t_re if re[slot] is None else re[slot] + t_re
+                                im[slot] = t_im if im[slot] is None else im[slot] + t_im
+            for slot in range(count * momenta):
+                sum_ref[2 * slot, rows] = re[slot]
+                sum_ref[2 * slot + 1, rows] = im[slot]
+            return carry
+
+        return step
+
+    lax.fori_loop(0, plan.rows // 8, run(0), 0)
+    lax.fori_loop(plan.rows // 8, plan.held // 8, run(4 * plan.classes), 0)
+    lane = lax.broadcasted_iota(jnp.int32, (plan.rest_pad, LANES), 1)
+    for k in range(plan.group):
+        target = rank ^ k
+        parts = []
+        tail = jnp.zeros((plan.rest_pad, LANES), F32)
+        for e in range(plan.energies):
+            for z in range(2):
+                slab = 2 * e + z
+                place = place_of(plan, target, e, z)
+                parts.append(sum_ref[place, : plan.rows])
+                piece = sum_ref[place, plan.rows :]
+                if slab:
+                    piece = pltpu.roll(piece, slab * plan.rest, 1)
+                mine = (lane >= slab * plan.rest) & (lane < (slab + 1) * plan.rest)
+                tail = jnp.where(mine, piece, tail)
+        parts.append(tail)
+        if plan.tail > plan.rest_pad:
+            parts.append(jnp.zeros((plan.tail - plan.rest_pad, LANES), F32))
+        outs[k][...] = jnp.concatenate(parts, axis=0).astype(BF16)
+
+
+def gather_kernel(plan, rank_ref, *refs):
+    messages = refs[: plan.group]
+    out_ref, wide_ref, rest_ref = refs[plan.group :]
+    rank = rank_ref[0]
+    for k, message in enumerate(messages):
+        source = rank ^ k
+        tile = source // plan.halves
+        half = source % plan.halves
+        values = message[...].astype(F32)
+        lanes = pl.ds(pl.multiple_of(tile * LANES, LANES), LANES)
+        rows = pl.ds(pl.multiple_of(half * plan.rows, 8), plan.rows)
+        tail = values[plan.main_rows : plan.main_rows + plan.rest_pad]
+        for slab in range(plan.slabs):
+            wide_ref[slab, rows, lanes] = values[slab * plan.rows : (slab + 1) * plan.rows]
+            turned = tail if slab == 0 else pltpu.roll(tail, LANES - slab * plan.rest, 1)
+            rest_ref[slab, source] = turned
+    for e in range(plan.energies):
+        for z in range(2):
+            slab = 2 * e + z
+            parts = [rest_ref[slab, source, : plan.rest_rows] for source in range(plan.group)]
+            rest = jnp.concatenate(parts, axis=0)[:, : plan.rest]
+            whole = jnp.concatenate([wide_ref[slab], rest], axis=1)
+            out_ref[e, 0, z] = whole.astype(BF16)
+
+
+def next_kernel(plan, polar_ref, ret_ref, near_ref, dirs_ref, mod_ref, out_ref, v_ref, dense_ref):
+    bonds, atoms, order = plan.bonds, plan.atoms, plan.order
+    padded = -(-bonds // 8) * 8
+    lines = []
+    for p in range(plan.n_phonon):
+        rest = jnp.zeros((4, LANES), F32)
+        for tile in range(plan.tiles):
+            main = jnp.zeros((4, LANES), F32)
+            for half in range(plan.halves):
+                block = polar_ref[(tile * plan.halves + half) * plan.n_phonon + p]
+                main = main + block[:4]
+                rest = rest + block[4:]
+            lines.append(main)
+        lines.append(rest[:, : plan.rest])
+    flat = jnp.concatenate(lines, axis=1)
+    bond = lax.broadcasted_iota(jnp.int32, (padded, plan.columns), 0)
+    keep = bond == mod_ref[...]
+    tall = jnp.concatenate(
+        [jnp.where(keep, flat[row : row + 1], 0.0) for row in range(2 * plan.modes)], axis=0
+    )
+    upper = tall.astype(BF16)
+    lower = (tall - upper.astype(F32)).astype(BF16)
+    atom = lax.broadcasted_iota(jnp.int32, (atoms, plan.columns), 0)
+    column = lax.broadcasted_iota(jnp.int32, (atoms, plan.columns), 1)
+    inside = column - atom * bonds
+    chosen = jnp.where((inside >= 0) & (inside < bonds), 1.0, 0.0).astype(BF16)
+    contract = (((1,), (1,)), ((), ()))
+    by_bond = lax.dot_general(upper, chosen, contract, preferred_element_type=F32)
+    by_bond = by_bond + lax.dot_general(lower, chosen, contract, preferred_element_type=F32)
+    ways = [(i, j) for i in range(3) for j in range(i, 3)]
+    for way, (i, j) in enumerate(ways):
+        pair = dirs_ref[i] * dirs_ref[j]
+        for row in range(2 * plan.modes):
+            values = by_bond[row * padded : row * padded + bonds]
+            v_ref[row * len(ways) + way, :bonds] = values * pair
+
+    def step(chunk, carry):
+        first = pl.multiple_of(chunk * 16, 16)
+        number = lax.broadcasted_iota(jnp.int32, (16, atoms), 0) + first
+        for row in range(2 * plan.modes):
+            sums = [jnp.zeros((16, atoms), F32) for _ in ways]
+            for n in range(bonds):
+                hit = number == near_ref[n : n + 1]
+                for way in range(len(ways)):
+                    value = v_ref[row * len(ways) + way, n : n + 1]
+                    sums[way] = sums[way] + jnp.where(hit, value, 0.0)
+            for way, (i, j) in enumerate(ways):
+                block = sums[way].astype(BF16)
+                dense_ref[
+                    row, pl.ds(pl.multiple_of(j * atoms + first, 16), 16), i * atoms : (i + 1) * atoms
+                ] = block
+                if i != j:
+                    dense_ref[
+                        row,
+                        pl.ds(pl.multiple_of(i * atoms + first, 16), 16),
+                        j * atoms : (j + 1) * atoms,
+                    ] = block
+        return carry
+
+    lax.fori_loop(0, atoms // 16, step, 0)
+    plain = (((1,), (0,)), ((), ()))
+    for m in range(plan.modes):
+        ret_re, ret_im = ret_ref[m, 0], ret_ref[m, 1]
+        dense_re, dense_im = dense_ref[2 * m], dense_ref[2 * m + 1]
+
+        def times(left, right, how):
+            return lax.dot_general(left, right, how, preferred_element_type=F32)
+
+        half_re = (times(ret_re, dense_re, plain) + times(ret_im, dense_im, plain)).astype(BF16)
+        half_im = (times(ret_re, dense_im, plain) - times(ret_im, dense_re, plain)).astype(BF16)
+        next_re = times(ret_re, half_re, contract) - times(ret_im, half_im, contract)
+        next_im = times(ret_re, half_im, contract) + times(ret_im, half_re, contract)
+        out_ref[m, 0] = next_re.astype(BF16)
+        out_ref[m, 1] = next_im.astype(BF16)
+
+
+def mode_tables(plan, energy_offset, momentum_offset, absorb):
+    label = (energy_offset - 1) * plan.all_momenta + momentum_offset
+    line = jnp.arange(8, dtype=jnp.int32)
+    shape = (2, 2, plan.classes, 2, plan.devices, 8)
+    wanted = jnp.arange(plan.classes, dtype=jnp.int32)
+    labels = label.reshape(plan.devices, plan.modes)
+    weights = absorb.reshape(plan.devices, plan.modes)
+    inner = line % 4 // 2
+    by_line = sum(jnp.where(inner == i, labels[:, i : i + 1], 0) for i in range(plan.modes))
+    scale = sum(jnp.where(inner == i, weights[:, i : i + 1], 0.0) for i in range(plan.modes))
+    used = (inner < plan.modes)[None, :]
+    same = (by_line[None] == wanted[:, None, None]) & used[None]
+    part = (line % 2)[None, :] == jnp.arange(2, dtype=jnp.int32)[:, None]
+    kind = (line // 4)[None, :] == jnp.arange(2, dtype=jnp.int32)[:, None]
+    hit = (
+        same[None, :, None] & part[None, None, :, None] & kind[:, None, None, None]
+    ).astype(F32)
+    table = jnp.stack([hit, hit * scale[None, None, None]], axis=1)
+    return table.reshape(4 * 2 * plan.classes, plan.devices * 8)
+
+
+def exchange(plan, blocks):
+    routes = [[(i, i ^ k) for i in range(plan.group)] for k in range(plan.group)]
+    moved = [lax.ppermute(blocks[k], GROUP, routes[k]) for k in range(1, plan.group)]
+    return [blocks[0]] + moved
+
+
+def dealt(
+    plan, g_less, g_great, d_less, d_ret, neighbours, bond_dirs, energy_offset, momentum_offset, absorb
+):
+    rank = lax.axis_index(GROUP).astype(jnp.int32).reshape(1)
+    group, held = plan.group, plan.held
+    slots = plan.all_energies * plan.all_momenta * 2
+    mod = np.arange(plan.columns, dtype=np.int32)[None] % plan.bonds
+    table = mode_tables(plan, energy_offset, momentum_offset, absorb)
+    lines = 2 * plan.classes
+    picks = jnp.concatenate([table[:lines], table[2 * lines : 3 * lines]], axis=0)
+
+    message = jax.ShapeDtypeStruct((2, plan.message, LANES), BF16)
+    blocks = call(
+        functools.partial(deal_kernel, plan), [message] * group, rank, g_less, g_great,
+        scalars=1, scratch=[pltpu.VMEM((2, plan.entries + plan.tail, LANES), F32)],
+        moved=4 * g_less.size * 2,
+    )
+    small = jax.ShapeDtypeStruct((plan.devices, 8, LANES), F32)
+    coupling = call(functools.partial(couple_kernel, plan), small, d_less, bond_dirs, mod)
+    blocks = exchange(plan, blocks)
+    coupling = lax.all_to_all(coupling, EVERY, 0, 0, tiled=True)
+    block_scratch = pltpu.VMEM((slots, held, LANES), F32)
+    polar = call(
+        functools.partial(polar_kernel, plan), small, rank, picks, *blocks,
+        scalars=1, scratch=[block_scratch] * 2,
+    )
+    answer = jax.ShapeDtypeStruct((plan.message, LANES), BF16)
+    sums = call(
+        functools.partial(energy_kernel, plan), [answer] * group, rank, table, coupling, *blocks,
+        scalars=1,
+        scratch=[block_scratch, block_scratch, pltpu.VMEM((4 * lines, LANES), F32)],
+    )
+    polar = lax.all_to_all(polar, EVERY, 0, 0, tiled=True)
+    sums = exchange(plan, sums)
+    self_energy = call(
+        functools.partial(gather_kernel, plan), jax.ShapeDtypeStruct(g_less.shape, BF16), rank, *sums,
+        scalars=1,
+        scratch=[
+            pltpu.VMEM((plan.slabs, plan.entries, plan.tiles * LANES), F32),
+            pltpu.VMEM((plan.slabs, group, plan.rest_pad, LANES), F32),
+        ],
+    )
+    padded = -(-plan.bonds // 8) * 8
+    d_next = call(
+        functools.partial(next_kernel, plan), jax.ShapeDtypeStruct(d_ret.shape, BF16),
+        polar, d_ret, neighbours, bond_dirs, mod,
+        scratch=[
+            pltpu.VMEM((12 * plan.modes, padded, plan.atoms), F32),
+            pltpu.VMEM((2 * plan.modes, plan.order, plan.order), BF16),
+        ],
+    )
+    return self_energy, d_next
+
+
+def local(*arrays):
+    plan = Plan(
+        arrays[0].shape, arrays[2].shape, arrays[3].shape,
+        lax.axis_size("energy"), lax.axis_size("momentum"), lax.axis_size("phonon"),
+    )
+    return dealt(plan, *arrays) if plan.fits() else general(*arrays)
+
+
 def solution(mesh):
     in_specs = (
         P("energy", "momentum", None, None, "phonon"),

time: 221 us -> 62.7 us (0.28)
  blocking collectives: 91.6 us -> 0 us
  waiting for transfers between devices: 34.6 us -> 13.7 us
  local copies, waits for them, and re-layouts: 23.2 us -> 5 us
  other arithmetic: 18.4 us -> 1.26 us
  Pallas kernels: 0 us -> 15.5 us
  matrix products: 14.5 us -> 0 us
  between operations: 14.6 us -> 0.88 us
  starting transfers between devices: 23.3 us -> 26 us
    all_gather x2 -> x0, blocking collectives: 67.6 us -> none  [the longest x1 38 us: local(): polar_full = lax.all_gather(polar_summed, 'phonon', axis=2, tiled=True)]
    psum x1 -> x0, blocking collectives: 24 us -> none  [local(): polar_summed = lax.psum(polar_local, ('energy', 'momentum'))]
    ppermute x6 -> x14, waiting for transfers between devices: 29.3 us -> 13.6 us  [exchange(): lax.ppermute(blocks[k], GROUP, routes[k])]
    pallas_call x0 -> x6, Pallas kernels: none -> 15.5 us  [call(): pl.pallas_call(kernel, out_shape=out_shape, in_specs=specs, out_specs=[vm...]
    dot_general x24 -> x0, matrix products: 14.5 us -> none  [the longest x1 4.01 us: local(): dense = jnp.einsum('mzijna,nab->mziajb', weighted, link, precision=HIGH)]
    reduce_sum x5 -> x0, other arithmetic: 13.6 us -> none  [the longest x3 9.54 us: scaled_blocks(): real_part = jnp.sum(real_w * real_b - imag_w * imag_b, axis=2)]
    unnamed x29 -> x20, local copies, waits for them, and re-layouts: 11.1 us -> 2.62 us
    all_to_all x1 -> x2, starting transfers between devices: 4.87 us -> 12.7 us  [the longest x1 7.3 us: dealt(): coupling = lax.all_to_all(coupling, EVERY, 0, 0, tiled=True)]
  transfers between devices with their start and end apart: 9 -> 16, of which waited for: 3 -> 6; matrix products, arithmetic and copies ran while one was open for 19% -> 6% of each run, Pallas kernels for 0% -> 12%
where the time goes in v1:
time: 62.7 us; the launch traced here: 62.4 us
  starting transfers between devices  26 us (41%)
  Pallas kernels  15.5 us (25%)
  waiting for transfers between devices  13.7 us (22%)
  local copies, waits for them, and re-layouts  5 us (8%)
  other arithmetic  1.26 us (2%)
  between operations  0.88 us (1%)
    pallas_call x6, Pallas kernels, call(): pl.pallas_call(kernel, out_shape=out_shape, in_specs=specs, out_specs=[vm...  15.5 us
    ppermute x14, waiting for transfers between devices, exchange(): lax.ppermute(blocks[k], GROUP, routes[k])  13.6 us
    ppermute x14, starting transfers between devices, exchange(): lax.ppermute(blocks[k], GROUP, routes[k])  13.3 us
    all_to_all x1, starting transfers between devices, dealt(): coupling = lax.all_to_all(coupling, EVERY, 0, 0, tiled=True)  7.3 us
    all_to_all x1, starting transfers between devices, dealt(): polar = lax.all_to_all(polar, EVERY, 0, 0, tiled=True)  5.4 us
    unnamed x20, local copies, waits for them, and re-layouts  2.62 us
    another operation x1, local copies, waits for them, and re-layouts, mode_tables(): table = jnp.stack([hit, hit * scale[None, None, None]], axis=1)  1.3 us
  transfers between devices with their start and end apart: 16, of which 6 were waited for; matrix products, arithmetic and copies ran while one was open for 6% of the time, Pallas kernels for 12%

profile of v1, /device:TPU:0, one launch (start us, length us, event | category | flops | bytes accessed | tf_op | source)
XLA Modules:
  0.0 62.4 jit_solution(16337806628469028145)
XLA Ops:
  0.6 0.0 copy-start.2
  0.6 0.0 copy-start.1
  0.6 0.9 %copy.20.dirs_ref = f32[3,17,128]{2,1,0:T(8,128)S(1)} copy(f32[3,17,128]{2,0,1:T(4,128)} %param.15) | data formatting | bytes 52224 | tf_op args[5]
  1.5 1.0 %copy.19.less_ref = f32[2,2,9,17,128]{4,3,2,1,0:T(8,128)S(1)} copy(f32[2,2,9,17,128]{4,1,3,2,0:T(2,128)} %param.12) | data formatting | bytes 626688 | tf_op args[2]
  2.5 0.0 copy-start.3
  2.5 0.7 %copy-done.3 = s32[1,2176]{1,0:T(1,128)S(1)} copy-done((s32[1,2176]{1,0:T(1,128)S(1)}, s32[1,2176]{1,0:T(1,128)}, u32[]{:S(2)}) %copy-start.3) | copy-done | bytes 8728
  3.2 1.2 %shard_map.113 = f32[32,8,128]{2,1,0:T(8,128)} custom-call(f32[2,2,9,17,128]{4,3,2,1,0:T(8,128)S(1)} %copy.19.less_ref, f32[3,17,128]{2,1,0:T(8,128)S(1)} %copy.20.dirs_ref, s32[1,2176]{1,0:T(1,128)S(1)} %copy-done.3), custom_call_target="tpu_custom_call" | custom-call | tf_op jit(solution)/shard_map/pallas_call | solution.py:214
  4.5 7.3 %all-to-all-start = ((f32[32,8,128]{2,1,0:T(8,128)}), f32[32,8,128]{2,1,0:T(8,128)S(1)}, u32[]{:S(2)}, u32[]{:S(2)}) async-start(f32[32,8,128]{2,1,0:T(8,128)} %shard_map.113), calls=%async_computation | async-start | bytes 262144 | tf_op jit(solution)/shard_map/all_to_all | solution.py:566
  11.8 0.0 copy-done.2
  11.8 0.0 copy-done.1
  11.8 1.0 %shard_map.114 = (bf16[2,320,128]{2,1,0:T(8,128)(2,1)S(1)}, bf16[2,320,128]{2,1,0:T(8,128)(2,1)S(1)}, bf16[2,320,128]{2,1,0:T(8,128)(2,1)S(1)}, bf16[2,320,128]{...) custom-call(s32[1]{0:T(128)} %bitcast.rank_ref, ...), custom_call_target="tpu_custom_call" | custom-call | bytes 2506752 | tf_op jit(solution)/shard_map/pallas_call | solution.py:214
  12.8 0.3 collective-permute-start
  13.0 1.7 %collective-permute-start.1 = (bf16[2,320,128]{2,1,0:T(8,128)(2,1)S(1)}, bf16[2,320,128]{2,1,0:T(8,128)(2,1)S(1)}, u32[]{:S(2)}, u32[]{:S(2)}) collective-permute-start(bf16[2,320,128]{2,1,0:T(8,128)(2,1)S(1)} %get-tuple-element.20), channel_id=1, source_target_pairs={{0,8},{4,12},{8,0},{12,4},{16,24},{20,28},{24,16},{28,20},{1,9},{5... | collective-permute-start | bytes 491528 | tf_op jit(solution)/shard_map/ppermute | solution.py:542
  14.7 0.0 collective-permute-start.2
  14.7 1.7 %collective-permute-start.3 = (bf16[2,320,128]{2,1,0:T(8,128)(2,1)S(1)}, bf16[2,320,128]{2,1,0:T(8,128)(2,1)S(1)}, u32[]{:S(2)}, u32[]{:S(2)}) collective-permute-start(bf16[2,320,128]{2,1,0:T(8,128)(2,1)S(1)} %get-tuple-element.22), channel_id=1, source_target_pairs={{0,16},{4,20},{8,24},{12,28},{16,0},{20,4},{24,8},{28,12},{1,17},{... | collective-permute-start | bytes 491528 | tf_op jit(solution)/shard_map/ppermute | solution.py:542
  16.4 0.1 collective-permute-start.4
  16.6 0.0 copy-done.7
  16.6 0.1 reshape.230
  16.7 0.2 slice_reduce_fusion.3
  16.9 0.1 reshape.231
  17.0 0.2 slice_reduce_fusion.1
  17.2 0.1 select_add_fusion.1
  17.3 0.1 fusion
  17.4 0.1 broadcast_and_fusion
  17.5 0.1 select_add_fusion
  17.5 0.1 and_select_fusion
  17.6 0.1 and_convert_fusion
  17.7 0.7 %pad_maximum_fusion = f32[2,2,8,2,32,8]{4,5,3,2,1,0:T(8,128)} fusion(f32[2,1,8,2,32,8]{4,5,3,2,1,0:T(8,128)S(1)} %and_select_fusion, f32[2,1,8,2,32,8]{4,5,3,2,1,0:T(8,128)S(1)} %and_convert_fusion), kind=kLoop, calls=%fused_computation | loop fusion | flops 16384 | bytes 131072 | tf_op jit(solution)/shard_map/stack | solution.py:536
  18.4 1.3 %copy.18 = f32[2,2,8,2,32,8]{5,4,3,2,1,0:T(8,128)S(1)} copy(f32[2,2,8,2,32,8]{4,5,3,2,1,0:T(8,128)} %pad_maximum_fusion) | data formatting | bytes 131072 | tf_op jit(solution)/shard_map/stack | solution.py:536
  19.8 0.5 reshape.232.weigh_ref
  20.3 0.0 collective-permute-done.refs_1_
  20.3 2.6 %collective-permute-start.5 = (bf16[2,320,128]{2,1,0:T(8,128)(2,1)S(1)}, bf16[2,320,128]{2,1,0:T(8,128)(2,1)S(1)}, u32[]{:S(2)}, u32[]{:S(2)}) collective-permute-start(bf16[2,320,128]{2,1,0:T(8,128)(2,1)S(1)} %get-tuple-element.24), channel_id=1, source_target_pairs={{0,24},{4,28},{8,16},{12,20},{16,8},{20,12},{24,0},{28,4},{1,25},{... | collective-permute-start | bytes 491528 | tf_op jit(solution)/shard_map/ppermute | solution.py:542
  22.9 0.0 collective-permute-done.1.refs_2_
  22.9 0.0 collective-permute-start.6
  23.0 0.4 collective-permute-done.2.refs_3_
  23.4 0.0 collective-permute-done.3.refs_4_
  23.4 7.8 %collective-permute-done.4.refs_5_ = bf16[2,320,128]{2,1,0:T(8,128)(2,1)S(1)} collective-permute-done((bf16[2,320,128]{2,1,0:T(8,128)(2,1)S(1)}, bf16[2,320,128]{2,1,0:T(8,128)(2,1)S(1)}, u32[]{:S(2)}, u32[]{:S(2)}) %collective-permute-start.4) | collective-permute-done | bytes 163872 | tf_op jit(solution)/shard_map/ppermute | solution.py:542
  31.2 0.0 collective-permute-done.5.refs_6_
  31.2 0.5 collective-permute-done.6.refs_7_
  31.7 2.6 %shard_map.117 = f32[32,8,128]{2,1,0:T(8,128)} custom-call(s32[1]{0:T(128)} %bitcast.rank_ref, f32[32,256]{1,0:T(8,128)S(1)} %pad_maximum_fusion.1.pick_ref, bf16[2,320,128]{2,1,0:T(8,128)(2,1)S(1)} %get-tuple-element.18.refs_0_, bf16[2,320,128]{2,1,0:T(8,128)(2,1)S(1)} %collective-permute-done.refs_1_, ...), custom_call_target="tpu_custom_call" | custom-call | tf_op jit(solution)/shard_map/pallas_call | solution.py:214
  34.3 0.0 all-to-all-done.coupling_ref
  34.3 5.4 %all-to-all-start.1 = ((f32[32,8,128]{2,1,0:T(8,128)}), f32[32,8,128]{2,1,0:T(8,128)S(1)}, u32[]{:S(2)}, u32[]{:S(2)}) async-start(f32[32,8,128]{2,1,0:T(8,128)} %shard_map.117), calls=%async_computation.1 | async-start | bytes 262144 | tf_op jit(solution)/shard_map/all_to_all | solution.py:578
  39.7 0.0 copy-start
  39.7 0.0 copy-start.4
  39.7 0.0 copy-start.5
  39.7 2.8 %shard_map.115 = (bf16[320,128]{1,0:T(8,128)(2,1)S(1)}, bf16[320,128]{1,0:T(8,128)(2,1)S(1)}, bf16[320,128]{1,0:T(8,128)(2,1)S(1)}, bf16[320,128]{1,0:T(8,128)(2...) custom-call(s32[1]{0:T(128)} %bitcast.rank_ref, ...), custom_call_target="tpu_custom_call" | custom-call | tf_op jit(solution)/shard_map/pallas_call | solution.py:214
  42.5 0.3 collective-permute-start.7
  42.8 1.7 %collective-permute-start.8 = (bf16[320,128]{1,0:T(8,128)(2,1)S(1)}, bf16[320,128]{1,0:T(8,128)(2,1)S(1)}, u32[]{:S(2)}, u32[]{:S(2)}) collective-permute-start(bf16[320,128]{1,0:T(8,128)(2,1)S(1)} %get-tuple-element.28), channel_id=1, source_target_pairs={{0,8},{4,12},{8,0},{12,4},{16,24},{20,28},{24,16},{28,20},{1,9},{5... | collective-permute-start | bytes 245768 | tf_op jit(solution)/shard_map/ppermute | solution.py:542
  44.5 0.0 collective-permute-start.9
  44.5 1.7 %collective-permute-start.10 = (bf16[320,128]{1,0:T(8,128)(2,1)S(1)}, bf16[320,128]{1,0:T(8,128)(2,1)S(1)}, u32[]{:S(2)}, u32[]{:S(2)}) collective-permute-start(bf16[320,128]{1,0:T(8,128)(2,1)S(1)} %get-tuple-element.30), channel_id=1, source_target_pairs={{0,16},{4,20},{8,24},{12,28},{16,0},{20,4},{24,8},{28,12},{1,17},{... | collective-permute-start | bytes 245768 | tf_op jit(solution)/shard_map/ppermute | solution.py:542
  46.2 0.1 collective-permute-start.11
  46.3 0.0 collective-permute-done.7.refs_1_
  46.3 2.6 %collective-permute-start.12 = (bf16[320,128]{1,0:T(8,128)(2,1)S(1)}, bf16[320,128]{1,0:T(8,128)(2,1)S(1)}, u32[]{:S(2)}, u32[]{:S(2)}) collective-permute-start(bf16[320,128]{1,0:T(8,128)(2,1)S(1)} %get-tuple-element.32), channel_id=1, source_target_pairs={{0,24},{4,28},{8,16},{12,20},{16,8},{20,12},{24,0},{28,4},{1,25},{... | collective-permute-start | bytes 245768 | tf_op jit(solution)/shard_map/ppermute | solution.py:542
  48.9 0.0 collective-permute-done.8.refs_2_
  48.9 0.5 collective-permute-start.13
  49.4 0.0 collective-permute-done.9.refs_3_
  49.4 0.1 collective-permute-done.10.refs_4_
  49.5 4.3 %collective-permute-done.11.refs_5_ = bf16[320,128]{1,0:T(8,128)(2,1)S(1)} collective-permute-done((bf16[320,128]{1,0:T(8,128)(2,1)S(1)}, bf16[320,128]{1,0:T(8,128)(2,1)S(1)}, u32[]{:S(2)}, u32[]{:S(2)}) %collective-permute-start.11) | collective-permute-done | bytes 81952 | tf_op jit(solution)/shard_map/ppermute | solution.py:542
  53.8 0.0 collective-permute-done.12.refs_6_
  53.8 0.6 collective-permute-done.13.refs_7_
  54.4 1.2 %shard_map.116 = bf16[2,1,2,144,544]{4,3,2,1,0:T(8,128)(2,1)} custom-call(s32[1]{0:T(128)} %bitcast.rank_ref, bf16[320,128]{1,0:T(8,128)(2,1)S(1)} %get-tuple-element.26.refs_0_, bf16[320,128]{1,0:T(8,128)(2,1)S(1)} %collective-permute-done.7.refs_1_, bf16[320,128]{1,0:T(8,128)(2,1)S(1)} %collective-permute-done.8.refs_2_, ...), custom_call_target="tpu_custom_call" | custom-call | tf_op jit(solution)/shard_map/pallas_call | solution.py:214
  55.5 0.0 all-to-all-done.1.polar_ref
  55.5 0.0 copy-done.5
  55.6 6.8 %shard_map.118 = bf16[2,2,384,384]{3,2,1,0:T(8,128)(2,1)} custom-call(f32[32,8,128]{2,1,0:T(8,128)S(1)} %all-to-all-done.1.polar_ref, bf16[2,2,384,384]{3,2,1,0:T(8,128)(2,1)S(1)} %copy-done, s32[17,128]{1,0:T(8,128)S(1)} %copy-done.5, f32[3,17,128]{2,1,0:T(8,128)S(1)} %copy.20.dirs_ref, s32[1,2176]{1,0:T(1,128)S(1)} %copy-done.4), custom_call_target="tpu_custom_call" | custom-call | tf_op jit(solution)/shard_map/pallas_call | solution.py:214
  (16 shorter events, 0.1 us)
Async XLA Ops:
  0.6 11.2 %copy-start.2 = (bf16[2,1,2,144,544]{4,3,2,1,0:T(8,128)(2,1)S(1)}, bf16[2,1,2,144,544]{4,3,2,1,0:T(8,128)(2,1)}, u32[]{:S(2)}) copy-start(bf16[2,1,2,144,544]{4,3,2,1,0:T(8,128)(2,1)} %great_ref.1) | copy-start | bytes 1880068
  0.6 11.2 %copy-start.1 = (bf16[2,1,2,144,544]{4,3,2,1,0:T(8,128)(2,1)S(1)}, bf16[2,1,2,144,544]{4,3,2,1,0:T(8,128)(2,1)}, u32[]{:S(2)}) copy-start(bf16[2,1,2,144,544]{4,3,2,1,0:T(8,128)(2,1)} %less_ref.2) | copy-start | bytes 1880068
  2.5 0.7 %copy-start.3 = (s32[1,2176]{1,0:T(1,128)S(1)}, s32[1,2176]{1,0:T(1,128)}, u32[]{:S(2)}) copy-start(s32[1,2176]{1,0:T(1,128)} %constant.74.clone.mod_ref) | copy-start | bytes 26116
  3.2 13.4 %copy-start.7 = (s32[64]{0:T(128)S(1)}, s32[64]{0:T(128)}, u32[]{:S(2)}) copy-start(s32[64]{0:T(128)} %param.17) | copy-start | bytes 772
  3.2 13.4 %copy-start.8 = (s32[64]{0:T(128)S(1)}, s32[64]{0:T(128)}, u32[]{:S(2)}) copy-start(s32[64]{0:T(128)} %param.16) | copy-start | bytes 772
  3.2 13.7 %copy-start.6 = (f32[64]{0:T(128)S(1)}, f32[64]{0:T(128)}, u32[]{:S(2)}) copy-start(f32[64]{0:T(128)} %param.18) | copy-start | bytes 772
  4.5 29.8 %all-to-all-start = ((f32[32,8,128]{2,1,0:T(8,128)}), f32[32,8,128]{2,1,0:T(8,128)S(1)}, u32[]{:S(2)}, u32[]{:S(2)}) async-start(f32[32,8,128]{2,1,0:T(8,128)} %shard_map.113), calls=%async_computation | async-start | bytes 262144 | tf_op jit(solution)/shard_map/all_to_all | solution.py:566
  12.8 7.5 %collective-permute-start = (bf16[2,320,128]{2,1,0:T(8,128)(2,1)S(1)}, bf16[2,320,128]{2,1,0:T(8,128)(2,1)S(1)}, u32[]{:S(2)}, u32[]{:S(2)}) collective-permute-start(bf16[2,320,128]{2,1,0:T(8,128)(2,1)S(1)} %get-tuple-element.19), channel_id=1, source_target_pairs={{0,4},{4,0},{8,12},{12,8},{16,20},{20,16},{24,28},{28,24},{1,5},{5... | collective-permute-start | bytes 491528 | tf_op jit(solution)/shard_map/ppermute | solution.py:542
  13.0 9.9 %collective-permute-start.1 = (bf16[2,320,128]{2,1,0:T(8,128)(2,1)S(1)}, bf16[2,320,128]{2,1,0:T(8,128)(2,1)S(1)}, u32[]{:S(2)}, u32[]{:S(2)}) collective-permute-start(bf16[2,320,128]{2,1,0:T(8,128)(2,1)S(1)} %get-tuple-element.20), channel_id=1, source_target_pairs={{0,8},{4,12},{8,0},{12,4},{16,24},{20,28},{24,16},{28,20},{1,9},{5... | collective-permute-start | bytes 491528 | tf_op jit(solution)/shard_map/ppermute | solution.py:542
  14.7 8.7 %collective-permute-start.2 = (bf16[2,320,128]{2,1,0:T(8,128)(2,1)}, bf16[2,320,128]{2,1,0:T(8,128)(2,1)S(1)}, u32[]{:S(2)}, u32[]{:S(2)}) collective-permute-start(bf16[2,320,128]{2,1,0:T(8,128)(2,1)} %get-tuple-element.21), channel_id=1, source_target_pairs={{0,12},{4,8},{8,4},{12,0},{16,28},{20,24},{24,20},{28,16},{1,13},{... | collective-permute-start | bytes 491528 | tf_op jit(solution)/shard_map/ppermute | solution.py:542
  14.7 8.7 %collective-permute-start.3 = (bf16[2,320,128]{2,1,0:T(8,128)(2,1)S(1)}, bf16[2,320,128]{2,1,0:T(8,128)(2,1)S(1)}, u32[]{:S(2)}, u32[]{:S(2)}) collective-permute-start(bf16[2,320,128]{2,1,0:T(8,128)(2,1)S(1)} %get-tuple-element.22), channel_id=1, source_target_pairs={{0,16},{4,20},{8,24},{12,28},{16,0},{20,4},{24,8},{28,12},{1,17},{... | collective-permute-start | bytes 491528 | tf_op jit(solution)/shard_map/ppermute | solution.py:542
  16.4 14.8 %collective-permute-start.4 = (bf16[2,320,128]{2,1,0:T(8,128)(2,1)S(1)}, bf16[2,320,128]{2,1,0:T(8,128)(2,1)S(1)}, u32[]{:S(2)}, u32[]{:S(2)}) collective-permute-start(bf16[2,320,128]{2,1,0:T(8,128)(2,1)S(1)} %get-tuple-element.23), channel_id=1, source_target_pairs={{0,20},{4,16},{8,28},{12,24},{16,4},{20,0},{24,12},{28,8},{1,21},{... | collective-permute-start | bytes 491528 | tf_op jit(solution)/shard_map/ppermute | solution.py:542
  20.3 10.9 %collective-permute-start.5 = (bf16[2,320,128]{2,1,0:T(8,128)(2,1)S(1)}, bf16[2,320,128]{2,1,0:T(8,128)(2,1)S(1)}, u32[]{:S(2)}, u32[]{:S(2)}) collective-permute-start(bf16[2,320,128]{2,1,0:T(8,128)(2,1)S(1)} %get-tuple-element.24), channel_id=1, source_target_pairs={{0,24},{4,28},{8,16},{12,20},{16,8},{20,12},{24,0},{28,4},{1,25},{... | collective-permute-start | bytes 491528 | tf_op jit(solution)/shard_map/ppermute | solution.py:542
  22.9 8.8 %collective-permute-start.6 = (bf16[2,320,128]{2,1,0:T(8,128)(2,1)S(1)}, bf16[2,320,128]{2,1,0:T(8,128)(2,1)S(1)}, u32[]{:S(2)}, u32[]{:S(2)}) collective-permute-start(bf16[2,320,128]{2,1,0:T(8,128)(2,1)S(1)} %get-tuple-element.25), channel_id=1, source_target_pairs={{0,28},{4,24},{8,20},{12,16},{16,12},{20,8},{24,4},{28,0},{1,29},{... | collective-permute-start | bytes 491528 | tf_op jit(solution)/shard_map/ppermute | solution.py:542
  34.3 21.2 %all-to-all-start.1 = ((f32[32,8,128]{2,1,0:T(8,128)}), f32[32,8,128]{2,1,0:T(8,128)S(1)}, u32[]{:S(2)}, u32[]{:S(2)}) async-start(f32[32,8,128]{2,1,0:T(8,128)} %shard_map.117), calls=%async_computation.1 | async-start | bytes 262144 | tf_op jit(solution)/shard_map/all_to_all | solution.py:578
  39.7 15.8 %copy-start = (bf16[2,2,384,384]{3,2,1,0:T(8,128)(2,1)S(1)}, bf16[2,2,384,384]{3,2,1,0:T(8,128)(2,1)}, u32[]{:S(2)}) copy-start(bf16[2,2,384,384]{3,2,1,0:T(8,128)(2,1)} %ret_ref.1) | copy-start | bytes 3538948
  39.7 15.8 %copy-start.4 = (s32[1,2176]{1,0:T(1,128)S(1)}, s32[1,2176]{1,0:T(1,128)}, u32[]{:S(2)}) copy-start(s32[1,2176]{1,0:T(1,128)} %constant.74.clone.mod_ref) | copy-start | bytes 26116
  39.7 15.8 %copy-start.5 = (s32[17,128]{1,0:T(8,128)S(1)}, s32[17,128]{1,0:T(8,128)}, u32[]{:S(2)}) copy-start(s32[17,128]{1,0:T(8,128)} %near_ref.1) | copy-start | bytes 26116
  42.5 3.8 %collective-permute-start.7 = (bf16[320,128]{1,0:T(8,128)(2,1)S(1)}, bf16[320,128]{1,0:T(8,128)(2,1)S(1)}, u32[]{:S(2)}, u32[]{:S(2)}) collective-permute-start(bf16[320,128]{1,0:T(8,128)(2,1)S(1)} %get-tuple-element.27), channel_id=1, source_target_pairs={{0,4},{4,0},{8,12},{12,8},{16,20},{20,16},{24,28},{28,24},{1,5},{5... | collective-permute-start | bytes 245768 | tf_op jit(solution)/shard_map/ppermute | solution.py:542
  42.8 6.1 %collective-permute-start.8 = (bf16[320,128]{1,0:T(8,128)(2,1)S(1)}, bf16[320,128]{1,0:T(8,128)(2,1)S(1)}, u32[]{:S(2)}, u32[]{:S(2)}) collective-permute-start(bf16[320,128]{1,0:T(8,128)(2,1)S(1)} %get-tuple-element.28), channel_id=1, source_target_pairs={{0,8},{4,12},{8,0},{12,4},{16,24},{20,28},{24,16},{28,20},{1,9},{5... | collective-permute-start | bytes 245768 | tf_op jit(solution)/shard_map/ppermute | solution.py:542
  44.5 4.9 %collective-permute-start.9 = (bf16[320,128]{1,0:T(8,128)(2,1)S(1)}, bf16[320,128]{1,0:T(8,128)(2,1)S(1)}, u32[]{:S(2)}, u32[]{:S(2)}) collective-permute-start(bf16[320,128]{1,0:T(8,128)(2,1)S(1)} %get-tuple-element.29), channel_id=1, source_target_pairs={{0,12},{4,8},{8,4},{12,0},{16,28},{20,24},{24,20},{28,16},{1,13},{... | collective-permute-start | bytes 245768 | tf_op jit(solution)/shard_map/ppermute | solution.py:542
  44.5 5.0 %collective-permute-start.10 = (bf16[320,128]{1,0:T(8,128)(2,1)S(1)}, bf16[320,128]{1,0:T(8,128)(2,1)S(1)}, u32[]{:S(2)}, u32[]{:S(2)}) collective-permute-start(bf16[320,128]{1,0:T(8,128)(2,1)S(1)} %get-tuple-element.30), channel_id=1, source_target_pairs={{0,16},{4,20},{8,24},{12,28},{16,0},{20,4},{24,8},{28,12},{1,17},{... | collective-permute-start | bytes 245768 | tf_op jit(solution)/shard_map/ppermute | solution.py:542
  46.2 7.6 %collective-permute-start.11 = (bf16[320,128]{1,0:T(8,128)(2,1)S(1)}, bf16[320,128]{1,0:T(8,128)(2,1)S(1)}, u32[]{:S(2)}, u32[]{:S(2)}) collective-permute-start(bf16[320,128]{1,0:T(8,128)(2,1)S(1)} %get-tuple-element.31), channel_id=1, source_target_pairs={{0,20},{4,16},{8,28},{12,24},{16,4},{20,0},{24,12},{28,8},{1,21},{... | collective-permute-start | bytes 245768 | tf_op jit(solution)/shard_map/ppermute | solution.py:542
  46.3 7.5 %collective-permute-start.12 = (bf16[320,128]{1,0:T(8,128)(2,1)S(1)}, bf16[320,128]{1,0:T(8,128)(2,1)S(1)}, u32[]{:S(2)}, u32[]{:S(2)}) collective-permute-start(bf16[320,128]{1,0:T(8,128)(2,1)S(1)} %get-tuple-element.32), channel_id=1, source_target_pairs={{0,24},{4,28},{8,16},{12,20},{16,8},{20,12},{24,0},{28,4},{1,25},{... | collective-permute-start | bytes 245768 | tf_op jit(solution)/shard_map/ppermute | solution.py:542
  48.9 5.5 %collective-permute-start.13 = (bf16[320,128]{1,0:T(8,128)(2,1)S(1)}, bf16[320,128]{1,0:T(8,128)(2,1)S(1)}, u32[]{:S(2)}, u32[]{:S(2)}) collective-permute-start(bf16[320,128]{1,0:T(8,128)(2,1)S(1)} %get-tuple-element.33), channel_id=1, source_target_pairs={{0,28},{4,24},{8,20},{12,16},{16,12},{20,8},{24,4},{28,0},{1,29},{... | collective-permute-start | bytes 245768 | tf_op jit(solution)/shard_map/ppermute | solution.py:542

commit v2 on v1

--- a/solution.py
+++ b/solution.py
@@ -2,7 +2,6 @@
 
 import jax
 import jax.numpy as jnp
-import numpy as np
 from jax import lax
 from jax.experimental import pallas as pl
 from jax.experimental.pallas import tpu as pltpu
@@ -185,6 +184,9 @@
         self.tail = self.message - self.main_rows
         self.held = self.rows + self.rest_pad
         self.columns = self.width * n_phonon
+        self.partners = sorted(
+            range(self.group), key=lambda k: (k > 0, k < n_momentum, k % n_momentum, k)
+        )
 
     def fits(self):
         return (
@@ -234,8 +236,8 @@
         ]
         rest_ref[which, : plan.entries] = jnp.concatenate(pieces, axis=1)
         rest_ref[which, plan.entries :] = jnp.zeros((plan.tail, LANES), F32)
-    for k in range(plan.group):
-        target = rank ^ k
+    for k, partner in enumerate(plan.partners):
+        target = rank ^ partner
         tile = target // plan.halves
         half = target % plan.halves
         lanes = pl.ds(pl.multiple_of(tile * LANES, LANES), LANES)
@@ -253,33 +255,72 @@
             outs[k][which] = jnp.concatenate(parts, axis=0).astype(BF16)
 
 
-def couple_kernel(plan, less_ref, dirs_ref, mod_ref, out_ref):
-    bonds, width = plan.bonds, plan.width
-    padded = -(-bonds // 8) * 8
-    dirs = dirs_ref[...]
-    rows = []
-    for m in range(plan.modes):
-        for z in range(2):
-            total = jnp.zeros((bonds, plan.atoms), F32)
-            for i in range(3):
-                for j in range(3):
-                    total = total + less_ref[m, z, 3 * i + j] * (dirs[i] * dirs[j])
-            rows.append(jnp.pad(total, ((0, padded - bonds), (0, 0))))
-    stacked = jnp.concatenate(rows, axis=0).astype(BF16)
+def bond_of(plan, shape):
+    column = lax.broadcasted_iota(jnp.int32, shape, len(shape) - 1)
+    atom = jnp.floor((column.astype(F32) + 0.5) * (1.0 / plan.bonds)).astype(jnp.int32)
+    return column - atom * plan.bonds
+
+
+def atom_table(plan):
     atom = lax.broadcasted_iota(jnp.int32, (plan.atoms, plan.columns), 0)
     column = lax.broadcasted_iota(jnp.int32, (plan.atoms, plan.columns), 1)
-    inside = column - atom * bonds
-    chosen = jnp.where((inside >= 0) & (inside < bonds), 1.0, 0.0).astype(BF16)
-    spread = jnp.dot(stacked, chosen, preferred_element_type=F32)
-    bond = lax.broadcasted_iota(jnp.int32, (padded, plan.columns), 0)
-    keep = bond == mod_ref[...]
-    lines = []
-    for row in range(2 * plan.modes):
-        piece = spread[row * padded : (row + 1) * padded]
-        lines.append(jnp.sum(jnp.where(keep, piece, 0.0), axis=0, keepdims=True))
-    while len(lines) < 4:
-        lines.append(jnp.zeros((1, plan.columns), F32))
-    flat = jnp.concatenate(lines, axis=0)
+    inside = column - atom * plan.bonds
+    return jnp.where((inside >= 0) & (inside < plan.bonds), 1.0, 0.0).astype(BF16)
+
+
+def mode_table(plan, energy_ref, momentum_ref, absorb_ref):
+    width = plan.devices * 8
+    modes = plan.devices * plan.modes
+    label = (energy_ref[...] - 1) * plan.all_momenta + momentum_ref[...]
+    stacked = jnp.concatenate(
+        [label.astype(F32), absorb_ref[...], jnp.zeros((6, modes), F32)], axis=0
+    )
+    mode = lax.broadcasted_iota(jnp.int32, (modes, width), 0)
+    column = lax.broadcasted_iota(jnp.int32, (modes, width), 1)
+    inner = (column & 3) >> 1
+    chosen = (mode == (column >> 3) * plan.modes + inner) & (inner < plan.modes)
+    spread = jnp.dot(
+        stacked, jnp.where(chosen, 1.0, 0.0), precision=HIGH, preferred_element_type=F32
+    )
+    label = (spread[:1] + 0.5).astype(jnp.int32)
+    column = lax.broadcasted_iota(jnp.int32, (2 * plan.classes, width), 1)
+    row = lax.broadcasted_iota(jnp.int32, (2 * plan.classes, width), 0)
+    hit = (label == (row >> 1)) & ((column & 1) == (row & 1))
+    hit = hit & (((column & 3) >> 1) < plan.modes)
+    blocks = []
+    for kind in range(2):
+        here = hit & (((column >> 2) & 1) == kind)
+        blocks.append(jnp.where(here, 1.0, 0.0))
+        blocks.append(jnp.where(here, spread[1:2], 0.0))
+    return jnp.concatenate(blocks, axis=0)
+
+
+def couple_kernel(
+    plan, less_ref, dirs_ref, energy_ref, momentum_ref, absorb_ref, out_ref, table_ref, pair_ref, held_ref
+):
+    bonds, width = plan.bonds, plan.width
+    held_ref[...] = jnp.zeros(held_ref.shape, F32)
+    for n in range(bonds):
+        pairs = [dirs_ref[n, i : i + 1] * dirs_ref[n, j : j + 1] for i in range(3) for j in range(3)]
+        for way, (i, j) in enumerate((i, j) for i in range(3) for j in range(i, 3)):
+            pair_ref[way, n : n + 1] = pairs[3 * i + j]
+        for m in range(plan.modes):
+            total = less_ref[m, 0, n] * pairs[0]
+            for t in range(1, 9):
+                total = total + less_ref[m, t, n] * pairs[t]
+            row = (m * bonds + n) * 2
+            held_ref[row : row + 2] = total
+    rows = held_ref.shape[0]
+    spread = jnp.dot(held_ref[...].astype(BF16), atom_table(plan), preferred_element_type=F32)
+    row = lax.broadcasted_iota(jnp.int32, (rows, 1), 0)
+    bond = (row >> 1) - jnp.where(row >= 2 * bonds, bonds, 0)
+    keep = bond == bond_of(plan, (1, plan.columns))
+    kept = jnp.where(keep, spread, 0.0).astype(BF16)
+    line = lax.broadcasted_iota(jnp.int32, (8, rows), 0)
+    row = lax.broadcasted_iota(jnp.int32, (8, rows), 1)
+    owner = jnp.where(row >= 2 * bonds, 2, 0) + (row & 1)
+    gather = jnp.where((line == owner) & (row < 2 * bonds * plan.modes), 1.0, 0.0).astype(BF16)
+    flat = jnp.dot(gather, kept, preferred_element_type=F32)[:4]
     for p in range(plan.n_phonon):
         start = p * width
         rest = flat[:, start + plan.tiles * LANES : start + width]
@@ -289,6 +330,7 @@
             block = jnp.concatenate([main, rest], axis=0)
             for half in range(plan.halves):
                 out_ref[(tile * plan.halves + half) * plan.n_phonon + p] = block
+    table_ref[...] = mode_table(plan, energy_ref, momentum_ref, absorb_ref)
 
 
 def place_of(plan, source, e, z):
@@ -298,8 +340,8 @@
 
 def stage_blocks(plan, rank, which, messages, held_ref):
     row = lax.broadcasted_iota(jnp.int32, (plan.rest_pad, LANES), 0)
-    for k, message in enumerate(messages):
-        source = rank ^ k
+    for partner, message in zip(plan.partners, messages):
+        source = rank ^ partner
         values = message[which].astype(F32)
         tail = values[plan.main_rows : plan.main_rows + plan.rest_pad]
         tail = jnp.where(row < plan.rest_rows, tail, 0.0)
@@ -312,7 +354,7 @@
                 held_ref[place, plan.rows :] = turned
 
 
-def polar_kernel(plan, rank_ref, pick_ref, *refs):
+def polar_kernel(plan, rank_ref, table_ref, *refs):
     messages = refs[: plan.group]
     out_ref, low_ref, high_ref = refs[plan.group :]
     rank = rank_ref[0]
@@ -342,8 +384,10 @@
     scale = float(count * momenta * plan.entries) ** (-0.5)
     lines = [jnp.sum(part, axis=0, keepdims=True) * scale for part in main + rest]
     table = jnp.concatenate(lines, axis=0)
+    lines = 2 * plan.classes
+    picks = jnp.concatenate([table_ref[:lines], table_ref[2 * lines : 3 * lines]], axis=0)
     picked = lax.dot_general(
-        pick_ref[...], table, (((0,), (0,)), ((), ())), precision=HIGH, preferred_element_type=F32
+        picks, table, (((0,), (0,)), ((), ())), precision=HIGH, preferred_element_type=F32
     )
     out_ref[...] = picked.reshape(out_ref.shape)
 
@@ -395,8 +439,8 @@
     lax.fori_loop(0, plan.rows // 8, run(0), 0)
     lax.fori_loop(plan.rows // 8, plan.held // 8, run(4 * plan.classes), 0)
     lane = lax.broadcasted_iota(jnp.int32, (plan.rest_pad, LANES), 1)
-    for k in range(plan.group):
-        target = rank ^ k
+    for k, partner in enumerate(plan.partners):
+        target = rank ^ partner
         parts = []
         tail = jnp.zeros((plan.rest_pad, LANES), F32)
         for e in range(plan.energies):
@@ -419,8 +463,8 @@
     messages = refs[: plan.group]
     out_ref, wide_ref, rest_ref = refs[plan.group :]
     rank = rank_ref[0]
-    for k, message in enumerate(messages):
-        source = rank ^ k
+    for partner, message in zip(plan.partners, messages):
+        source = rank ^ partner
         tile = source // plan.halves
         half = source % plan.halves
         values = message[...].astype(F32)
@@ -440,7 +484,7 @@
             out_ref[e, 0, z] = whole.astype(BF16)
 
 
-def next_kernel(plan, polar_ref, ret_ref, near_ref, dirs_ref, mod_ref, out_ref, v_ref, dense_ref):
+def next_kernel(plan, polar_ref, ret_ref, near_ref, pair_ref, out_ref, v_ref, dense_ref):
     bonds, atoms, order = plan.bonds, plan.atoms, plan.order
     padded = -(-bonds // 8) * 8
     lines = []
@@ -455,26 +499,23 @@
             lines.append(main)
         lines.append(rest[:, : plan.rest])
     flat = jnp.concatenate(lines, axis=1)
-    bond = lax.broadcasted_iota(jnp.int32, (padded, plan.columns), 0)
-    keep = bond == mod_ref[...]
+    bond = lax.broadcasted_iota(jnp.int32, (padded, 1), 0)
+    keep = bond == bond_of(plan, (1, plan.columns))
     tall = jnp.concatenate(
         [jnp.where(keep, flat[row : row + 1], 0.0) for row in range(2 * plan.modes)], axis=0
     )
     upper = tall.astype(BF16)
     lower = (tall - upper.astype(F32)).astype(BF16)
-    atom = lax.broadcasted_iota(jnp.int32, (atoms, plan.columns), 0)
-    column = lax.broadcasted_iota(jnp.int32, (atoms, plan.columns), 1)
-    inside = column - atom * bonds
-    chosen = jnp.where((inside >= 0) & (inside < bonds), 1.0, 0.0).astype(BF16)
     contract = (((1,), (1,)), ((), ()))
-    by_bond = lax.dot_general(upper, chosen, contract, preferred_element_type=F32)
-    by_bond = by_bond + lax.dot_general(lower, chosen, contract, preferred_element_type=F32)
+    both = lax.dot_general(
+        jnp.concatenate([upper, lower], axis=0), atom_table(plan), contract, preferred_element_type=F32
+    )
+    by_bond = both[: tall.shape[0]] + both[tall.shape[0] :]
     ways = [(i, j) for i in range(3) for j in range(i, 3)]
-    for way, (i, j) in enumerate(ways):
-        pair = dirs_ref[i] * dirs_ref[j]
+    for way in range(len(ways)):
         for row in range(2 * plan.modes):
             values = by_bond[row * padded : row * padded + bonds]
-            v_ref[row * len(ways) + way, :bonds] = values * pair
+            v_ref[row * len(ways) + way, :bonds] = values * pair_ref[way]
 
     def step(chunk, carry):
         first = pl.multiple_of(chunk * 16, 16)
@@ -516,31 +557,11 @@
         out_ref[m, 1] = next_im.astype(BF16)
 
 
-def mode_tables(plan, energy_offset, momentum_offset, absorb):
-    label = (energy_offset - 1) * plan.all_momenta + momentum_offset
-    line = jnp.arange(8, dtype=jnp.int32)
-    shape = (2, 2, plan.classes, 2, plan.devices, 8)
-    wanted = jnp.arange(plan.classes, dtype=jnp.int32)
-    labels = label.reshape(plan.devices, plan.modes)
-    weights = absorb.reshape(plan.devices, plan.modes)
-    inner = line % 4 // 2
-    by_line = sum(jnp.where(inner == i, labels[:, i : i + 1], 0) for i in range(plan.modes))
-    scale = sum(jnp.where(inner == i, weights[:, i : i + 1], 0.0) for i in range(plan.modes))
-    used = (inner < plan.modes)[None, :]
-    same = (by_line[None] == wanted[:, None, None]) & used[None]
-    part = (line % 2)[None, :] == jnp.arange(2, dtype=jnp.int32)[:, None]
-    kind = (line // 4)[None, :] == jnp.arange(2, dtype=jnp.int32)[:, None]
-    hit = (
-        same[None, :, None] & part[None, None, :, None] & kind[:, None, None, None]
-    ).astype(F32)
-    table = jnp.stack([hit, hit * scale[None, None, None]], axis=1)
-    return table.reshape(4 * 2 * plan.classes, plan.devices * 8)
-
-
 def exchange(plan, blocks):
-    routes = [[(i, i ^ k) for i in range(plan.group)] for k in range(plan.group)]
-    moved = [lax.ppermute(blocks[k], GROUP, routes[k]) for k in range(1, plan.group)]
-    return [blocks[0]] + moved
+    moved = [blocks[0]]
+    for partner, block in zip(plan.partners[1:], blocks[1:]):
+        moved.append(lax.ppermute(block, GROUP, [(i, i ^ partner) for i in range(plan.group)]))
+    return moved
 
 
 def dealt(
@@ -549,10 +570,8 @@
     rank = lax.axis_index(GROUP).astype(jnp.int32).reshape(1)
     group, held = plan.group, plan.held
     slots = plan.all_energies * plan.all_momenta * 2
-    mod = np.arange(plan.columns, dtype=np.int32)[None] % plan.bonds
-    table = mode_tables(plan, energy_offset, momentum_offset, absorb)
     lines = 2 * plan.classes
-    picks = jnp.concatenate([table[:lines], table[2 * lines : 3 * lines]], axis=0)
+    modes = plan.devices * plan.modes
 
     message = jax.ShapeDtypeStruct((2, plan.message, LANES), BF16)
     blocks = call(
@@ -560,39 +579,56 @@
         scalars=1, scratch=[pltpu.VMEM((2, plan.entries + plan.tail, LANES), F32)],
         moved=4 * g_less.size * 2,
     )
+    own, d_less, bond_dirs = lax.optimization_barrier((blocks[0], d_less, bond_dirs))
+    blocks = exchange(plan, [own] + list(blocks[1:]))
     small = jax.ShapeDtypeStruct((plan.devices, 8, LANES), F32)
-    coupling = call(functools.partial(couple_kernel, plan), small, d_less, bond_dirs, mod)
-    blocks = exchange(plan, blocks)
+    coupling, table, pairs = call(
+        functools.partial(couple_kernel, plan),
+        [
+            small,
+            jax.ShapeDtypeStruct((4 * lines, plan.devices * 8), F32),
+            jax.ShapeDtypeStruct((6, plan.bonds, plan.atoms), F32),
+        ],
+        d_less.transpose(0, 2, 3, 1, 4), bond_dirs.transpose(1, 0, 2),
+        energy_offset.reshape(1, modes), momentum_offset.reshape(1, modes), absorb.reshape(1, modes),
+        scratch=[pltpu.VMEM((-(-2 * plan.bonds * plan.modes // 16) * 16, plan.atoms), F32)],
+        moved=4 * d_less.size,
+    )
     coupling = lax.all_to_all(coupling, EVERY, 0, 0, tiled=True)
     block_scratch = pltpu.VMEM((slots, held, LANES), F32)
     polar = call(
-        functools.partial(polar_kernel, plan), small, rank, picks, *blocks,
-        scalars=1, scratch=[block_scratch] * 2,
-    )
+        functools.partial(polar_kernel, plan), small, rank, table, *blocks,
+        scalars=1, scratch=[block_scratch] * 2, moved=8 * 2**20,
+    )
+    polar = lax.all_to_all(polar, EVERY, 0, 0, tiled=True)
     answer = jax.ShapeDtypeStruct((plan.message, LANES), BF16)
     sums = call(
         functools.partial(energy_kernel, plan), [answer] * group, rank, table, coupling, *blocks,
         scalars=1,
         scratch=[block_scratch, block_scratch, pltpu.VMEM((4 * lines, LANES), F32)],
-    )
-    polar = lax.all_to_all(polar, EVERY, 0, 0, tiled=True)
+        moved=8 * 2**20,
+    )
     sums = exchange(plan, sums)
+    padded = -(-plan.bonds // 8) * 8
+    d_next = call(
+        functools.partial(next_kernel, plan), jax.ShapeDtypeStruct(d_ret.shape, BF16),
+        polar, d_ret, neighbours, pairs,
+        scratch=[
+            pltpu.VMEM((12 * plan.modes, padded, plan.atoms), F32),
+            pltpu.VMEM((2 * plan.modes, plan.order, plan.order), BF16),
+        ],
+        moved=20 * 2**20,
+    )
+    d_next, own = lax.optimization_barrier((d_next, sums[0]))
     self_energy = call(
-        functools.partial(gather_kernel, plan), jax.ShapeDtypeStruct(g_less.shape, BF16), rank, *sums,
+        functools.partial(gather_kernel, plan), jax.ShapeDtypeStruct(g_less.shape, BF16), rank,
+        own, *sums[1:],
         scalars=1,
         scratch=[
             pltpu.VMEM((plan.slabs, plan.entries, plan.tiles * LANES), F32),
             pltpu.VMEM((plan.slabs, group, plan.rest_pad, LANES), F32),
         ],
-    )
-    padded = -(-plan.bonds // 8) * 8
-    d_next = call(
-        functools.partial(next_kernel, plan), jax.ShapeDtypeStruct(d_ret.shape, BF16),
-        polar, d_ret, neighbours, bond_dirs, mod,
-        scratch=[
-            pltpu.VMEM((12 * plan.modes, padded, plan.atoms), F32),
-            pltpu.VMEM((2 * plan.modes, plan.order, plan.order), BF16),
-        ],
+        moved=4 * 2**20,
     )
     return self_energy, d_next
 

time: 62.7 us -> 54.8 us (0.87)
  waiting for transfers between devices: 13.7 us -> 9.19 us
  local copies, waits for them, and re-layouts: 5 us -> 2.26 us
  other arithmetic: 1.26 us -> 0 us
  starting transfers between devices: 26 us -> 27.1 us
    ppermute x14, starting transfers between devices: 13.3 us -> 18.7 us  [exchange(): lax.ppermute(block, GROUP, [(i, i ^ partner) for i in range(plan.group)])]
    ppermute x14, waiting for transfers between devices: 13.6 us -> 9.18 us  [exchange(): lax.ppermute(block, GROUP, [(i, i ^ partner) for i in range(plan.group)])]
    all_to_all x1, starting transfers between devices: 7.3 us -> 3.97 us  [dealt(): coupling = lax.all_to_all(coupling, EVERY, 0, 0, tiled=True)]
    another operation x1 -> x0, local copies, waits for them, and re-layouts: 1.3 us -> none  [mode_tables(): table = jnp.stack([hit, hit * scale[None, None, None]], axis=1)]
    all_to_all x1, starting transfers between devices: 5.4 us -> 4.48 us  [dealt(): polar = lax.all_to_all(polar, EVERY, 0, 0, tiled=True)]
    another operation x1 -> x0, other arithmetic: 0.73 us -> none  [mode_tables(): table = jnp.stack([hit, hit * scale[None, None, None]], axis=1)]
    reshape x3 -> x0, local copies, waits for them, and re-layouts: 0.72 us -> none  [the longest x1 0.53 us: mode_tables(): return table.reshape(4 * 2 * plan.classes, plan.devices * 8)]
    unnamed x20 -> x18, local copies, waits for them, and re-layouts: 2.62 us -> 2.26 us
  transfers between devices with their start and end apart: 16 -> 16, of which waited for: 6 -> 4; matrix products, arithmetic and copies ran while one was open for 6% -> 0% of each run, Pallas kernels for 12% -> 25%
where the time goes in v2:
time: 54.8 us; the launch traced here: 54.6 us
  starting transfers between devices  27.1 us (49%)
  Pallas kernels  15.3 us (28%)
  waiting for transfers between devices  9.19 us (17%)
  local copies, waits for them, and re-layouts  2.26 us (4%)
  between operations  0.75 us (1%)
    ppermute x14, starting transfers between devices, exchange(): lax.ppermute(block, GROUP, [(i, i ^ partner) for i in range(plan.group)])  18.7 us
    pallas_call x6, Pallas kernels, call(): pl.pallas_call(kernel, out_shape=out_shape, in_specs=specs, out_specs=[vm...  15.3 us
    ppermute x14, waiting for transfers between devices, exchange(): lax.ppermute(block, GROUP, [(i, i ^ partner) for i in range(plan.group)])  9.18 us
    all_to_all x1, starting transfers between devices, dealt(): polar = lax.all_to_all(polar, EVERY, 0, 0, tiled=True)  4.48 us
    all_to_all x1, starting transfers between devices, dealt(): coupling = lax.all_to_all(coupling, EVERY, 0, 0, tiled=True)  3.97 us
    unnamed x18, local copies, waits for them, and re-layouts  2.26 us
  transfers between devices with their start and end apart: 16, of which 4 were waited for; matrix products, arithmetic and copies ran while one was open for 0% of the time, Pallas kernels for 25%

profile of v2, /device:TPU:0, one launch (start us, length us, event | category | flops | bytes accessed | tf_op | source)
XLA Modules:
  0.0 54.6 jit_solution(14528812017272762874)
XLA Ops:
  0.6 0.0 copy-start.8
  0.6 0.0 copy-start.7
  0.7 0.0 copy-start.6
  0.7 0.0 copy-start.1
  0.7 1.1 %copy-done.1 = bf16[2,1,2,144,544]{4,3,2,1,0:T(8,128)(2,1)S(1)} copy-done((bf16[2,1,2,144,544]{4,3,2,1,0:T(8,128)(2,1)S(1)}, bf16[2,1,2,144,544]{4,3,2,1,0:T(8,128)(2,1)}, u32[]{:S(2)}) %copy-start.1) | copy-done | bytes 626712
  1.8 0.0 copy-start.2
  1.8 1.1 %copy-done.2 = bf16[2,1,2,144,544]{4,3,2,1,0:T(8,128)(2,1)S(1)} copy-done((bf16[2,1,2,144,544]{4,3,2,1,0:T(8,128)(2,1)S(1)}, bf16[2,1,2,144,544]{4,3,2,1,0:T(8,128)(2,1)}, u32[]{:S(2)}) %copy-start.2) | copy-done | bytes 626712
  2.9 0.0 copy-start.3
  2.9 0.0 copy-start.4
  2.9 0.4 shard_map.104
  3.3 3.0 %collective-permute-start = (bf16[2,320,128]{2,1,0:T(8,128)(2,1)S(1)}, bf16[2,320,128]{2,1,0:T(8,128)(2,1)S(1)}, u32[]{:S(2)}, u32[]{:S(2)}) collective-permute-start(bf16[2,320,128]{2,1,0:T(8,128)(2,1)S(1)} %get-tuple-element.31), channel_id=1, source_target_pairs={{0,8},{4,12},{8,0},{12,4},{16,24},{20,28},{24,16},{28,20},{1,9},{5... | collective-permute-start | bytes 491528 | tf_op jit(solution)/shard_map/ppermute | solution.py:563
  6.3 1.5 %collective-permute-start.1 = (bf16[2,320,128]{2,1,0:T(8,128)(2,1)S(1)}, bf16[2,320,128]{2,1,0:T(8,128)(2,1)S(1)}, u32[]{:S(2)}, u32[]{:S(2)}) collective-permute-start(bf16[2,320,128]{2,1,0:T(8,128)(2,1)S(1)} %get-tuple-element.32), channel_id=1, source_target_pairs={{0,16},{4,20},{8,24},{12,28},{16,0},{20,4},{24,8},{28,12},{1,17},{... | collective-permute-start | bytes 491528 | tf_op jit(solution)/shard_map/ppermute | solution.py:563
  7.8 0.0 copy-done.8
  7.8 0.0 copy-done.7
  7.8 0.0 copy-done.6
  7.8 0.0 copy-done.3
  7.8 0.0 copy-done.4
  7.8 1.4 %shard_map.105 = (f32[32,8,128]{2,1,0:T(8,128)}, f32[64,256]{1,0:T(8,128)S(1)}, f32[6,17,128]{2,1,0:T(8,128)S(1)}) custom-call(f32[2,9,17,2,128]{4,3,2,1,0:T(2,128)S(1)} %bitcast.6, f32[17,3,128]{2,1,0:T(4,128)S(1)} %bitcast.7, s32[1,64]{1,0:T(1,128)S(1)} %bitcast.8, s32[1,64]{1,0:T(1,128)S(1)} %bitcast.9, f32[1,64]{1,0:T(1,128)S(1)} %bitcast.10), custom_call_target="tpu_custom_call" | custom-call | bytes 313344 | tf_op jit(solution)/shard_map/pallas_call | solution.py:216
  9.3 4.0 %all-to-all-start.1 = ((f32[32,8,128]{2,1,0:T(8,128)}), f32[32,8,128]{2,1,0:T(8,128)S(1)}, u32[]{:S(2)}, u32[]{:S(2)}) async-start(f32[32,8,128]{2,1,0:T(8,128)} %get-tuple-element.39), calls=%async_computation.1 | async-start | bytes 262144 | tf_op jit(solution)/shard_map/all_to_all | solution.py:597
  13.3 2.7 %collective-permute-start.2 = (bf16[2,320,128]{2,1,0:T(8,128)(2,1)S(1)}, bf16[2,320,128]{2,1,0:T(8,128)(2,1)S(1)}, u32[]{:S(2)}, u32[]{:S(2)}) collective-permute-start(bf16[2,320,128]{2,1,0:T(8,128)(2,1)S(1)} %get-tuple-element.33), channel_id=1, source_target_pairs={{0,24},{4,28},{8,16},{12,20},{16,8},{20,12},{24,0},{28,4},{1,25},{... | collective-permute-start | bytes 491528 | tf_op jit(solution)/shard_map/ppermute | solution.py:563
  16.0 0.0 collective-permute-start.3
  16.0 0.5 collective-permute-start.4
  16.5 0.0 collective-permute-done.refs_1_
  16.5 2.1 %collective-permute-start.5 = (bf16[2,320,128]{2,1,0:T(8,128)(2,1)S(1)}, bf16[2,320,128]{2,1,0:T(8,128)(2,1)S(1)}, u32[]{:S(2)}, u32[]{:S(2)}) collective-permute-start(bf16[2,320,128]{2,1,0:T(8,128)(2,1)S(1)} %get-tuple-element.36), channel_id=1, source_target_pairs={{0,28},{4,24},{8,20},{12,16},{16,12},{20,8},{24,4},{28,0},{1,29},{... | collective-permute-start | bytes 491528 | tf_op jit(solution)/shard_map/ppermute | solution.py:563
  18.7 0.0 collective-permute-done.1.refs_2_
  18.7 0.6 %collective-permute-start.6 = (bf16[2,320,128]{2,1,0:T(8,128)(2,1)S(1)}, bf16[2,320,128]{2,1,0:T(8,128)(2,1)S(1)}, u32[]{:S(2)}, u32[]{:S(2)}) collective-permute-start(bf16[2,320,128]{2,1,0:T(8,128)(2,1)S(1)} %get-tuple-element.37), channel_id=1, source_target_pairs={{0,4},{4,0},{8,12},{12,8},{16,20},{20,16},{24,28},{28,24},{1,5},{5... | collective-permute-start | bytes 491528 | tf_op jit(solution)/shard_map/ppermute | solution.py:563
  19.3 3.1 %collective-permute-done.2.refs_3_ = bf16[2,320,128]{2,1,0:T(8,128)(2,1)S(1)} collective-permute-done((bf16[2,320,128]{2,1,0:T(8,128)(2,1)S(1)}, bf16[2,320,128]{2,1,0:T(8,128)(2,1)S(1)}, u32[]{:S(2)}, u32[]{:S(2)}) %collective-permute-start.2) | collective-permute-done | bytes 163872 | tf_op jit(solution)/shard_map/ppermute | solution.py:563
  22.4 2.3 %collective-permute-done.3.refs_4_ = bf16[2,320,128]{2,1,0:T(8,128)(2,1)S(1)} collective-permute-done((bf16[2,320,128]{2,1,0:T(8,128)(2,1)S(1)}, bf16[2,320,128]{2,1,0:T(8,128)(2,1)S(1)}, u32[]{:S(2)}, u32[]{:S(2)}) %collective-permute-start.3) | collective-permute-done | bytes 163872 | tf_op jit(solution)/shard_map/ppermute | solution.py:563
  24.7 0.8 %collective-permute-done.4.refs_5_ = bf16[2,320,128]{2,1,0:T(8,128)(2,1)S(1)} collective-permute-done((bf16[2,320,128]{2,1,0:T(8,128)(2,1)S(1)}, bf16[2,320,128]{2,1,0:T(8,128)(2,1)S(1)}, u32[]{:S(2)}, u32[]{:S(2)}) %collective-permute-start.4) | collective-permute-done | bytes 163872 | tf_op jit(solution)/shard_map/ppermute | solution.py:563
  25.5 3.0 %collective-permute-done.5.refs_6_ = bf16[2,320,128]{2,1,0:T(8,128)(2,1)S(1)} collective-permute-done((bf16[2,320,128]{2,1,0:T(8,128)(2,1)S(1)}, bf16[2,320,128]{2,1,0:T(8,128)(2,1)S(1)}, u32[]{:S(2)}, u32[]{:S(2)}) %collective-permute-start.5) | collective-permute-done | bytes 163872 | tf_op jit(solution)/shard_map/ppermute | solution.py:563
  28.5 0.0 collective-permute-done.6.refs_7_
  28.5 2.6 %shard_map.106 = f32[32,8,128]{2,1,0:T(8,128)} custom-call(s32[1]{0:T(128)} %bitcast.rank_ref, f32[64,256]{1,0:T(8,128)S(1)} %get-tuple-element.29.table_ref.weigh_ref, bf16[2,320,128]{2,1,0:T(8,128)(2,1)S(1)} %get-tuple-element.30.refs_0_, bf16[2,320,128]{2,1,0:T(8,128)(2,1)S(1)} %collective-permute-done.refs_1_, ...), custom_call_target="tpu_custom_call" | custom-call | bytes 8388608 | tf_op jit(solution)/shard_map/pallas_call | solution.py:216
  31.1 0.0 copy-start
  31.1 0.0 copy-start.5
  31.1 0.0 all-to-all-done.1.coupling_ref
  31.1 4.5 %all-to-all-start = ((f32[32,8,128]{2,1,0:T(8,128)}), f32[32,8,128]{2,1,0:T(8,128)S(1)}, u32[]{:S(2)}, u32[]{:S(2)}) async-start(f32[32,8,128]{2,1,0:T(8,128)} %shard_map.106), calls=%async_computation | async-start | bytes 262144 | tf_op jit(solution)/shard_map/all_to_all | solution.py:603
  35.6 2.8 %shard_map.108 = (bf16[320,128]{1,0:T(8,128)(2,1)S(1)}, bf16[320,128]{1,0:T(8,128)(2,1)S(1)}, bf16[320,128]{1,0:T(8,128)(2,1)S(1)}, bf16[320,128]{1,0:T(8,128)(2...) custom-call(s32[1]{0:T(128)} %bitcast.rank_ref, ...), custom_call_target="tpu_custom_call" | custom-call | bytes 8388608 | tf_op jit(solution)/shard_map/pallas_call | solution.py:216
  38.4 1.8 %collective-permute-start.7 = (bf16[320,128]{1,0:T(8,128)(2,1)S(1)}, bf16[320,128]{1,0:T(8,128)(2,1)S(1)}, u32[]{:S(2)}, u32[]{:S(2)}) collective-permute-start(bf16[320,128]{1,0:T(8,128)(2,1)S(1)} %get-tuple-element.42), channel_id=1, source_target_pairs={{0,8},{4,12},{8,0},{12,4},{16,24},{20,28},{24,16},{28,20},{1,9},{5... | collective-permute-start | bytes 245768 | tf_op jit(solution)/shard_map/ppermute | solution.py:563
  40.2 1.5 %collective-permute-start.8 = (bf16[320,128]{1,0:T(8,128)(2,1)S(1)}, bf16[320,128]{1,0:T(8,128)(2,1)S(1)}, u32[]{:S(2)}, u32[]{:S(2)}) collective-permute-start(bf16[320,128]{1,0:T(8,128)(2,1)S(1)} %get-tuple-element.43), channel_id=1, source_target_pairs={{0,16},{4,20},{8,24},{12,28},{16,0},{20,4},{24,8},{28,12},{1,17},{... | collective-permute-start | bytes 245768 | tf_op jit(solution)/shard_map/ppermute | solution.py:563
  41.6 0.3 collective-permute-start.9
  41.9 0.7 %collective-permute-start.10 = (bf16[320,128]{1,0:T(8,128)(2,1)S(1)}, bf16[320,128]{1,0:T(8,128)(2,1)S(1)}, u32[]{:S(2)}, u32[]{:S(2)}) collective-permute-start(bf16[320,128]{1,0:T(8,128)(2,1)S(1)} %get-tuple-element.45), channel_id=1, source_target_pairs={{0,12},{4,8},{8,4},{12,0},{16,28},{20,24},{24,20},{28,16},{1,13},{... | collective-permute-start | bytes 245768 | tf_op jit(solution)/shard_map/ppermute | solution.py:563
  42.6 2.3 %collective-permute-start.11 = (bf16[320,128]{1,0:T(8,128)(2,1)S(1)}, bf16[320,128]{1,0:T(8,128)(2,1)S(1)}, u32[]{:S(2)}, u32[]{:S(2)}) collective-permute-start(bf16[320,128]{1,0:T(8,128)(2,1)S(1)} %get-tuple-element.46), channel_id=1, source_target_pairs={{0,20},{4,16},{8,28},{12,24},{16,4},{20,0},{24,12},{28,8},{1,21},{... | collective-permute-start | bytes 245768 | tf_op jit(solution)/shard_map/ppermute | solution.py:563
  44.9 0.0 collective-permute-done.7.refs_1_
  44.9 0.0 collective-permute-start.12
  44.9 0.0 collective-permute-done.8.refs_2_
  44.9 1.5 %collective-permute-start.13 = (bf16[320,128]{1,0:T(8,128)(2,1)S(1)}, bf16[320,128]{1,0:T(8,128)(2,1)S(1)}, u32[]{:S(2)}, u32[]{:S(2)}) collective-permute-start(bf16[320,128]{1,0:T(8,128)(2,1)S(1)} %get-tuple-element.48), channel_id=1, source_target_pairs={{0,4},{4,0},{8,12},{12,8},{16,20},{20,16},{24,28},{28,24},{1,5},{5... | collective-permute-start | bytes 245768 | tf_op jit(solution)/shard_map/ppermute | solution.py:563
  46.4 0.0 all-to-all-done.polar_ref
  46.4 0.0 copy-done
  46.4 0.0 copy-done.5
  46.4 6.9 %shard_map.107 = bf16[2,2,384,384]{3,2,1,0:T(8,128)(2,1)} custom-call(f32[32,8,128]{2,1,0:T(8,128)S(1)} %all-to-all-done.polar_ref, bf16[2,2,384,384]{3,2,1,0:T(8,128)(2,1)S(1)} %copy-done, s32[17,128]{1,0:T(8,128)S(1)} %copy-done.5, f32[6,17,128]{2,1,0:T(8,128)S(1)} %get-tuple-element.38.pair_ref), custom_call_target="tpu_custom_call" | custom-call | bytes 20971520 | tf_op jit(solution)/shard_map/pallas_call | solution.py:216
  53.4 0.0 collective-permute-done.9.refs_3_
  53.4 0.0 collective-permute-done.10.refs_4_
  53.4 0.0 collective-permute-done.11.refs_5_
  53.4 0.0 collective-permute-done.12.refs_6_
  53.4 0.0 collective-permute-done.13.refs_7_
  53.4 1.2 %shard_map.109 = bf16[2,1,2,144,544]{4,3,2,1,0:T(8,128)(2,1)} custom-call(s32[1]{0:T(128)} %bitcast.rank_ref, bf16[320,128]{1,0:T(8,128)(2,1)S(1)} %get-tuple-element.41.refs_0_, bf16[320,128]{1,0:T(8,128)(2,1)S(1)} %collective-permute-done.7.refs_1_, bf16[320,128]{1,0:T(8,128)(2,1)S(1)} %collective-permute-done.8.refs_2_, ...), custom_call_target="tpu_custom_call" | custom-call | bytes 4194304 | tf_op jit(solution)/shard_map/pallas_call | solution.py:216
Async XLA Ops:
  0.6 7.2 %copy-start.8 = (f32[64]{0:T(128)S(1)}, f32[64]{0:T(128)}, u32[]{:S(2)}) copy-start(f32[64]{0:T(128)} %param.17) | copy-start | bytes 772
  0.6 7.2 %copy-start.7 = (s32[64]{0:T(128)S(1)}, s32[64]{0:T(128)}, u32[]{:S(2)}) copy-start(s32[64]{0:T(128)} %param.16) | copy-start | bytes 772
  0.7 7.2 %copy-start.6 = (s32[64]{0:T(128)S(1)}, s32[64]{0:T(128)}, u32[]{:S(2)}) copy-start(s32[64]{0:T(128)} %param.15) | copy-start | bytes 772
  0.7 1.1 %copy-start.1 = (bf16[2,1,2,144,544]{4,3,2,1,0:T(8,128)(2,1)S(1)}, bf16[2,1,2,144,544]{4,3,2,1,0:T(8,128)(2,1)}, u32[]{:S(2)}) copy-start(bf16[2,1,2,144,544]{4,3,2,1,0:T(8,128)(2,1)} %less_ref.1) | copy-start | bytes 1880068
  1.8 1.1 %copy-start.2 = (bf16[2,1,2,144,544]{4,3,2,1,0:T(8,128)(2,1)S(1)}, bf16[2,1,2,144,544]{4,3,2,1,0:T(8,128)(2,1)}, u32[]{:S(2)}) copy-start(bf16[2,1,2,144,544]{4,3,2,1,0:T(8,128)(2,1)} %great_ref.1) | copy-start | bytes 1880068
  2.9 4.9 %copy-start.3 = (f32[2,2,9,17,128]{4,1,3,2,0:T(2,128)S(1)}, f32[2,2,9,17,128]{4,1,3,2,0:T(2,128)}, u32[]{:S(2)}) copy-start(f32[2,2,9,17,128]{4,1,3,2,0:T(2,128)} %param.11) | copy-start | bytes 940036
  2.9 4.9 %copy-start.4 = (f32[3,17,128]{2,0,1:T(4,128)S(1)}, f32[3,17,128]{2,0,1:T(4,128)}, u32[]{:S(2)}) copy-start(f32[3,17,128]{2,0,1:T(4,128)} %param.14) | copy-start | bytes 78340
  3.3 13.2 %collective-permute-start = (bf16[2,320,128]{2,1,0:T(8,128)(2,1)S(1)}, bf16[2,320,128]{2,1,0:T(8,128)(2,1)S(1)}, u32[]{:S(2)}, u32[]{:S(2)}) collective-permute-start(bf16[2,320,128]{2,1,0:T(8,128)(2,1)S(1)} %get-tuple-element.31), channel_id=1, source_target_pairs={{0,8},{4,12},{8,0},{12,4},{16,24},{20,28},{24,16},{28,20},{1,9},{5... | collective-permute-start | bytes 491528 | tf_op jit(solution)/shard_map/ppermute | solution.py:563
  6.3 12.4 %collective-permute-start.1 = (bf16[2,320,128]{2,1,0:T(8,128)(2,1)S(1)}, bf16[2,320,128]{2,1,0:T(8,128)(2,1)S(1)}, u32[]{:S(2)}, u32[]{:S(2)}) collective-permute-start(bf16[2,320,128]{2,1,0:T(8,128)(2,1)S(1)} %get-tuple-element.32), channel_id=1, source_target_pairs={{0,16},{4,20},{8,24},{12,28},{16,0},{20,4},{24,8},{28,12},{1,17},{... | collective-permute-start | bytes 491528 | tf_op jit(solution)/shard_map/ppermute | solution.py:563
  9.3 21.8 %all-to-all-start.1 = ((f32[32,8,128]{2,1,0:T(8,128)}), f32[32,8,128]{2,1,0:T(8,128)S(1)}, u32[]{:S(2)}, u32[]{:S(2)}) async-start(f32[32,8,128]{2,1,0:T(8,128)} %get-tuple-element.39), calls=%async_computation.1 | async-start | bytes 262144 | tf_op jit(solution)/shard_map/all_to_all | solution.py:597
  13.3 9.2 %collective-permute-start.2 = (bf16[2,320,128]{2,1,0:T(8,128)(2,1)S(1)}, bf16[2,320,128]{2,1,0:T(8,128)(2,1)S(1)}, u32[]{:S(2)}, u32[]{:S(2)}) collective-permute-start(bf16[2,320,128]{2,1,0:T(8,128)(2,1)S(1)} %get-tuple-element.33), channel_id=1, source_target_pairs={{0,24},{4,28},{8,16},{12,20},{16,8},{20,12},{24,0},{28,4},{1,25},{... | collective-permute-start | bytes 491528 | tf_op jit(solution)/shard_map/ppermute | solution.py:563
  16.0 8.7 %collective-permute-start.3 = (bf16[2,320,128]{2,1,0:T(8,128)(2,1)S(1)}, bf16[2,320,128]{2,1,0:T(8,128)(2,1)S(1)}, u32[]{:S(2)}, u32[]{:S(2)}) collective-permute-start(bf16[2,320,128]{2,1,0:T(8,128)(2,1)S(1)} %get-tuple-element.34), channel_id=1, source_target_pairs={{0,12},{4,8},{8,4},{12,0},{16,28},{20,24},{24,20},{28,16},{1,13},{... | collective-permute-start | bytes 491528 | tf_op jit(solution)/shard_map/ppermute | solution.py:563
  16.0 9.5 %collective-permute-start.4 = (bf16[2,320,128]{2,1,0:T(8,128)(2,1)S(1)}, bf16[2,320,128]{2,1,0:T(8,128)(2,1)S(1)}, u32[]{:S(2)}, u32[]{:S(2)}) collective-permute-start(bf16[2,320,128]{2,1,0:T(8,128)(2,1)S(1)} %get-tuple-element.35), channel_id=1, source_target_pairs={{0,20},{4,16},{8,28},{12,24},{16,4},{20,0},{24,12},{28,8},{1,21},{... | collective-permute-start | bytes 491528 | tf_op jit(solution)/shard_map/ppermute | solution.py:563
  16.5 11.9 %collective-permute-start.5 = (bf16[2,320,128]{2,1,0:T(8,128)(2,1)S(1)}, bf16[2,320,128]{2,1,0:T(8,128)(2,1)S(1)}, u32[]{:S(2)}, u32[]{:S(2)}) collective-permute-start(bf16[2,320,128]{2,1,0:T(8,128)(2,1)S(1)} %get-tuple-element.36), channel_id=1, source_target_pairs={{0,28},{4,24},{8,20},{12,16},{16,12},{20,8},{24,4},{28,0},{1,29},{... | collective-permute-start | bytes 491528 | tf_op jit(solution)/shard_map/ppermute | solution.py:563
  18.7 9.8 %collective-permute-start.6 = (bf16[2,320,128]{2,1,0:T(8,128)(2,1)S(1)}, bf16[2,320,128]{2,1,0:T(8,128)(2,1)S(1)}, u32[]{:S(2)}, u32[]{:S(2)}) collective-permute-start(bf16[2,320,128]{2,1,0:T(8,128)(2,1)S(1)} %get-tuple-element.37), channel_id=1, source_target_pairs={{0,4},{4,0},{8,12},{12,8},{16,20},{20,16},{24,28},{28,24},{1,5},{5... | collective-permute-start | bytes 491528 | tf_op jit(solution)/shard_map/ppermute | solution.py:563
  31.1 15.4 %copy-start = (bf16[2,2,384,384]{3,2,1,0:T(8,128)(2,1)S(1)}, bf16[2,2,384,384]{3,2,1,0:T(8,128)(2,1)}, u32[]{:S(2)}) copy-start(bf16[2,2,384,384]{3,2,1,0:T(8,128)(2,1)} %ret_ref.1) | copy-start | bytes 3538948
  31.1 15.4 %copy-start.5 = (s32[17,128]{1,0:T(8,128)S(1)}, s32[17,128]{1,0:T(8,128)}, u32[]{:S(2)}) copy-start(s32[17,128]{1,0:T(8,128)} %near_ref.1) | copy-start | bytes 26116
  31.1 15.3 %all-to-all-start = ((f32[32,8,128]{2,1,0:T(8,128)}), f32[32,8,128]{2,1,0:T(8,128)S(1)}, u32[]{:S(2)}, u32[]{:S(2)}) async-start(f32[32,8,128]{2,1,0:T(8,128)} %shard_map.106), calls=%async_computation | async-start | bytes 262144 | tf_op jit(solution)/shard_map/all_to_all | solution.py:603
  38.4 6.5 %collective-permute-start.7 = (bf16[320,128]{1,0:T(8,128)(2,1)S(1)}, bf16[320,128]{1,0:T(8,128)(2,1)S(1)}, u32[]{:S(2)}, u32[]{:S(2)}) collective-permute-start(bf16[320,128]{1,0:T(8,128)(2,1)S(1)} %get-tuple-element.42), channel_id=1, source_target_pairs={{0,8},{4,12},{8,0},{12,4},{16,24},{20,28},{24,16},{28,20},{1,9},{5... | collective-permute-start | bytes 245768 | tf_op jit(solution)/shard_map/ppermute | solution.py:563
  40.2 4.7 %collective-permute-start.8 = (bf16[320,128]{1,0:T(8,128)(2,1)S(1)}, bf16[320,128]{1,0:T(8,128)(2,1)S(1)}, u32[]{:S(2)}, u32[]{:S(2)}) collective-permute-start(bf16[320,128]{1,0:T(8,128)(2,1)S(1)} %get-tuple-element.43), channel_id=1, source_target_pairs={{0,16},{4,20},{8,24},{12,28},{16,0},{20,4},{24,8},{28,12},{1,17},{... | collective-permute-start | bytes 245768 | tf_op jit(solution)/shard_map/ppermute | solution.py:563
  41.6 11.7 %collective-permute-start.9 = (bf16[320,128]{1,0:T(8,128)(2,1)S(1)}, bf16[320,128]{1,0:T(8,128)(2,1)S(1)}, u32[]{:S(2)}, u32[]{:S(2)}) collective-permute-start(bf16[320,128]{1,0:T(8,128)(2,1)S(1)} %get-tuple-element.44), channel_id=1, source_target_pairs={{0,24},{4,28},{8,16},{12,20},{16,8},{20,12},{24,0},{28,4},{1,25},{... | collective-permute-start | bytes 245768 | tf_op jit(solution)/shard_map/ppermute | solution.py:563
  41.9 11.5 %collective-permute-start.10 = (bf16[320,128]{1,0:T(8,128)(2,1)S(1)}, bf16[320,128]{1,0:T(8,128)(2,1)S(1)}, u32[]{:S(2)}, u32[]{:S(2)}) collective-permute-start(bf16[320,128]{1,0:T(8,128)(2,1)S(1)} %get-tuple-element.45), channel_id=1, source_target_pairs={{0,12},{4,8},{8,4},{12,0},{16,28},{20,24},{24,20},{28,16},{1,13},{... | collective-permute-start | bytes 245768 | tf_op jit(solution)/shard_map/ppermute | solution.py:563
  42.6 10.8 %collective-permute-start.11 = (bf16[320,128]{1,0:T(8,128)(2,1)S(1)}, bf16[320,128]{1,0:T(8,128)(2,1)S(1)}, u32[]{:S(2)}, u32[]{:S(2)}) collective-permute-start(bf16[320,128]{1,0:T(8,128)(2,1)S(1)} %get-tuple-element.46), channel_id=1, source_target_pairs={{0,20},{4,16},{8,28},{12,24},{16,4},{20,0},{24,12},{28,8},{1,21},{... | collective-permute-start | bytes 245768 | tf_op jit(solution)/shard_map/ppermute | solution.py:563
  44.9 8.5 %collective-permute-start.12 = (bf16[320,128]{1,0:T(8,128)(2,1)S(1)}, bf16[320,128]{1,0:T(8,128)(2,1)S(1)}, u32[]{:S(2)}, u32[]{:S(2)}) collective-permute-start(bf16[320,128]{1,0:T(8,128)(2,1)S(1)} %get-tuple-element.47), channel_id=1, source_target_pairs={{0,28},{4,24},{8,20},{12,16},{16,12},{20,8},{24,4},{28,0},{1,29},{... | collective-permute-start | bytes 245768 | tf_op jit(solution)/shard_map/ppermute | solution.py:563
  44.9 8.5 %collective-permute-start.13 = (bf16[320,128]{1,0:T(8,128)(2,1)S(1)}, bf16[320,128]{1,0:T(8,128)(2,1)S(1)}, u32[]{:S(2)}, u32[]{:S(2)}) collective-permute-start(bf16[320,128]{1,0:T(8,128)(2,1)S(1)} %get-tuple-element.48), channel_id=1, source_target_pairs={{0,4},{4,0},{8,12},{12,8},{16,20},{20,16},{24,28},{28,24},{1,5},{5... | collective-permute-start | bytes 245768 | tf_op jit(solution)/shard_map/ppermute | solution.py:563

commit v3 on v2

--- a/solution.py
+++ b/solution.py
@@ -154,7 +154,6 @@
     return (self_energy, d_next)
 
 
-GROUP = ("energy", "momentum")
 EVERY = ("energy", "momentum", "phonon")
 F32 = jnp.float32
 BF16 = jnp.bfloat16
@@ -165,46 +164,38 @@
         self.energies, self.momenta, _, self.entries, self.width = g_shape
         self.modes, _, _, self.bonds, self.atoms = d_shape
         self.order = ret_shape[2]
+        self.n_energy = n_energy
         self.n_momentum = n_momentum
         self.n_phonon = n_phonon
-        self.group = n_energy * n_momentum
-        self.devices = self.group * n_phonon
+        self.devices = n_energy * n_momentum * n_phonon
         self.all_energies = self.energies * n_energy
         self.all_momenta = self.momenta * n_momentum
         self.classes = REACH * self.all_momenta
         self.slabs = 2 * self.energies
         self.tiles = self.width // LANES
         self.rest = self.width % LANES
-        self.halves = self.group // max(self.tiles, 1)
-        self.rows = self.entries // max(self.halves, 1)
-        self.rest_rows = self.entries // self.group
-        self.main_rows = self.slabs * self.rows
+        self.rest_rows = self.entries // n_energy
+        self.main_rows = self.slabs * self.entries
         self.rest_pad = -(-self.rest_rows // 8) * 8
         self.message = -(-(self.main_rows + self.rest_pad) // 16) * 16
         self.tail = self.message - self.main_rows
-        self.held = self.rows + self.rest_pad
+        self.held = self.entries + self.rest_pad
         self.columns = self.width * n_phonon
-        self.partners = sorted(
-            range(self.group), key=lambda k: (k > 0, k < n_momentum, k % n_momentum, k)
-        )
 
     def fits(self):
         return (
             self.momenta == 1
-            and self.group & (self.group - 1) == 0
-            and self.tiles > 0
-            and self.halves * self.tiles == self.group
-            and self.entries % (8 * self.halves) == 0
+            and self.all_momenta == 2
+            and self.n_energy == self.tiles
+            and self.n_energy & (self.n_energy - 1) == 0
             and self.entries % 16 == 0
-            and self.entries % self.group == 0
+            and self.entries % self.n_energy == 0
             and self.rest > 0
             and self.slabs * self.rest == LANES
-            and self.tail >= self.rest_pad
-            and self.modes * 4 <= 8
+            and self.modes <= 2
             and self.atoms == LANES
             and self.order == 3 * self.atoms
             and self.all_energies <= 8
-            and self.all_momenta <= 2
         )
 
 
@@ -224,35 +215,21 @@
     )(*operands)
 
 
-def deal_kernel(plan, rank_ref, less_ref, great_ref, *refs):
-    outs, rest_ref = refs[: plan.group], refs[plan.group]
+def deal_kernel(plan, rank_ref, source_ref, *refs):
+    outs, rest_ref = refs[: plan.n_energy], refs[plan.n_energy]
     rank = rank_ref[0]
-    sources = (less_ref, great_ref)
-    for which, source in enumerate(sources):
-        pieces = [
-            source[e, 0, z, :, plan.tiles * LANES :].astype(F32)
-            for e in range(plan.energies)
-            for z in range(2)
-        ]
-        rest_ref[which, : plan.entries] = jnp.concatenate(pieces, axis=1)
-        rest_ref[which, plan.entries :] = jnp.zeros((plan.tail, LANES), F32)
-    for k, partner in enumerate(plan.partners):
+    slabs = [(e, z) for e in range(plan.energies) for z in range(2)]
+    pieces = [source_ref[e, 0, z, :, plan.tiles * LANES :].astype(F32) for e, z in slabs]
+    rest_ref[: plan.entries] = jnp.concatenate(pieces, axis=1)
+    rest_ref[plan.entries :] = jnp.zeros((plan.tail, LANES), F32)
+    for partner in range(plan.n_energy):
         target = rank ^ partner
-        tile = target // plan.halves
-        half = target % plan.halves
-        lanes = pl.ds(pl.multiple_of(tile * LANES, LANES), LANES)
-        for which, source in enumerate(sources):
-            parts = []
-            for e in range(plan.energies):
-                for z in range(2):
-                    whole = source[e, 0, z, :, lanes].astype(F32)
-                    part = whole[: plan.rows]
-                    for other in range(1, plan.halves):
-                        piece = whole[other * plan.rows : (other + 1) * plan.rows]
-                        part = jnp.where(half == other, piece, part)
-                    parts.append(part)
-            parts.append(rest_ref[which, pl.ds(target * plan.rest_rows, plan.tail), :])
-            outs[k][which] = jnp.concatenate(parts, axis=0).astype(BF16)
+        lanes = pl.ds(pl.multiple_of(target * LANES, LANES), LANES)
+        for slab, (e, z) in enumerate(slabs):
+            rows = slice(slab * plan.entries, (slab + 1) * plan.entries)
+            outs[partner][rows] = source_ref[e, 0, z, :, lanes]
+        rest = rest_ref[pl.ds(target * plan.rest_rows, plan.tail), :]
+        outs[partner][plan.main_rows :] = rest.astype(BF16)
 
 
 def bond_of(plan, shape):
@@ -328,160 +305,144 @@
         for tile in range(plan.tiles):
             main = flat[:, start + tile * LANES : start + (tile + 1) * LANES]
             block = jnp.concatenate([main, rest], axis=0)
-            for half in range(plan.halves):
-                out_ref[(tile * plan.halves + half) * plan.n_phonon + p] = block
+            for half in range(plan.n_momentum):
+                out_ref[(tile * plan.n_momentum + half) * plan.n_phonon + p] = block
     table_ref[...] = mode_table(plan, energy_ref, momentum_ref, absorb_ref)
 
 
-def place_of(plan, source, e, z):
-    energy = plan.energies * (source // plan.n_momentum) + e
-    return (energy * plan.all_momenta + source % plan.n_momentum) * 2 + z
-
-
-def stage_blocks(plan, rank, which, messages, held_ref):
+def stage_blocks(plan, rank, messages, held_ref, stride, offset):
     row = lax.broadcasted_iota(jnp.int32, (plan.rest_pad, LANES), 0)
-    for partner, message in zip(plan.partners, messages):
-        source = rank ^ partner
-        values = message[which].astype(F32)
-        tail = values[plan.main_rows : plan.main_rows + plan.rest_pad]
+    for partner, message in enumerate(messages):
+        first = plan.energies * (rank ^ partner)
+        tail = message[plan.main_rows :].astype(F32)[: plan.rest_pad]
         tail = jnp.where(row < plan.rest_rows, tail, 0.0)
         for e in range(plan.energies):
             for z in range(2):
                 slab = 2 * e + z
-                place = place_of(plan, source, e, z)
-                held_ref[place, : plan.rows] = values[slab * plan.rows : (slab + 1) * plan.rows]
+                place = ((first + e) * stride + offset) * 2 + z
+                rows = slice(slab * plan.entries, (slab + 1) * plan.entries)
+                held_ref[place, : plan.entries] = message[rows].astype(F32)
                 turned = tail if slab == 0 else pltpu.roll(tail, LANES - slab * plan.rest, 1)
-                held_ref[place, plan.rows :] = turned
+                held_ref[place, plan.entries :] = turned
 
 
 def polar_kernel(plan, rank_ref, table_ref, *refs):
-    messages = refs[: plan.group]
-    out_ref, low_ref, high_ref = refs[plan.group :]
+    chips = plan.n_energy
+    out_ref, low_ref, high_ref = refs[3 * chips :]
     rank = rank_ref[0]
-    stage_blocks(plan, rank, 0, messages, low_ref)
-    stage_blocks(plan, rank, 1, messages, high_ref)
-    count, momenta = plan.all_energies, plan.all_momenta
+    stage_blocks(plan, rank, refs[:chips], low_ref, 2, 0)
+    stage_blocks(plan, rank, refs[chips : 2 * chips], low_ref, 2, 1)
+    stage_blocks(plan, rank, refs[2 * chips : 3 * chips], high_ref, 1, 0)
+    count = plan.all_energies
 
     def step(chunk, sums):
         rows = pl.ds(pl.multiple_of(chunk * 8, 8), 8)
         sums = list(sums)
-        for energy_step in range(1, REACH + 1):
-            for q in range(momenta):
-                index = ((energy_step - 1) * momenta + q) * 2
-                for energy in range(energy_step, count):
-                    for k in range(momenta):
-                        low = (energy * momenta + k) * 2
-                        high = ((energy - energy_step) * momenta + (k - q) % momenta) * 2
-                        low_re, low_im = low_ref[low, rows], low_ref[low + 1, rows]
-                        high_re, high_im = high_ref[high, rows], high_ref[high + 1, rows]
-                        sums[index] = sums[index] + (low_re * high_re + low_im * high_im)
-                        sums[index + 1] = sums[index + 1] + (low_im * high_re - low_re * high_im)
+        for energy in range(count):
+            high_re, high_im = high_ref[2 * energy, rows], high_ref[2 * energy + 1, rows]
+            for energy_step in range(1, REACH + 1):
+                if energy + energy_step >= count:
+                    continue
+                for q in range(2):
+                    index = ((energy_step - 1) * 2 + q) * 2
+                    low = ((energy + energy_step) * 2 + q) * 2
+                    low_re, low_im = low_ref[low, rows], low_ref[low + 1, rows]
+                    sums[index] = sums[index] + (low_re * high_re + low_im * high_im)
+                    sums[index + 1] = sums[index + 1] + (low_im * high_re - low_re * high_im)
         return tuple(sums)
 
     none = tuple(jnp.zeros((8, LANES), F32) for _ in range(2 * plan.classes))
-    main = lax.fori_loop(0, plan.rows // 8, step, none)
-    rest = lax.fori_loop(plan.rows // 8, plan.held // 8, step, none)
-    scale = float(count * momenta * plan.entries) ** (-0.5)
+    main = lax.fori_loop(0, plan.entries // 8, step, none)
+    rest = lax.fori_loop(plan.entries // 8, plan.held // 8, step, none)
+    scale = float(count * 2 * plan.entries) ** (-0.5)
     lines = [jnp.sum(part, axis=0, keepdims=True) * scale for part in main + rest]
-    table = jnp.concatenate(lines, axis=0)
+    sums = jnp.concatenate(lines, axis=0)
     lines = 2 * plan.classes
     picks = jnp.concatenate([table_ref[:lines], table_ref[2 * lines : 3 * lines]], axis=0)
     picked = lax.dot_general(
-        picks, table, (((0,), (0,)), ((), ())), precision=HIGH, preferred_element_type=F32
+        picks, sums, (((0,), (0,)), ((), ())), precision=HIGH, preferred_element_type=F32
     )
     out_ref[...] = picked.reshape(out_ref.shape)
 
 
-def energy_kernel(plan, rank_ref, weigh_ref, coupling_ref, *refs):
-    messages = refs[: plan.group]
-    outs = refs[plan.group : 2 * plan.group]
-    low_ref, sum_ref, weight_ref = refs[2 * plan.group :]
+def energy_kernel(plan, rank_ref, table_ref, coupling_ref, *refs):
+    chips = plan.n_energy
+    outs = refs[2 * chips : 3 * chips]
+    low_ref, sum_ref, weight_ref = refs[3 * chips :]
     rank = rank_ref[0]
     flat = coupling_ref[...].reshape(plan.devices * 8, LANES)
-    weight_ref[...] = jnp.dot(weigh_ref[...], flat, precision=HIGH, preferred_element_type=F32)
-    stage_blocks(plan, rank, 0, messages, low_ref)
-    count, momenta = plan.all_energies, plan.all_momenta
+    weight_ref[...] = jnp.dot(table_ref[...], flat, precision=HIGH, preferred_element_type=F32)
+    stage_blocks(plan, rank, refs[:chips], low_ref, 2, 0)
+    stage_blocks(plan, rank, refs[chips : 2 * chips], low_ref, 2, 1)
+    count = plan.all_energies
 
     def run(base):
         def step(chunk, carry):
             rows = pl.ds(pl.multiple_of(chunk * 8, 8), 8)
-            re = [None] * (count * momenta)
-            im = [None] * (count * momenta)
+            re = [None] * count
+            im = [None] * count
             for energy_step in range(1, REACH + 1):
-                for q in range(momenta):
-                    index = base + ((energy_step - 1) * momenta + q) * 2
-                    pairs = []
+                for q in range(2):
+                    index = base + ((energy_step - 1) * 2 + q) * 2
                     for part, sign in ((0, -1), (1, 1)):
                         at = index + part * 2 * plan.classes
                         w_re = jnp.broadcast_to(weight_ref[at : at + 1], (8, LANES))
                         w_im = jnp.broadcast_to(weight_ref[at + 1 : at + 2], (8, LANES))
-                        pairs.append((sign, w_re, w_im))
-                    for energy in range(count):
-                        for k in range(momenta):
-                            slot = energy * momenta + k
-                            for sign, w_re, w_im in pairs:
-                                other = energy + sign * energy_step
-                                if other < 0 or other >= count:
-                                    continue
-                                at = (other * momenta + (k + sign * q) % momenta) * 2
-                                b_re, b_im = low_ref[at, rows], low_ref[at + 1, rows]
-                                t_re = w_re * b_re - w_im * b_im
-                                t_im = w_re * b_im + w_im * b_re
-                                re[slot] = t_re if re[slot] is None else re[slot] + t_re
-                                im[slot] = t_im if im[slot] is None else im[slot] + t_im
-            for slot in range(count * momenta):
-                sum_ref[2 * slot, rows] = re[slot]
-                sum_ref[2 * slot + 1, rows] = im[slot]
+                        for energy in range(count):
+                            other = energy + sign * energy_step
+                            if other < 0 or other >= count:
+                                continue
+                            at = (other * 2 + q) * 2
+                            b_re, b_im = low_ref[at, rows], low_ref[at + 1, rows]
+                            t_re = w_re * b_re - w_im * b_im
+                            t_im = w_re * b_im + w_im * b_re
+                            re[energy] = t_re if re[energy] is None else re[energy] + t_re
+                            im[energy] = t_im if im[energy] is None else im[energy] + t_im
+            for energy in range(count):
+                sum_ref[2 * energy, rows] = re[energy]
+                sum_ref[2 * energy + 1, rows] = im[energy]
             return carry
 
         return step
 
-    lax.fori_loop(0, plan.rows // 8, run(0), 0)
-    lax.fori_loop(plan.rows // 8, plan.held // 8, run(4 * plan.classes), 0)
+    lax.fori_loop(0, plan.entries // 8, run(0), 0)
+    lax.fori_loop(plan.entries // 8, plan.held // 8, run(4 * plan.classes), 0)
     lane = lax.broadcasted_iota(jnp.int32, (plan.rest_pad, LANES), 1)
-    for k, partner in enumerate(plan.partners):
-        target = rank ^ partner
-        parts = []
+    for partner in range(chips):
+        first = plan.energies * (rank ^ partner)
         tail = jnp.zeros((plan.rest_pad, LANES), F32)
-        for e in range(plan.energies):
-            for z in range(2):
-                slab = 2 * e + z
-                place = place_of(plan, target, e, z)
-                parts.append(sum_ref[place, : plan.rows])
-                piece = sum_ref[place, plan.rows :]
-                if slab:
-                    piece = pltpu.roll(piece, slab * plan.rest, 1)
-                mine = (lane >= slab * plan.rest) & (lane < (slab + 1) * plan.rest)
-                tail = jnp.where(mine, piece, tail)
-        parts.append(tail)
+        for slab in range(plan.slabs):
+            place = 2 * first + slab
+            rows = slice(slab * plan.entries, (slab + 1) * plan.entries)
+            outs[partner][rows] = sum_ref[place, : plan.entries].astype(BF16)
+            piece = sum_ref[place, plan.entries :]
+            if slab:
+                piece = pltpu.roll(piece, slab * plan.rest, 1)
+            mine = (lane >= slab * plan.rest) & (lane < (slab + 1) * plan.rest)
+            tail = jnp.where(mine, piece, tail)
         if plan.tail > plan.rest_pad:
-            parts.append(jnp.zeros((plan.tail - plan.rest_pad, LANES), F32))
-        outs[k][...] = jnp.concatenate(parts, axis=0).astype(BF16)
+            blank = jnp.zeros((plan.tail - plan.rest_pad, LANES), F32)
+            tail = jnp.concatenate([tail, blank], axis=0)
+        outs[partner][plan.main_rows :] = tail.astype(BF16)
 
 
 def gather_kernel(plan, rank_ref, *refs):
-    messages = refs[: plan.group]
-    out_ref, wide_ref, rest_ref = refs[plan.group :]
+    chips = plan.n_energy
+    out_ref, rest_ref = refs[chips:]
     rank = rank_ref[0]
-    for partner, message in zip(plan.partners, messages):
+    for partner, message in enumerate(refs[:chips]):
         source = rank ^ partner
-        tile = source // plan.halves
-        half = source % plan.halves
-        values = message[...].astype(F32)
-        lanes = pl.ds(pl.multiple_of(tile * LANES, LANES), LANES)
-        rows = pl.ds(pl.multiple_of(half * plan.rows, 8), plan.rows)
-        tail = values[plan.main_rows : plan.main_rows + plan.rest_pad]
+        lanes = pl.ds(pl.multiple_of(source * LANES, LANES), LANES)
+        tail = message[plan.main_rows :].astype(F32)[: plan.rest_pad]
         for slab in range(plan.slabs):
-            wide_ref[slab, rows, lanes] = values[slab * plan.rows : (slab + 1) * plan.rows]
+            rows = slice(slab * plan.entries, (slab + 1) * plan.entries)
+            out_ref[slab // 2, 0, slab % 2, :, lanes] = message[rows]
             turned = tail if slab == 0 else pltpu.roll(tail, LANES - slab * plan.rest, 1)
             rest_ref[slab, source] = turned
-    for e in range(plan.energies):
-        for z in range(2):
-            slab = 2 * e + z
-            parts = [rest_ref[slab, source, : plan.rest_rows] for source in range(plan.group)]
-            rest = jnp.concatenate(parts, axis=0)[:, : plan.rest]
-            whole = jnp.concatenate([wide_ref[slab], rest], axis=1)
-            out_ref[e, 0, z] = whole.astype(BF16)
+    for slab in range(plan.slabs):
+        parts = [rest_ref[slab, source, : plan.rest_rows] for source in range(chips)]
+        rest = jnp.concatenate(parts, axis=0)[:, : plan.rest]
+        out_ref[slab // 2, 0, slab % 2, :, plan.tiles * LANES :] = rest.astype(BF16)
 
 
 def next_kernel(plan, polar_ref, ret_ref, near_ref, pair_ref, out_ref, v_ref, dense_ref):
@@ -492,8 +453,8 @@
         rest = jnp.zeros((4, LANES), F32)
         for tile in range(plan.tiles):
             main = jnp.zeros((4, LANES), F32)
-            for half in range(plan.halves):
-                block = polar_ref[(tile * plan.halves + half) * plan.n_phonon + p]
+            for half in range(plan.n_momentum):
+                block = polar_ref[(tile * plan.n_momentum + half) * plan.n_phonon + p]
                 main = main + block[:4]
                 rest = rest + block[4:]
             lines.append(main)
@@ -527,60 +488,67 @@
                 for way in range(len(ways)):
                     value = v_ref[row * len(ways) + way, n : n + 1]
                     sums[way] = sums[way] + jnp.where(hit, value, 0.0)
+            m, z = row // 2, row % 2
             for way, (i, j) in enumerate(ways):
                 block = sums[way].astype(BF16)
-                dense_ref[
-                    row, pl.ds(pl.multiple_of(j * atoms + first, 16), 16), i * atoms : (i + 1) * atoms
-                ] = block
-                if i != j:
-                    dense_ref[
-                        row,
-                        pl.ds(pl.multiple_of(i * atoms + first, 16), 16),
-                        j * atoms : (j + 1) * atoms,
-                    ] = block
+                other = block if z else (-sums[way]).astype(BF16)
+                for up, left in {(j, i), (i, j)}:
+                    place = pl.multiple_of(up * atoms + first, 16)
+                    columns = left * atoms
+                    dense_ref[m, pl.ds(place, 16), pl.ds(z * order + columns, atoms)] = block
+                    place = pl.multiple_of(order + up * atoms + first, 16)
+                    dense_ref[m, pl.ds(place, 16), pl.ds((1 - z) * order + columns, atoms)] = other
         return carry
 
     lax.fori_loop(0, atoms // 16, step, 0)
-    plain = (((1,), (0,)), ((), ()))
     for m in range(plan.modes):
-        ret_re, ret_im = ret_ref[m, 0], ret_ref[m, 1]
-        dense_re, dense_im = dense_ref[2 * m], dense_ref[2 * m + 1]
-
-        def times(left, right, how):
-            return lax.dot_general(left, right, how, preferred_element_type=F32)
-
-        half_re = (times(ret_re, dense_re, plain) + times(ret_im, dense_im, plain)).astype(BF16)
-        half_im = (times(ret_re, dense_im, plain) - times(ret_im, dense_re, plain)).astype(BF16)
-        next_re = times(ret_re, half_re, contract) - times(ret_im, half_im, contract)
-        next_im = times(ret_re, half_im, contract) + times(ret_im, half_re, contract)
-        out_ref[m, 0] = next_re.astype(BF16)
-        out_ref[m, 1] = next_im.astype(BF16)
-
-
-def exchange(plan, blocks):
-    moved = [blocks[0]]
-    for partner, block in zip(plan.partners[1:], blocks[1:]):
-        moved.append(lax.ppermute(block, GROUP, [(i, i ^ partner) for i in range(plan.group)]))
-    return moved
+        ret = jnp.concatenate([ret_ref[m, 0], ret_ref[m, 1]], axis=1)
+        half = jnp.dot(ret, dense_ref[m], preferred_element_type=F32).astype(BF16)
+        half_re, half_im = half[:, :order], half[:, order:]
+        right = jnp.concatenate(
+            [
+                jnp.concatenate([half_re, -half_im], axis=1),
+                jnp.concatenate([half_im, half_re], axis=1),
+            ],
+            axis=0,
+        )
+        after = lax.dot_general(ret, right, contract, preferred_element_type=F32)
+        out_ref[m, 0] = after[:, :order].astype(BF16)
+        out_ref[m, 1] = after[:, order:].astype(BF16)
+
+
+def swap(block, axis, distance):
+    return lax.ppermute(block, axis, [(i, i ^ distance) for i in range(lax.axis_size(axis))])
+
+
+def to_chips(plan, blocks):
+    return [blocks[0]] + [swap(blocks[k], "energy", k) for k in range(1, plan.n_energy)]
 
 
 def dealt(
     plan, g_less, g_great, d_less, d_ret, neighbours, bond_dirs, energy_offset, momentum_offset, absorb
 ):
-    rank = lax.axis_index(GROUP).astype(jnp.int32).reshape(1)
-    group, held = plan.group, plan.held
-    slots = plan.all_energies * plan.all_momenta * 2
+    rank = lax.axis_index("energy").astype(jnp.int32).reshape(1)
+    chips, held, count = plan.n_energy, plan.held, plan.all_energies
     lines = 2 * plan.classes
     modes = plan.devices * plan.modes
-
-    message = jax.ShapeDtypeStruct((2, plan.message, LANES), BF16)
-    blocks = call(
-        functools.partial(deal_kernel, plan), [message] * group, rank, g_less, g_great,
-        scalars=1, scratch=[pltpu.VMEM((2, plan.entries + plan.tail, LANES), F32)],
-        moved=4 * g_less.size * 2,
-    )
-    own, d_less, bond_dirs = lax.optimization_barrier((blocks[0], d_less, bond_dirs))
-    blocks = exchange(plan, [own] + list(blocks[1:]))
+    message = jax.ShapeDtypeStruct((plan.message, LANES), BF16)
+
+    def deal(blocks):
+        return call(
+            functools.partial(deal_kernel, plan), [message] * chips, rank, blocks,
+            scalars=1, scratch=[pltpu.VMEM((plan.entries + plan.tail, LANES), F32)],
+            moved=4 * blocks.size,
+        )
+
+    low_blocks = deal(g_less)
+    own, g_great = lax.optimization_barrier((low_blocks[0], g_great))
+    low_blocks = [own] + list(low_blocks[1:])
+    low = to_chips(plan, low_blocks)
+    high_blocks = deal(g_great)
+    own, d_less, bond_dirs = lax.optimization_barrier((high_blocks[0], d_less, bond_dirs))
+    high = to_chips(plan, [own] + list(high_blocks[1:]))
+    low_beside = [swap(block, "momentum", 1) for block in low]
     small = jax.ShapeDtypeStruct((plan.devices, 8, LANES), F32)
     coupling, table, pairs = call(
         functools.partial(couple_kernel, plan),
@@ -595,27 +563,27 @@
         moved=4 * d_less.size,
     )
     coupling = lax.all_to_all(coupling, EVERY, 0, 0, tiled=True)
-    block_scratch = pltpu.VMEM((slots, held, LANES), F32)
+    low_scratch = pltpu.VMEM((4 * count, held, LANES), F32)
+    half_scratch = pltpu.VMEM((2 * count, held, LANES), F32)
     polar = call(
-        functools.partial(polar_kernel, plan), small, rank, table, *blocks,
-        scalars=1, scratch=[block_scratch] * 2, moved=8 * 2**20,
+        functools.partial(polar_kernel, plan), small, rank, table, *low, *low_beside, *high,
+        scalars=1, scratch=[low_scratch, half_scratch], moved=8 * 2**20,
     )
     polar = lax.all_to_all(polar, EVERY, 0, 0, tiled=True)
-    answer = jax.ShapeDtypeStruct((plan.message, LANES), BF16)
     sums = call(
-        functools.partial(energy_kernel, plan), [answer] * group, rank, table, coupling, *blocks,
-        scalars=1,
-        scratch=[block_scratch, block_scratch, pltpu.VMEM((4 * lines, LANES), F32)],
+        functools.partial(energy_kernel, plan), [message] * chips,
+        rank, table, coupling, *low, *low_beside,
+        scalars=1, scratch=[low_scratch, half_scratch, pltpu.VMEM((4 * lines, LANES), F32)],
         moved=8 * 2**20,
     )
-    sums = exchange(plan, sums)
+    sums = to_chips(plan, sums)
     padded = -(-plan.bonds // 8) * 8
     d_next = call(
         functools.partial(next_kernel, plan), jax.ShapeDtypeStruct(d_ret.shape, BF16),
         polar, d_ret, neighbours, pairs,
         scratch=[
             pltpu.VMEM((12 * plan.modes, padded, plan.atoms), F32),
-            pltpu.VMEM((2 * plan.modes, plan.order, plan.order), BF16),
+            pltpu.VMEM((plan.modes, 2 * plan.order, 2 * plan.order), BF16),
         ],
         moved=20 * 2**20,
     )
@@ -623,11 +591,7 @@
     self_energy = call(
         functools.partial(gather_kernel, plan), jax.ShapeDtypeStruct(g_less.shape, BF16), rank,
         own, *sums[1:],
-        scalars=1,
-        scratch=[
-            pltpu.VMEM((plan.slabs, plan.entries, plan.tiles * LANES), F32),
-            pltpu.VMEM((plan.slabs, group, plan.rest_pad, LANES), F32),
-        ],
+        scalars=1, scratch=[pltpu.VMEM((plan.slabs, chips, plan.rest_pad, LANES), F32)],
         moved=4 * 2**20,
     )
     return self_energy, d_next

time: 54.8 us -> 49.4 us (0.901)
  starting transfers between devices: 27.1 us -> 23.7 us
  Pallas kernels: 15.3 us -> 14.1 us
  local copies, waits for them, and re-layouts: 2.26 us -> 1.15 us
    ppermute x14 -> x13, starting transfers between devices: 18.7 us -> 14.1 us  [swap(): lax.ppermute(block, axis, [(i, i ^ distance) for i in range(lax.axis_size...]
    all_to_all x1, waiting for transfers between devices: 0.01 us -> 2.09 us  [dealt(): polar = lax.all_to_all(polar, EVERY, 0, 0, tiled=True)]
    ppermute x14 -> x13, waiting for transfers between devices: 9.18 us -> 7.3 us  [swap(): lax.ppermute(block, axis, [(i, i ^ distance) for i in range(lax.axis_size...]
    pallas_call x6 -> x7, Pallas kernels: 15.3 us -> 14.1 us  [call(): pl.pallas_call(kernel, out_shape=out_shape, in_specs=specs, out_specs=[vm...]
    unnamed x18, local copies, waits for them, and re-layouts: 2.26 us -> 1.15 us
    all_to_all x1, starting transfers between devices: 3.97 us -> 4.92 us  [dealt(): coupling = lax.all_to_all(coupling, EVERY, 0, 0, tiled=True)]
  transfers between devices with their start and end apart: 16 -> 15, of which waited for: 4 -> 2; matrix products, arithmetic and copies ran while one was open for 0% -> 0% of each run, Pallas kernels for 25% -> 26%
where the time goes in v3:
time: 49.4 us; the launch traced here: 49.1 us
  starting transfers between devices  23.7 us (48%)
  Pallas kernels  14.1 us (29%)
  waiting for transfers between devices  9.39 us (19%)
  local copies, waits for them, and re-layouts  1.15 us (2%)
  between operations  0.75 us (2%)
    pallas_call x7, Pallas kernels, call(): pl.pallas_call(kernel, out_shape=out_shape, in_specs=specs, out_specs=[vm...  14.1 us
    ppermute x13, starting transfers between devices, swap(): lax.ppermute(block, axis, [(i, i ^ distance) for i in range(lax.axis_size...  14.1 us
    ppermute x13, waiting for transfers between devices, swap(): lax.ppermute(block, axis, [(i, i ^ distance) for i in range(lax.axis_size...  7.3 us
    all_to_all x1, starting transfers between devices, dealt(): coupling = lax.all_to_all(coupling, EVERY, 0, 0, tiled=True)  4.92 us
    all_to_all x1, starting transfers between devices, dealt(): polar = lax.all_to_all(polar, EVERY, 0, 0, tiled=True)  4.72 us
    all_to_all x1, waiting for transfers between devices, dealt(): polar = lax.all_to_all(polar, EVERY, 0, 0, tiled=True)  2.09 us
    unnamed x18, local copies, waits for them, and re-layouts  1.15 us
  transfers between devices with their start and end apart: 15, of which 2 were waited for; matrix products, arithmetic and copies ran while one was open for 0% of the time, Pallas kernels for 26%

profile of v3, /device:TPU:0, one launch (start us, length us, event | category | flops | bytes accessed | tf_op | source)
XLA Modules:
  0.0 49.1 jit_solution(9229032560428083082)
XLA Ops:
  0.6 0.0 copy-start.8
  0.6 0.0 copy-start.7
  0.7 0.0 copy-start.6
  0.7 0.0 copy-start.1
  0.7 1.1 %copy-done.1 = bf16[2,1,2,144,544]{4,3,2,1,0:T(8,128)(2,1)S(1)} copy-done((bf16[2,1,2,144,544]{4,3,2,1,0:T(8,128)(2,1)S(1)}, bf16[2,1,2,144,544]{4,3,2,1,0:T(8,128)(2,1)}, u32[]{:S(2)}) %copy-start.1) | copy-done | bytes 626712
  1.8 0.0 copy-start.2
  1.8 0.0 copy-start.3
  1.8 0.0 copy-start.4
  1.8 0.1 shard_map.104
  1.9 0.5 %collective-permute-start.3 = (bf16[624,128]{1,0:T(8,128)(2,1)S(1)}, bf16[624,128]{1,0:T(8,128)(2,1)S(1)}, u32[]{:S(2)}, u32[]{:S(2)}) collective-permute-start(bf16[624,128]{1,0:T(8,128)(2,1)S(1)} %get-tuple-element.30.refs_0_), channel_id=1, source_target_pairs={{0,4},{4,0},{1,5},{5,1},{2,6},{6,2},{3,7},{7,3},{8,12},{12,8},{9,1... | collective-permute-start | bytes 479240 | tf_op jit(solution)/shard_map/ppermute | solution.py:521
  2.4 2.6 %collective-permute-start = (bf16[624,128]{1,0:T(8,128)(2,1)S(1)}, bf16[624,128]{1,0:T(8,128)(2,1)S(1)}, u32[]{:S(2)}, u32[]{:S(2)}) collective-permute-start(bf16[624,128]{1,0:T(8,128)(2,1)S(1)} %get-tuple-element.31), channel_id=1, source_target_pairs={{0,8},{8,0},{16,24},{24,16},{1,9},{9,1},{17,25},{25,17},{2,10},{10... | collective-permute-start | bytes 479240 | tf_op jit(solution)/shard_map/ppermute | solution.py:521
  5.0 1.5 %collective-permute-start.1 = (bf16[624,128]{1,0:T(8,128)(2,1)S(1)}, bf16[624,128]{1,0:T(8,128)(2,1)S(1)}, u32[]{:S(2)}, u32[]{:S(2)}) collective-permute-start(bf16[624,128]{1,0:T(8,128)(2,1)S(1)} %get-tuple-element.32), channel_id=1, source_target_pairs={{0,16},{8,24},{16,0},{24,8},{1,17},{9,25},{17,1},{25,9},{2,18},{10... | collective-permute-start | bytes 479240 | tf_op jit(solution)/shard_map/ppermute | solution.py:521
  6.5 0.0 collective-permute-start.2
  6.6 0.0 copy-done.2
  6.6 0.1 shard_map.105
  6.7 2.0 %collective-permute-start.7 = (bf16[624,128]{1,0:T(8,128)(2,1)S(1)}, bf16[624,128]{1,0:T(8,128)(2,1)S(1)}, u32[]{:S(2)}, u32[]{:S(2)}) collective-permute-start(bf16[624,128]{1,0:T(8,128)(2,1)S(1)} %get-tuple-element.35), channel_id=1, source_target_pairs={{0,8},{8,0},{16,24},{24,16},{1,9},{9,1},{17,25},{25,17},{2,10},{10... | collective-permute-start | bytes 479240 | tf_op jit(solution)/shard_map/ppermute | solution.py:521
  8.7 0.0 copy-done.8
  8.7 0.0 copy-done.7
  8.7 0.0 copy-done.6
  8.7 0.0 copy-done.3
  8.7 0.0 copy-done.4
  8.7 1.4 %shard_map.106 = (f32[32,8,128]{2,1,0:T(8,128)}, f32[64,256]{1,0:T(8,128)S(1)}, f32[6,17,128]{2,1,0:T(8,128)S(1)}) custom-call(f32[2,9,17,2,128]{4,3,2,1,0:T(2,128)S(1)} %bitcast.6, f32[17,3,128]{2,1,0:T(4,128)S(1)} %bitcast.7, s32[1,64]{1,0:T(1,128)S(1)} %bitcast.8, s32[1,64]{1,0:T(1,128)S(1)} %bitcast.9, f32[1,64]{1,0:T(1,128)S(1)} %bitcast.10), custom_call_target="tpu_custom_call" | custom-call | bytes 313344 | tf_op jit(solution)/shard_map/pallas_call | solution.py:207
  10.2 4.9 %all-to-all-start.1 = ((f32[32,8,128]{2,1,0:T(8,128)}), f32[32,8,128]{2,1,0:T(8,128)S(1)}, u32[]{:S(2)}, u32[]{:S(2)}) async-start(f32[32,8,128]{2,1,0:T(8,128)} %get-tuple-element.39), calls=%async_computation.1 | async-start | bytes 262144 | tf_op jit(solution)/shard_map/all_to_all | solution.py:565
  15.1 0.0 collective-permute-done.3.refs_4_
  15.1 1.8 %collective-permute-start.8 = (bf16[624,128]{1,0:T(8,128)(2,1)S(1)}, bf16[624,128]{1,0:T(8,128)(2,1)S(1)}, u32[]{:S(2)}, u32[]{:S(2)}) collective-permute-start(bf16[624,128]{1,0:T(8,128)(2,1)S(1)} %get-tuple-element.36), channel_id=1, source_target_pairs={{0,16},{8,24},{16,0},{24,8},{1,17},{9,25},{17,1},{25,9},{2,18},{10... | collective-permute-start | bytes 479240 | tf_op jit(solution)/shard_map/ppermute | solution.py:521
  16.9 0.0 collective-permute-done.refs_1_
  16.9 1.5 %collective-permute-start.9 = (bf16[624,128]{1,0:T(8,128)(2,1)S(1)}, bf16[624,128]{1,0:T(8,128)(2,1)S(1)}, u32[]{:S(2)}, u32[]{:S(2)}) collective-permute-start(bf16[624,128]{1,0:T(8,128)(2,1)S(1)} %get-tuple-element.37), channel_id=1, source_target_pairs={{0,24},{8,16},{16,8},{24,0},{1,25},{9,17},{17,9},{25,1},{2,26},{10... | collective-permute-start | bytes 479240 | tf_op jit(solution)/shard_map/ppermute | solution.py:521
  18.4 0.0 collective-permute-done.1.refs_2_
  18.4 0.0 collective-permute-start.4
  18.4 0.0 collective-permute-done.2.refs_3_
  18.4 0.5 %collective-permute-start.5 = (bf16[624,128]{1,0:T(8,128)(2,1)S(1)}, bf16[624,128]{1,0:T(8,128)(2,1)S(1)}, u32[]{:S(2)}, u32[]{:S(2)}) collective-permute-start(bf16[624,128]{1,0:T(8,128)(2,1)S(1)} %collective-permute-done.1.refs_2_), channel_id=1, source_target_pairs={{0,4},{4,0},{1,5},{5,1},{2,6},{6,2},{3,7},{7,3},{8,12},{12,8},{9,1... | collective-permute-start | bytes 479240 | tf_op jit(solution)/shard_map/ppermute | solution.py:521
  18.9 0.0 collective-permute-done.7.refs_9_
  18.9 0.1 collective-permute-start.6
  19.0 7.3 %collective-permute-done.8.refs_10_ = bf16[624,128]{1,0:T(8,128)(2,1)S(1)} collective-permute-done((bf16[624,128]{1,0:T(8,128)(2,1)S(1)}, bf16[624,128]{1,0:T(8,128)(2,1)S(1)}, u32[]{:S(2)}, u32[]{:S(2)}) %collective-permute-start.8) | collective-permute-done | bytes 159776 | tf_op jit(solution)/shard_map/ppermute | solution.py:521
  26.3 0.0 collective-permute-done.9.refs_11_
  26.3 0.0 collective-permute-done.4.refs_5_
  26.3 0.0 collective-permute-done.5.refs_6_
  26.3 0.0 collective-permute-done.6.refs_7_
  26.3 2.6 %shard_map.107 = f32[32,8,128]{2,1,0:T(8,128)} custom-call(s32[1]{0:T(128)} %bitcast.rank_ref, f32[64,256]{1,0:T(8,128)S(1)} %get-tuple-element.29.table_ref, bf16[624,128]{1,0:T(8,128)(2,1)S(1)} %get-tuple-element.30.refs_0_, bf16[624,128]{1,0:T(8,128)(2,1)S(1)} %collective-permute-done.refs_1_, bf16[624,128]{1,0:T(8,128)(2,1)S(1)} %collective-permute-done.1.refs_2_, ...), custom_call_target="tpu_custom_call" | custom-call | bytes 8388608 | tf_op jit(solution)/shard_map/pallas_call | solution.py:207
  28.9 0.0 copy-start
  28.9 0.0 copy-start.5
  28.9 0.0 all-to-all-done.1.coupling_ref
  28.9 4.7 %all-to-all-start = ((f32[32,8,128]{2,1,0:T(8,128)}), f32[32,8,128]{2,1,0:T(8,128)S(1)}, u32[]{:S(2)}, u32[]{:S(2)}) async-start(f32[32,8,128]{2,1,0:T(8,128)} %shard_map.107), calls=%async_computation | async-start | bytes 262144 | tf_op jit(solution)/shard_map/all_to_all | solution.py:572
  33.6 2.9 %shard_map.109 = (bf16[624,128]{1,0:T(8,128)(2,1)S(1)}, bf16[624,128]{1,0:T(8,128)(2,1)S(1)}, bf16[624,128]{1,0:T(8,128)(2,1)S(1)}, bf16[624,128]{1,0:T(8,128)(2,1)S(1)}) custom-call(s32[1]{0:T(128)} %bitcast.rank_ref, f32[64,256]{1,0:T(8,128)S(1)} %get-tuple-element.29.table_ref, f32[32,8,128]{2,1,0:T(8,128)S(1)} %all-to-all-done.1.coupling_ref, ...), custom_call_target="tpu_custom_call" | custom-call | bytes 8388608 | tf_op jit(solution)/shard_map/pallas_call | solution.py:207
  36.5 1.8 %collective-permute-start.10 = (bf16[624,128]{1,0:T(8,128)(2,1)S(1)}, bf16[624,128]{1,0:T(8,128)(2,1)S(1)}, u32[]{:S(2)}, u32[]{:S(2)}) collective-permute-start(bf16[624,128]{1,0:T(8,128)(2,1)S(1)} %get-tuple-element.42), channel_id=1, source_target_pairs={{0,8},{8,0},{16,24},{24,16},{1,9},{9,1},{17,25},{25,17},{2,10},{10... | collective-permute-start | bytes 479240 | tf_op jit(solution)/shard_map/ppermute | solution.py:521
  38.3 1.5 %collective-permute-start.11 = (bf16[624,128]{1,0:T(8,128)(2,1)S(1)}, bf16[624,128]{1,0:T(8,128)(2,1)S(1)}, u32[]{:S(2)}, u32[]{:S(2)}) collective-permute-start(bf16[624,128]{1,0:T(8,128)(2,1)S(1)} %get-tuple-element.43), channel_id=1, source_target_pairs={{0,16},{8,24},{16,0},{24,8},{1,17},{9,25},{17,1},{25,9},{2,18},{10... | collective-permute-start | bytes 479240 | tf_op jit(solution)/shard_map/ppermute | solution.py:521
  39.8 0.3 collective-permute-start.12
  40.0 2.1 %all-to-all-done.polar_ref = f32[32,8,128]{2,1,0:T(8,128)S(1)} async-done(((f32[32,8,128]{2,1,0:T(8,128)}), f32[32,8,128]{2,1,0:T(8,128)S(1)}, u32[]{:S(2)}, u32[]{:S(2)}) %all-to-all-start) | async-done | bytes 131104 | tf_op jit(solution)/shard_map/all_to_all | solution.py:572
  42.1 0.0 copy-done
  42.1 0.0 copy-done.5
  42.1 6.0 %shard_map.108 = bf16[2,2,384,384]{3,2,1,0:T(8,128)(2,1)} custom-call(f32[32,8,128]{2,1,0:T(8,128)S(1)} %all-to-all-done.polar_ref, bf16[2,2,384,384]{3,2,1,0:T(8,128)(2,1)S(1)} %copy-done, s32[17,128]{1,0:T(8,128)S(1)} %copy-done.5, f32[6,17,128]{2,1,0:T(8,128)S(1)} %get-tuple-element.38.pair_ref), custom_call_target="tpu_custom_call" | custom-call | bytes 20971520 | tf_op jit(solution)/shard_map/pallas_call | solution.py:207
  48.1 0.0 collective-permute-done.10.refs_1_
  48.1 0.0 collective-permute-done.11.refs_2_
  48.1 0.0 collective-permute-done.12.refs_3_
  48.1 1.0 %shard_map.110 = bf16[2,1,2,144,544]{4,3,2,1,0:T(8,128)(2,1)} custom-call(s32[1]{0:T(128)} %bitcast.rank_ref, bf16[624,128]{1,0:T(8,128)(2,1)S(1)} %get-tuple-element.41.refs_0_, bf16[624,128]{1,0:T(8,128)(2,1)S(1)} %collective-permute-done.10.refs_1_, bf16[624,128]{1,0:T(8,128)(2,1)S(1)} %collective-permute-done.11.refs_2_, ...), custom_call_target="tpu_custom_call" | custom-call | bytes 4194304 | tf_op jit(solution)/shard_map/pallas_call | solution.py:207
Async XLA Ops:
  0.6 8.1 %copy-start.8 = (f32[64]{0:T(128)S(1)}, f32[64]{0:T(128)}, u32[]{:S(2)}) copy-start(f32[64]{0:T(128)} %param.17) | copy-start | bytes 772
  0.6 8.1 %copy-start.7 = (s32[64]{0:T(128)S(1)}, s32[64]{0:T(128)}, u32[]{:S(2)}) copy-start(s32[64]{0:T(128)} %param.16) | copy-start | bytes 772
  0.7 8.1 %copy-start.6 = (s32[64]{0:T(128)S(1)}, s32[64]{0:T(128)}, u32[]{:S(2)}) copy-start(s32[64]{0:T(128)} %param.15) | copy-start | bytes 772
  0.7 1.1 %copy-start.1 = (bf16[2,1,2,144,544]{4,3,2,1,0:T(8,128)(2,1)S(1)}, bf16[2,1,2,144,544]{4,3,2,1,0:T(8,128)(2,1)}, u32[]{:S(2)}) copy-start(bf16[2,1,2,144,544]{4,3,2,1,0:T(8,128)(2,1)} %source_ref.1) | copy-start | bytes 1880068
  1.8 4.8 %copy-start.2 = (bf16[2,1,2,144,544]{4,3,2,1,0:T(8,128)(2,1)S(1)}, bf16[2,1,2,144,544]{4,3,2,1,0:T(8,128)(2,1)}, u32[]{:S(2)}) copy-start(bf16[2,1,2,144,544]{4,3,2,1,0:T(8,128)(2,1)} %source_ref.2) | copy-start | bytes 1880068
  1.8 6.9 %copy-start.3 = (f32[2,2,9,17,128]{4,1,3,2,0:T(2,128)S(1)}, f32[2,2,9,17,128]{4,1,3,2,0:T(2,128)}, u32[]{:S(2)}) copy-start(f32[2,2,9,17,128]{4,1,3,2,0:T(2,128)} %param.11) | copy-start | bytes 940036
  1.8 6.9 %copy-start.4 = (f32[3,17,128]{2,0,1:T(4,128)S(1)}, f32[3,17,128]{2,0,1:T(4,128)}, u32[]{:S(2)}) copy-start(f32[3,17,128]{2,0,1:T(4,128)} %param.14) | copy-start | bytes 78340
  1.9 13.2 %collective-permute-start.3 = (bf16[624,128]{1,0:T(8,128)(2,1)S(1)}, bf16[624,128]{1,0:T(8,128)(2,1)S(1)}, u32[]{:S(2)}, u32[]{:S(2)}) collective-permute-start(bf16[624,128]{1,0:T(8,128)(2,1)S(1)} %get-tuple-element.30.refs_0_), channel_id=1, source_target_pairs={{0,4},{4,0},{1,5},{5,1},{2,6},{6,2},{3,7},{7,3},{8,12},{12,8},{9,1... | collective-permute-start | bytes 479240 | tf_op jit(solution)/shard_map/ppermute | solution.py:521
  2.4 14.5 %collective-permute-start = (bf16[624,128]{1,0:T(8,128)(2,1)S(1)}, bf16[624,128]{1,0:T(8,128)(2,1)S(1)}, u32[]{:S(2)}, u32[]{:S(2)}) collective-permute-start(bf16[624,128]{1,0:T(8,128)(2,1)S(1)} %get-tuple-element.31), channel_id=1, source_target_pairs={{0,8},{8,0},{16,24},{24,16},{1,9},{9,1},{17,25},{25,17},{2,10},{10... | collective-permute-start | bytes 479240 | tf_op jit(solution)/shard_map/ppermute | solution.py:521
  5.0 13.4 %collective-permute-start.1 = (bf16[624,128]{1,0:T(8,128)(2,1)S(1)}, bf16[624,128]{1,0:T(8,128)(2,1)S(1)}, u32[]{:S(2)}, u32[]{:S(2)}) collective-permute-start(bf16[624,128]{1,0:T(8,128)(2,1)S(1)} %get-tuple-element.32), channel_id=1, source_target_pairs={{0,16},{8,24},{16,0},{24,8},{1,17},{9,25},{17,1},{25,9},{2,18},{10... | collective-permute-start | bytes 479240 | tf_op jit(solution)/shard_map/ppermute | solution.py:521
  6.5 11.9 %collective-permute-start.2 = (bf16[624,128]{1,0:T(8,128)(2,1)S(1)}, bf16[624,128]{1,0:T(8,128)(2,1)S(1)}, u32[]{:S(2)}, u32[]{:S(2)}) collective-permute-start(bf16[624,128]{1,0:T(8,128)(2,1)S(1)} %get-tuple-element.33), channel_id=1, source_target_pairs={{0,24},{8,16},{16,8},{24,0},{1,25},{9,17},{17,9},{25,1},{2,26},{10... | collective-permute-start | bytes 479240 | tf_op jit(solution)/shard_map/ppermute | solution.py:521
  6.7 12.2 %collective-permute-start.7 = (bf16[624,128]{1,0:T(8,128)(2,1)S(1)}, bf16[624,128]{1,0:T(8,128)(2,1)S(1)}, u32[]{:S(2)}, u32[]{:S(2)}) collective-permute-start(bf16[624,128]{1,0:T(8,128)(2,1)S(1)} %get-tuple-element.35), channel_id=1, source_target_pairs={{0,8},{8,0},{16,24},{24,16},{1,9},{9,1},{17,25},{25,17},{2,10},{10... | collective-permute-start | bytes 479240 | tf_op jit(solution)/shard_map/ppermute | solution.py:521
  10.2 18.7 %all-to-all-start.1 = ((f32[32,8,128]{2,1,0:T(8,128)}), f32[32,8,128]{2,1,0:T(8,128)S(1)}, u32[]{:S(2)}, u32[]{:S(2)}) async-start(f32[32,8,128]{2,1,0:T(8,128)} %get-tuple-element.39), calls=%async_computation.1 | async-start | bytes 262144 | tf_op jit(solution)/shard_map/all_to_all | solution.py:565
  15.1 11.2 %collective-permute-start.8 = (bf16[624,128]{1,0:T(8,128)(2,1)S(1)}, bf16[624,128]{1,0:T(8,128)(2,1)S(1)}, u32[]{:S(2)}, u32[]{:S(2)}) collective-permute-start(bf16[624,128]{1,0:T(8,128)(2,1)S(1)} %get-tuple-element.36), channel_id=1, source_target_pairs={{0,16},{8,24},{16,0},{24,8},{1,17},{9,25},{17,1},{25,9},{2,18},{10... | collective-permute-start | bytes 479240 | tf_op jit(solution)/shard_map/ppermute | solution.py:521
  16.9 9.3 %collective-permute-start.9 = (bf16[624,128]{1,0:T(8,128)(2,1)S(1)}, bf16[624,128]{1,0:T(8,128)(2,1)S(1)}, u32[]{:S(2)}, u32[]{:S(2)}) collective-permute-start(bf16[624,128]{1,0:T(8,128)(2,1)S(1)} %get-tuple-element.37), channel_id=1, source_target_pairs={{0,24},{8,16},{16,8},{24,0},{1,25},{9,17},{17,9},{25,1},{2,26},{10... | collective-permute-start | bytes 479240 | tf_op jit(solution)/shard_map/ppermute | solution.py:521
  18.4 7.9 %collective-permute-start.4 = (bf16[624,128]{1,0:T(8,128)(2,1)S(1)}, bf16[624,128]{1,0:T(8,128)(2,1)S(1)}, u32[]{:S(2)}, u32[]{:S(2)}) collective-permute-start(bf16[624,128]{1,0:T(8,128)(2,1)S(1)} %collective-permute-done.refs_1_), channel_id=1, source_target_pairs={{0,4},{4,0},{1,5},{5,1},{2,6},{6,2},{3,7},{7,3},{8,12},{12,8},{9,1... | collective-permute-start | bytes 479240 | tf_op jit(solution)/shard_map/ppermute | solution.py:521
  18.4 7.9 %collective-permute-start.5 = (bf16[624,128]{1,0:T(8,128)(2,1)S(1)}, bf16[624,128]{1,0:T(8,128)(2,1)S(1)}, u32[]{:S(2)}, u32[]{:S(2)}) collective-permute-start(bf16[624,128]{1,0:T(8,128)(2,1)S(1)} %collective-permute-done.1.refs_2_), channel_id=1, source_target_pairs={{0,4},{4,0},{1,5},{5,1},{2,6},{6,2},{3,7},{7,3},{8,12},{12,8},{9,1... | collective-permute-start | bytes 479240 | tf_op jit(solution)/shard_map/ppermute | solution.py:521
  18.9 7.4 %collective-permute-start.6 = (bf16[624,128]{1,0:T(8,128)(2,1)S(1)}, bf16[624,128]{1,0:T(8,128)(2,1)S(1)}, u32[]{:S(2)}, u32[]{:S(2)}) collective-permute-start(bf16[624,128]{1,0:T(8,128)(2,1)S(1)} %collective-permute-done.2.refs_3_), channel_id=1, source_target_pairs={{0,4},{4,0},{1,5},{5,1},{2,6},{6,2},{3,7},{7,3},{8,12},{12,8},{9,1... | collective-permute-start | bytes 479240 | tf_op jit(solution)/shard_map/ppermute | solution.py:521
  28.9 13.2 %copy-start = (bf16[2,2,384,384]{3,2,1,0:T(8,128)(2,1)S(1)}, bf16[2,2,384,384]{3,2,1,0:T(8,128)(2,1)}, u32[]{:S(2)}) copy-start(bf16[2,2,384,384]{3,2,1,0:T(8,128)(2,1)} %ret_ref.1) | copy-start | bytes 3538948
  28.9 13.2 %copy-start.5 = (s32[17,128]{1,0:T(8,128)S(1)}, s32[17,128]{1,0:T(8,128)}, u32[]{:S(2)}) copy-start(s32[17,128]{1,0:T(8,128)} %near_ref.1) | copy-start | bytes 26116
  28.9 13.2 %all-to-all-start = ((f32[32,8,128]{2,1,0:T(8,128)}), f32[32,8,128]{2,1,0:T(8,128)S(1)}, u32[]{:S(2)}, u32[]{:S(2)}) async-start(f32[32,8,128]{2,1,0:T(8,128)} %shard_map.107), calls=%async_computation | async-start | bytes 262144 | tf_op jit(solution)/shard_map/all_to_all | solution.py:572
  36.5 11.6 %collective-permute-start.10 = (bf16[624,128]{1,0:T(8,128)(2,1)S(1)}, bf16[624,128]{1,0:T(8,128)(2,1)S(1)}, u32[]{:S(2)}, u32[]{:S(2)}) collective-permute-start(bf16[624,128]{1,0:T(8,128)(2,1)S(1)} %get-tuple-element.42), channel_id=1, source_target_pairs={{0,8},{8,0},{16,24},{24,16},{1,9},{9,1},{17,25},{25,17},{2,10},{10... | collective-permute-start | bytes 479240 | tf_op jit(solution)/shard_map/ppermute | solution.py:521
  38.3 9.8 %collective-permute-start.11 = (bf16[624,128]{1,0:T(8,128)(2,1)S(1)}, bf16[624,128]{1,0:T(8,128)(2,1)S(1)}, u32[]{:S(2)}, u32[]{:S(2)}) collective-permute-start(bf16[624,128]{1,0:T(8,128)(2,1)S(1)} %get-tuple-element.43), channel_id=1, source_target_pairs={{0,16},{8,24},{16,0},{24,8},{1,17},{9,25},{17,1},{25,9},{2,18},{10... | collective-permute-start | bytes 479240 | tf_op jit(solution)/shard_map/ppermute | solution.py:521
  39.8 8.3 %collective-permute-start.12 = (bf16[624,128]{1,0:T(8,128)(2,1)S(1)}, bf16[624,128]{1,0:T(8,128)(2,1)S(1)}, u32[]{:S(2)}, u32[]{:S(2)}) collective-permute-start(bf16[624,128]{1,0:T(8,128)(2,1)S(1)} %get-tuple-element.44), channel_id=1, source_target_pairs={{0,24},{8,16},{16,8},{24,0},{1,25},{9,17},{17,9},{25,1},{2,26},{10... | collective-permute-start | bytes 479240 | tf_op jit(solution)/shard_map/ppermute | solution.py:521

commit v4 on v3

--- a/solution.py
+++ b/solution.py
@@ -548,6 +548,7 @@
     high_blocks = deal(g_great)
     own, d_less, bond_dirs = lax.optimization_barrier((high_blocks[0], d_less, bond_dirs))
     high = to_chips(plan, [own] + list(high_blocks[1:]))
+    low[0], low[1] = lax.optimization_barrier((low[0], low[1]))
     low_beside = [swap(block, "momentum", 1) for block in low]
     small = jax.ShapeDtypeStruct((plan.devices, 8, LANES), F32)
     coupling, table, pairs = call(

time: 49.4 us -> 47.1 us (0.953)
  waiting for transfers between devices: 9.39 us -> 6.88 us
    ppermute x13, waiting for transfers between devices: 7.3 us -> 4.8 us  [swap(): lax.ppermute(block, axis, [(i, i ^ distance) for i in range(lax.axis_size...]
    ppermute x13, starting transfers between devices: 14.1 us -> 15.4 us  [swap(): lax.ppermute(block, axis, [(i, i ^ distance) for i in range(lax.axis_size...]
    all_to_all x1, starting transfers between devices: 4.92 us -> 3.97 us  [dealt(): coupling = lax.all_to_all(coupling, EVERY, 0, 0, tiled=True)]
  transfers between devices with their start and end apart: 15 -> 15, of which waited for: 2 -> 2; matrix products, arithmetic and copies ran while one was open for 0% -> 0% of each run, Pallas kernels for 26% -> 28%
where the time goes in v4:
time: 47.1 us; the launch traced here: 46.9 us
  starting transfers between devices  24 us (51%)
  Pallas kernels  14.1 us (30%)
  waiting for transfers between devices  6.88 us (15%)
  local copies, waits for them, and re-layouts  1.15 us (2%)
  between operations  0.75 us (2%)
    ppermute x13, starting transfers between devices, swap(): lax.ppermute(block, axis, [(i, i ^ distance) for i in range(lax.axis_size...  15.4 us
    pallas_call x7, Pallas kernels, call(): pl.pallas_call(kernel, out_shape=out_shape, in_specs=specs, out_specs=[vm...  14.1 us
    ppermute x13, waiting for transfers between devices, swap(): lax.ppermute(block, axis, [(i, i ^ distance) for i in range(lax.axis_size...  4.8 us
    all_to_all x1, starting transfers between devices, dealt(): polar = lax.all_to_all(polar, EVERY, 0, 0, tiled=True)  4.63 us
    all_to_all x1, starting transfers between devices, dealt(): coupling = lax.all_to_all(coupling, EVERY, 0, 0, tiled=True)  3.97 us
    all_to_all x1, waiting for transfers between devices, dealt(): polar = lax.all_to_all(polar, EVERY, 0, 0, tiled=True)  2.08 us
    unnamed x18, local copies, waits for them, and re-layouts  1.15 us
  transfers between devices with their start and end apart: 15, of which 2 were waited for; matrix products, arithmetic and copies ran while one was open for 0% of the time, Pallas kernels for 28%

profile of v4, /device:TPU:0, one launch (start us, length us, event | category | flops | bytes accessed | tf_op | source)
XLA Modules:
  0.0 46.9 jit_solution(7499787654944588360)
XLA Ops:
  0.6 0.0 copy-start.8
  0.6 0.0 copy-start.7
  0.7 0.0 copy-start.6
  0.7 0.0 copy-start.1
  0.7 1.1 %copy-done.1 = bf16[2,1,2,144,544]{4,3,2,1,0:T(8,128)(2,1)S(1)} copy-done((bf16[2,1,2,144,544]{4,3,2,1,0:T(8,128)(2,1)S(1)}, bf16[2,1,2,144,544]{4,3,2,1,0:T(8,128)(2,1)}, u32[]{:S(2)}) %copy-start.1) | copy-done | bytes 626712
  1.8 0.0 copy-start.2
  1.8 0.0 copy-start.3
  1.8 0.0 copy-start.4
  1.8 0.1 shard_map.104
  1.9 3.0 %collective-permute-start = (bf16[624,128]{1,0:T(8,128)(2,1)S(1)}, bf16[624,128]{1,0:T(8,128)(2,1)S(1)}, u32[]{:S(2)}, u32[]{:S(2)}) collective-permute-start(bf16[624,128]{1,0:T(8,128)(2,1)S(1)} %get-tuple-element.33), channel_id=1, source_target_pairs={{0,8},{8,0},{16,24},{24,16},{1,9},{9,1},{17,25},{25,17},{2,10},{10... | collective-permute-start | bytes 479240 | tf_op jit(solution)/shard_map/ppermute | solution.py:521
  4.9 1.5 %collective-permute-start.1 = (bf16[624,128]{1,0:T(8,128)(2,1)S(1)}, bf16[624,128]{1,0:T(8,128)(2,1)S(1)}, u32[]{:S(2)}, u32[]{:S(2)}) collective-permute-start(bf16[624,128]{1,0:T(8,128)(2,1)S(1)} %get-tuple-element.36), channel_id=1, source_target_pairs={{0,16},{8,24},{16,0},{24,8},{1,17},{9,25},{17,1},{25,9},{2,18},{10... | collective-permute-start | bytes 479240 | tf_op jit(solution)/shard_map/ppermute | solution.py:521
  6.5 0.0 collective-permute-start.2
  6.5 0.0 copy-done.2
  6.5 0.1 shard_map.105
  6.6 2.0 %collective-permute-start.7 = (bf16[624,128]{1,0:T(8,128)(2,1)S(1)}, bf16[624,128]{1,0:T(8,128)(2,1)S(1)}, u32[]{:S(2)}, u32[]{:S(2)}) collective-permute-start(bf16[624,128]{1,0:T(8,128)(2,1)S(1)} %get-tuple-element.39), channel_id=1, source_target_pairs={{0,8},{8,0},{16,24},{24,16},{1,9},{9,1},{17,25},{25,17},{2,10},{10... | collective-permute-start | bytes 479240 | tf_op jit(solution)/shard_map/ppermute | solution.py:521
  8.6 1.5 %collective-permute-start.8 = (bf16[624,128]{1,0:T(8,128)(2,1)S(1)}, bf16[624,128]{1,0:T(8,128)(2,1)S(1)}, u32[]{:S(2)}, u32[]{:S(2)}) collective-permute-start(bf16[624,128]{1,0:T(8,128)(2,1)S(1)} %get-tuple-element.40), channel_id=1, source_target_pairs={{0,16},{8,24},{16,0},{24,8},{1,17},{9,25},{17,1},{25,9},{2,18},{10... | collective-permute-start | bytes 479240 | tf_op jit(solution)/shard_map/ppermute | solution.py:521
  10.1 0.0 copy-done.8
  10.1 0.0 copy-done.7
  10.1 0.0 copy-done.6
  10.1 0.0 copy-done.3
  10.2 0.0 copy-done.4
  10.2 1.4 %shard_map.106 = (f32[32,8,128]{2,1,0:T(8,128)}, f32[64,256]{1,0:T(8,128)S(1)}, f32[6,17,128]{2,1,0:T(8,128)S(1)}) custom-call(f32[2,9,17,2,128]{4,3,2,1,0:T(2,128)S(1)} %bitcast.6, f32[17,3,128]{2,1,0:T(4,128)S(1)} %bitcast.7, s32[1,64]{1,0:T(1,128)S(1)} %bitcast.8, s32[1,64]{1,0:T(1,128)S(1)} %bitcast.9, f32[1,64]{1,0:T(1,128)S(1)} %bitcast.10), custom_call_target="tpu_custom_call" | custom-call | bytes 313344 | tf_op jit(solution)/shard_map/pallas_call | solution.py:207
  11.6 4.0 %all-to-all-start.1 = ((f32[32,8,128]{2,1,0:T(8,128)}), f32[32,8,128]{2,1,0:T(8,128)S(1)}, u32[]{:S(2)}, u32[]{:S(2)}) async-start(f32[32,8,128]{2,1,0:T(8,128)} %get-tuple-element.43), calls=%async_computation.1 | async-start | bytes 262144 | tf_op jit(solution)/shard_map/all_to_all | solution.py:566
  15.6 0.0 collective-permute-done.refs_1_
  15.6 2.7 %collective-permute-start.9 = (bf16[624,128]{1,0:T(8,128)(2,1)S(1)}, bf16[624,128]{1,0:T(8,128)(2,1)S(1)}, u32[]{:S(2)}, u32[]{:S(2)}) collective-permute-start(bf16[624,128]{1,0:T(8,128)(2,1)S(1)} %get-tuple-element.41), channel_id=1, source_target_pairs={{0,24},{8,16},{16,8},{24,0},{1,25},{9,17},{17,9},{25,1},{2,26},{10... | collective-permute-start | bytes 479240 | tf_op jit(solution)/shard_map/ppermute | solution.py:521
  18.3 0.0 collective-permute-done.1.refs_2_
  18.3 0.0 collective-permute-start.3
  18.3 0.0 collective-permute-done.2.refs_3_
  18.3 0.5 %collective-permute-start.4 = (bf16[624,128]{1,0:T(8,128)(2,1)S(1)}, bf16[624,128]{1,0:T(8,128)(2,1)S(1)}, u32[]{:S(2)}, u32[]{:S(2)}) collective-permute-start(bf16[624,128]{1,0:T(8,128)(2,1)S(1)} %collective-permute-done.refs_1_), channel_id=1, source_target_pairs={{0,4},{4,0},{1,5},{5,1},{2,6},{6,2},{3,7},{7,3},{8,12},{12,8},{9,1... | collective-permute-start | bytes 479240 | tf_op jit(solution)/shard_map/ppermute | solution.py:521
  18.8 0.0 collective-permute-done.7.refs_9_
  18.8 0.1 collective-permute-start.5
  18.9 0.0 collective-permute-done.8.refs_10_
  18.9 0.4 collective-permute-start.6
  19.4 4.8 %collective-permute-done.9.refs_11_ = bf16[624,128]{1,0:T(8,128)(2,1)S(1)} collective-permute-done((bf16[624,128]{1,0:T(8,128)(2,1)S(1)}, bf16[624,128]{1,0:T(8,128)(2,1)S(1)}, u32[]{:S(2)}, u32[]{:S(2)}) %collective-permute-start.9) | collective-permute-done | bytes 159776 | tf_op jit(solution)/shard_map/ppermute | solution.py:521
  24.1 0.0 collective-permute-done.3.refs_4_
  24.1 0.0 collective-permute-done.4.refs_5_
  24.1 0.0 collective-permute-done.5.refs_6_
  24.1 0.0 collective-permute-done.6.refs_7_
  24.1 2.6 %shard_map.107 = f32[32,8,128]{2,1,0:T(8,128)} custom-call(s32[1]{0:T(128)} %bitcast.rank_ref, f32[64,256]{1,0:T(8,128)S(1)} %get-tuple-element.31.table_ref, bf16[624,128]{1,0:T(8,128)(2,1)S(1)} %get-tuple-element.34.refs_0_, bf16[624,128]{1,0:T(8,128)(2,1)S(1)} %collective-permute-done.refs_1_, bf16[624,128]{1,0:T(8,128)(2,1)S(1)} %collective-permute-done.1.refs_2_, ...), custom_call_target="tpu_custom_call" | custom-call | bytes 8388608 | tf_op jit(solution)/shard_map/pallas_call | solution.py:207
  26.7 0.0 copy-start
  26.7 0.0 copy-start.5
  26.7 0.0 all-to-all-done.1.coupling_ref
  26.7 4.6 %all-to-all-start = ((f32[32,8,128]{2,1,0:T(8,128)}), f32[32,8,128]{2,1,0:T(8,128)S(1)}, u32[]{:S(2)}, u32[]{:S(2)}) async-start(f32[32,8,128]{2,1,0:T(8,128)} %shard_map.107), calls=%async_computation | async-start | bytes 262144 | tf_op jit(solution)/shard_map/all_to_all | solution.py:573
  31.4 2.9 %shard_map.109 = (bf16[624,128]{1,0:T(8,128)(2,1)S(1)}, bf16[624,128]{1,0:T(8,128)(2,1)S(1)}, bf16[624,128]{1,0:T(8,128)(2,1)S(1)}, bf16[624,128]{1,0:T(8,128)(2,1)S(1)}) custom-call(s32[1]{0:T(128)} %bitcast.rank_ref, f32[64,256]{1,0:T(8,128)S(1)} %get-tuple-element.31.table_ref, f32[32,8,128]{2,1,0:T(8,128)S(1)} %all-to-all-done.1.coupling_ref, ...), custom_call_target="tpu_custom_call" | custom-call | bytes 8388608 | tf_op jit(solution)/shard_map/pallas_call | solution.py:207
  34.2 1.8 %collective-permute-start.10 = (bf16[624,128]{1,0:T(8,128)(2,1)S(1)}, bf16[624,128]{1,0:T(8,128)(2,1)S(1)}, u32[]{:S(2)}, u32[]{:S(2)}) collective-permute-start(bf16[624,128]{1,0:T(8,128)(2,1)S(1)} %get-tuple-element.46), channel_id=1, source_target_pairs={{0,8},{8,0},{16,24},{24,16},{1,9},{9,1},{17,25},{25,17},{2,10},{10... | collective-permute-start | bytes 479240 | tf_op jit(solution)/shard_map/ppermute | solution.py:521
  36.1 1.5 %collective-permute-start.11 = (bf16[624,128]{1,0:T(8,128)(2,1)S(1)}, bf16[624,128]{1,0:T(8,128)(2,1)S(1)}, u32[]{:S(2)}, u32[]{:S(2)}) collective-permute-start(bf16[624,128]{1,0:T(8,128)(2,1)S(1)} %get-tuple-element.47), channel_id=1, source_target_pairs={{0,16},{8,24},{16,0},{24,8},{1,17},{9,25},{17,1},{25,9},{2,18},{10... | collective-permute-start | bytes 479240 | tf_op jit(solution)/shard_map/ppermute | solution.py:521
  37.5 0.3 collective-permute-start.12
  37.8 2.1 %all-to-all-done.polar_ref = f32[32,8,128]{2,1,0:T(8,128)S(1)} async-done(((f32[32,8,128]{2,1,0:T(8,128)}), f32[32,8,128]{2,1,0:T(8,128)S(1)}, u32[]{:S(2)}, u32[]{:S(2)}) %all-to-all-start) | async-done | bytes 131104 | tf_op jit(solution)/shard_map/all_to_all | solution.py:573
  39.9 0.0 copy-done
  39.9 0.0 copy-done.5
  39.9 6.0 %shard_map.108 = bf16[2,2,384,384]{3,2,1,0:T(8,128)(2,1)} custom-call(f32[32,8,128]{2,1,0:T(8,128)S(1)} %all-to-all-done.polar_ref, bf16[2,2,384,384]{3,2,1,0:T(8,128)(2,1)S(1)} %copy-done, s32[17,128]{1,0:T(8,128)S(1)} %copy-done.5, f32[6,17,128]{2,1,0:T(8,128)S(1)} %get-tuple-element.42.pair_ref), custom_call_target="tpu_custom_call" | custom-call | bytes 20971520 | tf_op jit(solution)/shard_map/pallas_call | solution.py:207
  45.8 0.0 collective-permute-done.10.refs_1_
  45.8 0.0 collective-permute-done.11.refs_2_
  45.8 0.0 collective-permute-done.12.refs_3_
  45.8 1.0 %shard_map.110 = bf16[2,1,2,144,544]{4,3,2,1,0:T(8,128)(2,1)} custom-call(s32[1]{0:T(128)} %bitcast.rank_ref, bf16[624,128]{1,0:T(8,128)(2,1)S(1)} %get-tuple-element.45.refs_0_, bf16[624,128]{1,0:T(8,128)(2,1)S(1)} %collective-permute-done.10.refs_1_, bf16[624,128]{1,0:T(8,128)(2,1)S(1)} %collective-permute-done.11.refs_2_, ...), custom_call_target="tpu_custom_call" | custom-call | bytes 4194304 | tf_op jit(solution)/shard_map/pallas_call | solution.py:207
Async XLA Ops:
  0.6 9.5 %copy-start.8 = (f32[64]{0:T(128)S(1)}, f32[64]{0:T(128)}, u32[]{:S(2)}) copy-start(f32[64]{0:T(128)} %param.17) | copy-start | bytes 772
  0.6 9.5 %copy-start.7 = (s32[64]{0:T(128)S(1)}, s32[64]{0:T(128)}, u32[]{:S(2)}) copy-start(s32[64]{0:T(128)} %param.16) | copy-start | bytes 772
  0.7 9.5 %copy-start.6 = (s32[64]{0:T(128)S(1)}, s32[64]{0:T(128)}, u32[]{:S(2)}) copy-start(s32[64]{0:T(128)} %param.15) | copy-start | bytes 772
  0.7 1.1 %copy-start.1 = (bf16[2,1,2,144,544]{4,3,2,1,0:T(8,128)(2,1)S(1)}, bf16[2,1,2,144,544]{4,3,2,1,0:T(8,128)(2,1)}, u32[]{:S(2)}) copy-start(bf16[2,1,2,144,544]{4,3,2,1,0:T(8,128)(2,1)} %source_ref.1) | copy-start | bytes 1880068
  1.8 4.7 %copy-start.2 = (bf16[2,1,2,144,544]{4,3,2,1,0:T(8,128)(2,1)S(1)}, bf16[2,1,2,144,544]{4,3,2,1,0:T(8,128)(2,1)}, u32[]{:S(2)}) copy-start(bf16[2,1,2,144,544]{4,3,2,1,0:T(8,128)(2,1)} %source_ref.2) | copy-start | bytes 1880068
  1.8 8.4 %copy-start.3 = (f32[2,2,9,17,128]{4,1,3,2,0:T(2,128)S(1)}, f32[2,2,9,17,128]{4,1,3,2,0:T(2,128)}, u32[]{:S(2)}) copy-start(f32[2,2,9,17,128]{4,1,3,2,0:T(2,128)} %param.11) | copy-start | bytes 940036
  1.8 8.4 %copy-start.4 = (f32[3,17,128]{2,0,1:T(4,128)S(1)}, f32[3,17,128]{2,0,1:T(4,128)}, u32[]{:S(2)}) copy-start(f32[3,17,128]{2,0,1:T(4,128)} %param.14) | copy-start | bytes 78340
  1.9 13.7 %collective-permute-start = (bf16[624,128]{1,0:T(8,128)(2,1)S(1)}, bf16[624,128]{1,0:T(8,128)(2,1)S(1)}, u32[]{:S(2)}, u32[]{:S(2)}) collective-permute-start(bf16[624,128]{1,0:T(8,128)(2,1)S(1)} %get-tuple-element.33), channel_id=1, source_target_pairs={{0,8},{8,0},{16,24},{24,16},{1,9},{9,1},{17,25},{25,17},{2,10},{10... | collective-permute-start | bytes 479240 | tf_op jit(solution)/shard_map/ppermute | solution.py:521
  4.9 13.4 %collective-permute-start.1 = (bf16[624,128]{1,0:T(8,128)(2,1)S(1)}, bf16[624,128]{1,0:T(8,128)(2,1)S(1)}, u32[]{:S(2)}, u32[]{:S(2)}) collective-permute-start(bf16[624,128]{1,0:T(8,128)(2,1)S(1)} %get-tuple-element.36), channel_id=1, source_target_pairs={{0,16},{8,24},{16,0},{24,8},{1,17},{9,25},{17,1},{25,9},{2,18},{10... | collective-permute-start | bytes 479240 | tf_op jit(solution)/shard_map/ppermute | solution.py:521
  6.5 11.9 %collective-permute-start.2 = (bf16[624,128]{1,0:T(8,128)(2,1)S(1)}, bf16[624,128]{1,0:T(8,128)(2,1)S(1)}, u32[]{:S(2)}, u32[]{:S(2)}) collective-permute-start(bf16[624,128]{1,0:T(8,128)(2,1)S(1)} %get-tuple-element.37), channel_id=1, source_target_pairs={{0,24},{8,16},{16,8},{24,0},{1,25},{9,17},{17,9},{25,1},{2,26},{10... | collective-permute-start | bytes 479240 | tf_op jit(solution)/shard_map/ppermute | solution.py:521
  6.6 12.2 %collective-permute-start.7 = (bf16[624,128]{1,0:T(8,128)(2,1)S(1)}, bf16[624,128]{1,0:T(8,128)(2,1)S(1)}, u32[]{:S(2)}, u32[]{:S(2)}) collective-permute-start(bf16[624,128]{1,0:T(8,128)(2,1)S(1)} %get-tuple-element.39), channel_id=1, source_target_pairs={{0,8},{8,0},{16,24},{24,16},{1,9},{9,1},{17,25},{25,17},{2,10},{10... | collective-permute-start | bytes 479240 | tf_op jit(solution)/shard_map/ppermute | solution.py:521
  8.6 10.3 %collective-permute-start.8 = (bf16[624,128]{1,0:T(8,128)(2,1)S(1)}, bf16[624,128]{1,0:T(8,128)(2,1)S(1)}, u32[]{:S(2)}, u32[]{:S(2)}) collective-permute-start(bf16[624,128]{1,0:T(8,128)(2,1)S(1)} %get-tuple-element.40), channel_id=1, source_target_pairs={{0,16},{8,24},{16,0},{24,8},{1,17},{9,25},{17,1},{25,9},{2,18},{10... | collective-permute-start | bytes 479240 | tf_op jit(solution)/shard_map/ppermute | solution.py:521
  11.6 15.1 %all-to-all-start.1 = ((f32[32,8,128]{2,1,0:T(8,128)}), f32[32,8,128]{2,1,0:T(8,128)S(1)}, u32[]{:S(2)}, u32[]{:S(2)}) async-start(f32[32,8,128]{2,1,0:T(8,128)} %get-tuple-element.43), calls=%async_computation.1 | async-start | bytes 262144 | tf_op jit(solution)/shard_map/all_to_all | solution.py:566
  15.6 8.5 %collective-permute-start.9 = (bf16[624,128]{1,0:T(8,128)(2,1)S(1)}, bf16[624,128]{1,0:T(8,128)(2,1)S(1)}, u32[]{:S(2)}, u32[]{:S(2)}) collective-permute-start(bf16[624,128]{1,0:T(8,128)(2,1)S(1)} %get-tuple-element.41), channel_id=1, source_target_pairs={{0,24},{8,16},{16,8},{24,0},{1,25},{9,17},{17,9},{25,1},{2,26},{10... | collective-permute-start | bytes 479240 | tf_op jit(solution)/shard_map/ppermute | solution.py:521
  18.3 5.8 %collective-permute-start.3 = (bf16[624,128]{1,0:T(8,128)(2,1)S(1)}, bf16[624,128]{1,0:T(8,128)(2,1)S(1)}, u32[]{:S(2)}, u32[]{:S(2)}) collective-permute-start(bf16[624,128]{1,0:T(8,128)(2,1)S(1)} %get-tuple-element.34.refs_0_), channel_id=1, source_target_pairs={{0,4},{4,0},{1,5},{5,1},{2,6},{6,2},{3,7},{7,3},{8,12},{12,8},{9,1... | collective-permute-start | bytes 479240 | tf_op jit(solution)/shard_map/ppermute | solution.py:521
  18.3 5.8 %collective-permute-start.4 = (bf16[624,128]{1,0:T(8,128)(2,1)S(1)}, bf16[624,128]{1,0:T(8,128)(2,1)S(1)}, u32[]{:S(2)}, u32[]{:S(2)}) collective-permute-start(bf16[624,128]{1,0:T(8,128)(2,1)S(1)} %collective-permute-done.refs_1_), channel_id=1, source_target_pairs={{0,4},{4,0},{1,5},{5,1},{2,6},{6,2},{3,7},{7,3},{8,12},{12,8},{9,1... | collective-permute-start | bytes 479240 | tf_op jit(solution)/shard_map/ppermute | solution.py:521
  18.8 5.3 %collective-permute-start.5 = (bf16[624,128]{1,0:T(8,128)(2,1)S(1)}, bf16[624,128]{1,0:T(8,128)(2,1)S(1)}, u32[]{:S(2)}, u32[]{:S(2)}) collective-permute-start(bf16[624,128]{1,0:T(8,128)(2,1)S(1)} %collective-permute-done.1.refs_2_), channel_id=1, source_target_pairs={{0,4},{4,0},{1,5},{5,1},{2,6},{6,2},{3,7},{7,3},{8,12},{12,8},{9,1... | collective-permute-start | bytes 479240 | tf_op jit(solution)/shard_map/ppermute | solution.py:521
  18.9 5.2 %collective-permute-start.6 = (bf16[624,128]{1,0:T(8,128)(2,1)S(1)}, bf16[624,128]{1,0:T(8,128)(2,1)S(1)}, u32[]{:S(2)}, u32[]{:S(2)}) collective-permute-start(bf16[624,128]{1,0:T(8,128)(2,1)S(1)} %collective-permute-done.2.refs_3_), channel_id=1, source_target_pairs={{0,4},{4,0},{1,5},{5,1},{2,6},{6,2},{3,7},{7,3},{8,12},{12,8},{9,1... | collective-permute-start | bytes 479240 | tf_op jit(solution)/shard_map/ppermute | solution.py:521
  26.7 13.2 %copy-start = (bf16[2,2,384,384]{3,2,1,0:T(8,128)(2,1)S(1)}, bf16[2,2,384,384]{3,2,1,0:T(8,128)(2,1)}, u32[]{:S(2)}) copy-start(bf16[2,2,384,384]{3,2,1,0:T(8,128)(2,1)} %ret_ref.1) | copy-start | bytes 3538948
  26.7 13.2 %copy-start.5 = (s32[17,128]{1,0:T(8,128)S(1)}, s32[17,128]{1,0:T(8,128)}, u32[]{:S(2)}) copy-start(s32[17,128]{1,0:T(8,128)} %near_ref.1) | copy-start | bytes 26116
  26.7 13.1 %all-to-all-start = ((f32[32,8,128]{2,1,0:T(8,128)}), f32[32,8,128]{2,1,0:T(8,128)S(1)}, u32[]{:S(2)}, u32[]{:S(2)}) async-start(f32[32,8,128]{2,1,0:T(8,128)} %shard_map.107), calls=%async_computation | async-start | bytes 262144 | tf_op jit(solution)/shard_map/all_to_all | solution.py:573
  34.2 11.6 %collective-permute-start.10 = (bf16[624,128]{1,0:T(8,128)(2,1)S(1)}, bf16[624,128]{1,0:T(8,128)(2,1)S(1)}, u32[]{:S(2)}, u32[]{:S(2)}) collective-permute-start(bf16[624,128]{1,0:T(8,128)(2,1)S(1)} %get-tuple-element.46), channel_id=1, source_target_pairs={{0,8},{8,0},{16,24},{24,16},{1,9},{9,1},{17,25},{25,17},{2,10},{10... | collective-permute-start | bytes 479240 | tf_op jit(solution)/shard_map/ppermute | solution.py:521
  36.1 9.8 %collective-permute-start.11 = (bf16[624,128]{1,0:T(8,128)(2,1)S(1)}, bf16[624,128]{1,0:T(8,128)(2,1)S(1)}, u32[]{:S(2)}, u32[]{:S(2)}) collective-permute-start(bf16[624,128]{1,0:T(8,128)(2,1)S(1)} %get-tuple-element.47), channel_id=1, source_target_pairs={{0,16},{8,24},{16,0},{24,8},{1,17},{9,25},{17,1},{25,9},{2,18},{10... | collective-permute-start | bytes 479240 | tf_op jit(solution)/shard_map/ppermute | solution.py:521
  37.5 8.3 %collective-permute-start.12 = (bf16[624,128]{1,0:T(8,128)(2,1)S(1)}, bf16[624,128]{1,0:T(8,128)(2,1)S(1)}, u32[]{:S(2)}, u32[]{:S(2)}) collective-permute-start(bf16[624,128]{1,0:T(8,128)(2,1)S(1)} %get-tuple-element.48), channel_id=1, source_target_pairs={{0,24},{8,16},{16,8},{24,0},{1,25},{9,17},{17,9},{25,1},{2,26},{10... | collective-permute-start | bytes 479240 | tf_op jit(solution)/shard_map/ppermute | solution.py:521

commit v5 on v4

--- a/solution.py
+++ b/solution.py
@@ -199,7 +199,7 @@
         )
 
 
-def call(kernel, out_shape, *operands, scratch=(), scalars=0, flops=0, moved=0):
+def call(kernel, out_shape, *operands, scratch=(), scalars=0, flops=0, moved=0, out_space=pltpu.VMEM):
     smem = pl.BlockSpec(memory_space=pltpu.SMEM)
     vmem = pl.BlockSpec(memory_space=pltpu.VMEM)
     specs = [smem] * scalars + [vmem] * (len(operands) - scalars)
@@ -208,7 +208,7 @@
         kernel,
         out_shape=out_shape,
         in_specs=specs,
-        out_specs=[vmem] * len(out_shape) if many else vmem,
+        out_specs=[vmem] * len(out_shape) if many else pl.BlockSpec(memory_space=out_space),
         scratch_shapes=list(scratch),
         compiler_params=pltpu.CompilerParams(vmem_limit_bytes=48 * 2**20),
         cost_estimate=pl.CostEstimate(flops=flops, bytes_accessed=moved, transcendentals=0),
@@ -273,7 +273,8 @@
 
 
 def couple_kernel(
-    plan, less_ref, dirs_ref, energy_ref, momentum_ref, absorb_ref, out_ref, table_ref, pair_ref, held_ref
+    plan, less_ref, dirs_ref, energy_ref, momentum_ref, absorb_ref,
+    out_ref, table_ref, pair_ref, held_ref,
 ):
     bonds, width = plan.bonds, plan.width
     held_ref[...] = jnp.zeros(held_ref.shape, F32)
@@ -352,8 +353,8 @@
         return tuple(sums)
 
     none = tuple(jnp.zeros((8, LANES), F32) for _ in range(2 * plan.classes))
-    main = lax.fori_loop(0, plan.entries // 8, step, none)
-    rest = lax.fori_loop(plan.entries // 8, plan.held // 8, step, none)
+    main = lax.fori_loop(0, plan.entries // 8, step, none, unroll=3)
+    rest = lax.fori_loop(plan.entries // 8, plan.held // 8, step, none, unroll=5)
     scale = float(count * 2 * plan.entries) ** (-0.5)
     lines = [jnp.sum(part, axis=0, keepdims=True) * scale for part in main + rest]
     sums = jnp.concatenate(lines, axis=0)
@@ -405,8 +406,8 @@
 
         return step
 
-    lax.fori_loop(0, plan.entries // 8, run(0), 0)
-    lax.fori_loop(plan.entries // 8, plan.held // 8, run(4 * plan.classes), 0)
+    lax.fori_loop(0, plan.entries // 8, run(0), 0, unroll=2)
+    lax.fori_loop(plan.entries // 8, plan.held // 8, run(4 * plan.classes), 0, unroll=5)
     lane = lax.broadcasted_iota(jnp.int32, (plan.rest_pad, LANES), 1)
     for partner in range(chips):
         first = plan.energies * (rank ^ partner)
@@ -428,24 +429,31 @@
 
 def gather_kernel(plan, rank_ref, *refs):
     chips = plan.n_energy
-    out_ref, rest_ref = refs[chips:]
+    out_ref, rest_ref, held_ref, sems = refs[chips:]
     rank = rank_ref[0]
-    for partner, message in enumerate(refs[:chips]):
-        source = rank ^ partner
-        lanes = pl.ds(pl.multiple_of(source * LANES, LANES), LANES)
-        tail = message[plan.main_rows :].astype(F32)[: plan.rest_pad]
-        for slab in range(plan.slabs):
+    copies = []
+    for slab in range(plan.slabs):
+        place = (slab // 2, 0, slab % 2)
+        for partner, message in enumerate(refs[:chips]):
+            source = rank ^ partner
+            lanes = pl.ds(pl.multiple_of(source * LANES, LANES), LANES)
+            tail = message[plan.main_rows :].astype(F32)[: plan.rest_pad]
             rows = slice(slab * plan.entries, (slab + 1) * plan.entries)
-            out_ref[slab // 2, 0, slab % 2, :, lanes] = message[rows]
+            held_ref[slab // 2, 0, slab % 2, :, lanes] = message[rows]
             turned = tail if slab == 0 else pltpu.roll(tail, LANES - slab * plan.rest, 1)
             rest_ref[slab, source] = turned
-    for slab in range(plan.slabs):
         parts = [rest_ref[slab, source, : plan.rest_rows] for source in range(chips)]
         rest = jnp.concatenate(parts, axis=0)[:, : plan.rest]
-        out_ref[slab // 2, 0, slab % 2, :, plan.tiles * LANES :] = rest.astype(BF16)
-
-
-def next_kernel(plan, polar_ref, ret_ref, near_ref, pair_ref, out_ref, v_ref, dense_ref):
+        held_ref[slab // 2, 0, slab % 2, :, plan.tiles * LANES :] = rest.astype(BF16)
+        copies.append(pltpu.make_async_copy(held_ref.at[place], out_ref.at[place], sems.at[slab]))
+        copies[-1].start()
+    for copy in copies:
+        copy.wait()
+
+
+def next_kernel(
+    plan, polar_ref, ret_ref, near_ref, pair_ref, out_ref, v_ref, dense_ref, after_ref, sems
+):
     bonds, atoms, order = plan.bonds, plan.atoms, plan.order
     padded = -(-bonds // 8) * 8
     lines = []
@@ -473,48 +481,56 @@
     )
     by_bond = both[: tall.shape[0]] + both[tall.shape[0] :]
     ways = [(i, j) for i in range(3) for j in range(i, 3)]
-    for way in range(len(ways)):
-        for row in range(2 * plan.modes):
-            values = by_bond[row * padded : row * padded + bonds]
-            v_ref[row * len(ways) + way, :bonds] = values * pair_ref[way]
-
-    def step(chunk, carry):
-        first = pl.multiple_of(chunk * 16, 16)
-        number = lax.broadcasted_iota(jnp.int32, (16, atoms), 0) + first
-        for row in range(2 * plan.modes):
-            sums = [jnp.zeros((16, atoms), F32) for _ in ways]
+    near = near_ref[...]
+    for row in range(2 * plan.modes):
+        values = by_bond[row * padded : row * padded + bonds]
+        values = [values * pair_ref[way] for way in range(len(ways))]
+        sums = [jnp.zeros((bonds, atoms), F32) for _ in ways]
+        for n in range(bonds):
+            same = near == near[n : n + 1]
+            for way in range(len(ways)):
+                sums[way] = sums[way] + jnp.where(same, values[way][n : n + 1], 0.0)
+        for way in range(len(ways)):
+            v_ref[row * len(ways) + way, :bonds] = sums[way]
+
+    near = near.astype(BF16)
+
+    def build(m, first):
+        number = (lax.broadcasted_iota(jnp.int32, (16, atoms), 0) + first).astype(BF16)
+        for z in range(2):
+            row = 2 * m + z
+            blocks = [jnp.zeros((16, atoms), BF16) for _ in ways]
             for n in range(bonds):
-                hit = number == near_ref[n : n + 1]
+                hit = number == near[n : n + 1]
                 for way in range(len(ways)):
-                    value = v_ref[row * len(ways) + way, n : n + 1]
-                    sums[way] = sums[way] + jnp.where(hit, value, 0.0)
-            m, z = row // 2, row % 2
+                    value = v_ref[row * len(ways) + way, n : n + 1].astype(BF16)
+                    blocks[way] = jnp.where(hit, value, blocks[way])
             for way, (i, j) in enumerate(ways):
-                block = sums[way].astype(BF16)
-                other = block if z else (-sums[way]).astype(BF16)
-                for up, left in {(j, i), (i, j)}:
-                    place = pl.multiple_of(up * atoms + first, 16)
-                    columns = left * atoms
-                    dense_ref[m, pl.ds(place, 16), pl.ds(z * order + columns, atoms)] = block
-                    place = pl.multiple_of(order + up * atoms + first, 16)
-                    dense_ref[m, pl.ds(place, 16), pl.ds((1 - z) * order + columns, atoms)] = other
-        return carry
-
-    lax.fori_loop(0, atoms // 16, step, 0)
+                block = blocks[way]
+                other = block if z else -block
+                for up, left in sorted({(j, i), (i, j)}):
+                    place = pl.ds(pl.multiple_of(up * atoms + first, 16), 16)
+                    dense_ref[m, place, pl.ds(z * order + left * atoms, atoms)] = block
+                    place = pl.ds(pl.multiple_of(order + up * atoms + first, 16), 16)
+                    dense_ref[m, place, pl.ds((1 - z) * order + left * atoms, atoms)] = other
+
+    for m in range(plan.modes):
+        for chunk in range(atoms // 16):
+            build(m, chunk * 16)
+    copies = []
     for m in range(plan.modes):
         ret = jnp.concatenate([ret_ref[m, 0], ret_ref[m, 1]], axis=1)
         half = jnp.dot(ret, dense_ref[m], preferred_element_type=F32).astype(BF16)
         half_re, half_im = half[:, :order], half[:, order:]
-        right = jnp.concatenate(
-            [
-                jnp.concatenate([half_re, -half_im], axis=1),
-                jnp.concatenate([half_im, half_re], axis=1),
-            ],
-            axis=0,
-        )
-        after = lax.dot_general(ret, right, contract, preferred_element_type=F32)
-        out_ref[m, 0] = after[:, :order].astype(BF16)
-        out_ref[m, 1] = after[:, order:].astype(BF16)
+        for z, parts in enumerate(([half_re, -half_im], [half_im, half_re])):
+            right = jnp.concatenate(parts, axis=1)
+            after = lax.dot_general(ret, right, contract, preferred_element_type=F32)
+            after_ref[m, z] = after.astype(BF16)
+            copy = pltpu.make_async_copy(after_ref.at[m, z], out_ref.at[m, z], sems.at[m, z])
+            copy.start()
+            copies.append(copy)
+    for copy in copies:
+        copy.wait()
 
 
 def swap(block, axis, distance):
@@ -582,9 +598,12 @@
     d_next = call(
         functools.partial(next_kernel, plan), jax.ShapeDtypeStruct(d_ret.shape, BF16),
         polar, d_ret, neighbours, pairs,
+        out_space=pltpu.HBM,
         scratch=[
             pltpu.VMEM((12 * plan.modes, padded, plan.atoms), F32),
             pltpu.VMEM((plan.modes, 2 * plan.order, 2 * plan.order), BF16),
+            pltpu.VMEM(d_ret.shape, BF16),
+            pltpu.SemaphoreType.DMA((plan.modes, 2)),
         ],
         moved=20 * 2**20,
     )
@@ -592,8 +611,12 @@
     self_energy = call(
         functools.partial(gather_kernel, plan), jax.ShapeDtypeStruct(g_less.shape, BF16), rank,
         own, *sums[1:],
-        scalars=1, scratch=[pltpu.VMEM((plan.slabs, chips, plan.rest_pad, LANES), F32)],
-        moved=4 * 2**20,
+        scalars=1, out_space=pltpu.HBM, moved=4 * 2**20,
+        scratch=[
+            pltpu.VMEM((plan.slabs, chips, plan.rest_pad, LANES), F32),
+            pltpu.VMEM(g_less.shape, BF16),
+            pltpu.SemaphoreType.DMA((plan.slabs,)),
+        ],
     )
     return self_energy, d_next
 

time: 47.1 us -> 46.5 us (0.987)
  Pallas kernels: 14.1 us -> 12.7 us
  waiting for transfers between devices: 6.88 us -> 7.6 us
    pallas_call x7, Pallas kernels: 14.1 us -> 12.7 us  [call(): pl.pallas_call(kernel, out_shape=out_shape, in_specs=specs, out_specs=[vm...]
    ppermute x13, waiting for transfers between devices: 4.8 us -> 5.34 us  [swap(): lax.ppermute(block, axis, [(i, i ^ distance) for i in range(lax.axis_size...]
  transfers between devices with their start and end apart: 15 -> 15, of which waited for: 2 -> 3; matrix products, arithmetic and copies ran while one was open for 0% -> 0% of each run, Pallas kernels for 28% -> 25%
where the time goes in v5:
time: 46.5 us; the launch traced here: 46.2 us
  starting transfers between devices  24 us (52%)
  Pallas kernels  12.7 us (27%)
  waiting for transfers between devices  7.6 us (16%)
  local copies, waits for them, and re-layouts  1.15 us (2%)
  between operations  0.77 us (2%)
    ppermute x13, starting transfers between devices, swap(): lax.ppermute(block, axis, [(i, i ^ distance) for i in range(lax.axis_size...  15.4 us
    pallas_call x7, Pallas kernels, call(): pl.pallas_call(kernel, out_shape=out_shape, in_specs=specs, out_specs=[vm...  12.7 us
    ppermute x13, waiting for transfers between devices, swap(): lax.ppermute(block, axis, [(i, i ^ distance) for i in range(lax.axis_size...  5.34 us
    all_to_all x1, starting transfers between devices, dealt(): polar = lax.all_to_all(polar, EVERY, 0, 0, tiled=True)  4.63 us
    all_to_all x1, starting transfers between devices, dealt(): coupling = lax.all_to_all(coupling, EVERY, 0, 0, tiled=True)  3.97 us
    all_to_all x1, waiting for transfers between devices, dealt(): polar = lax.all_to_all(polar, EVERY, 0, 0, tiled=True)  2.26 us
    unnamed x18, local copies, waits for them, and re-layouts  1.15 us
  transfers between devices with their start and end apart: 15, of which 3 were waited for; matrix products, arithmetic and copies ran while one was open for 0% of the time, Pallas kernels for 25%

profile of v5, /device:TPU:0, one launch (start us, length us, event | category | flops | bytes accessed | tf_op | source)
XLA Modules:
  0.0 46.2 jit_solution(9217836893976189321)
XLA Ops:
  0.6 0.0 copy-start.8
  0.6 0.0 copy-start.7
  0.7 0.0 copy-start.6
  0.7 0.0 copy-start.1
  0.7 1.1 %copy-done.1 = bf16[2,1,2,144,544]{4,3,2,1,0:T(8,128)(2,1)S(1)} copy-done((bf16[2,1,2,144,544]{4,3,2,1,0:T(8,128)(2,1)S(1)}, bf16[2,1,2,144,544]{4,3,2,1,0:T(8,128)(2,1)}, u32[]{:S(2)}) %copy-start.1) | copy-done | bytes 626712
  1.8 0.0 copy-start.2
  1.8 0.0 copy-start.3
  1.8 0.0 copy-start.4
  1.8 0.1 shard_map.104
  1.9 3.0 %collective-permute-start = (bf16[624,128]{1,0:T(8,128)(2,1)S(1)}, bf16[624,128]{1,0:T(8,128)(2,1)S(1)}, u32[]{:S(2)}, u32[]{:S(2)}) collective-permute-start(bf16[624,128]{1,0:T(8,128)(2,1)S(1)} %get-tuple-element.33), channel_id=1, source_target_pairs={{0,8},{8,0},{16,24},{24,16},{1,9},{9,1},{17,25},{25,17},{2,10},{10... | collective-permute-start | bytes 479240 | tf_op jit(solution)/shard_map/ppermute | solution.py:537
  4.9 1.5 %collective-permute-start.1 = (bf16[624,128]{1,0:T(8,128)(2,1)S(1)}, bf16[624,128]{1,0:T(8,128)(2,1)S(1)}, u32[]{:S(2)}, u32[]{:S(2)}) collective-permute-start(bf16[624,128]{1,0:T(8,128)(2,1)S(1)} %get-tuple-element.36), channel_id=1, source_target_pairs={{0,16},{8,24},{16,0},{24,8},{1,17},{9,25},{17,1},{25,9},{2,18},{10... | collective-permute-start | bytes 479240 | tf_op jit(solution)/shard_map/ppermute | solution.py:537
  6.5 0.0 collective-permute-start.2
  6.5 0.0 copy-done.2
  6.5 0.1 shard_map.105
  6.6 2.0 %collective-permute-start.7 = (bf16[624,128]{1,0:T(8,128)(2,1)S(1)}, bf16[624,128]{1,0:T(8,128)(2,1)S(1)}, u32[]{:S(2)}, u32[]{:S(2)}) collective-permute-start(bf16[624,128]{1,0:T(8,128)(2,1)S(1)} %get-tuple-element.39), channel_id=1, source_target_pairs={{0,8},{8,0},{16,24},{24,16},{1,9},{9,1},{17,25},{25,17},{2,10},{10... | collective-permute-start | bytes 479240 | tf_op jit(solution)/shard_map/ppermute | solution.py:537
  8.6 1.5 %collective-permute-start.8 = (bf16[624,128]{1,0:T(8,128)(2,1)S(1)}, bf16[624,128]{1,0:T(8,128)(2,1)S(1)}, u32[]{:S(2)}, u32[]{:S(2)}) collective-permute-start(bf16[624,128]{1,0:T(8,128)(2,1)S(1)} %get-tuple-element.40), channel_id=1, source_target_pairs={{0,16},{8,24},{16,0},{24,8},{1,17},{9,25},{17,1},{25,9},{2,18},{10... | collective-permute-start | bytes 479240 | tf_op jit(solution)/shard_map/ppermute | solution.py:537
  10.1 0.0 copy-done.8
  10.1 0.0 copy-done.7
  10.1 0.0 copy-done.6
  10.1 0.0 copy-done.3
  10.2 0.0 copy-done.4
  10.2 1.4 %shard_map.106 = (f32[32,8,128]{2,1,0:T(8,128)}, f32[64,256]{1,0:T(8,128)S(1)}, f32[6,17,128]{2,1,0:T(8,128)S(1)}) custom-call(f32[2,9,17,2,128]{4,3,2,1,0:T(2,128)S(1)} %bitcast.6, f32[17,3,128]{2,1,0:T(4,128)S(1)} %bitcast.7, s32[1,64]{1,0:T(1,128)S(1)} %bitcast.8, s32[1,64]{1,0:T(1,128)S(1)} %bitcast.9, f32[1,64]{1,0:T(1,128)S(1)} %bitcast.10), custom_call_target="tpu_custom_call" | custom-call | bytes 313344 | tf_op jit(solution)/shard_map/pallas_call | solution.py:207
  11.6 4.0 %all-to-all-start.1 = ((f32[32,8,128]{2,1,0:T(8,128)}), f32[32,8,128]{2,1,0:T(8,128)S(1)}, u32[]{:S(2)}, u32[]{:S(2)}) async-start(f32[32,8,128]{2,1,0:T(8,128)} %get-tuple-element.43), calls=%async_computation.1 | async-start | bytes 262144 | tf_op jit(solution)/shard_map/all_to_all | solution.py:582
  15.6 0.0 collective-permute-done.refs_1_
  15.6 2.7 %collective-permute-start.9 = (bf16[624,128]{1,0:T(8,128)(2,1)S(1)}, bf16[624,128]{1,0:T(8,128)(2,1)S(1)}, u32[]{:S(2)}, u32[]{:S(2)}) collective-permute-start(bf16[624,128]{1,0:T(8,128)(2,1)S(1)} %get-tuple-element.41), channel_id=1, source_target_pairs={{0,24},{8,16},{16,8},{24,0},{1,25},{9,17},{17,9},{25,1},{2,26},{10... | collective-permute-start | bytes 479240 | tf_op jit(solution)/shard_map/ppermute | solution.py:537
  18.3 0.0 collective-permute-done.1.refs_2_
  18.3 0.0 collective-permute-start.3
  18.3 0.0 collective-permute-done.2.refs_3_
  18.3 0.5 %collective-permute-start.4 = (bf16[624,128]{1,0:T(8,128)(2,1)S(1)}, bf16[624,128]{1,0:T(8,128)(2,1)S(1)}, u32[]{:S(2)}, u32[]{:S(2)}) collective-permute-start(bf16[624,128]{1,0:T(8,128)(2,1)S(1)} %collective-permute-done.refs_1_), channel_id=1, source_target_pairs={{0,4},{4,0},{1,5},{5,1},{2,6},{6,2},{3,7},{7,3},{8,12},{12,8},{9,1... | collective-permute-start | bytes 479240 | tf_op jit(solution)/shard_map/ppermute | solution.py:537
  18.8 0.0 collective-permute-done.7.refs_9_
  18.8 0.1 collective-permute-start.5
  18.9 0.0 collective-permute-done.8.refs_10_
  18.9 0.4 collective-permute-start.6
  19.4 4.8 %collective-permute-done.9.refs_11_ = bf16[624,128]{1,0:T(8,128)(2,1)S(1)} collective-permute-done((bf16[624,128]{1,0:T(8,128)(2,1)S(1)}, bf16[624,128]{1,0:T(8,128)(2,1)S(1)}, u32[]{:S(2)}, u32[]{:S(2)}) %collective-permute-start.9) | collective-permute-done | bytes 159776 | tf_op jit(solution)/shard_map/ppermute | solution.py:537
  24.1 0.0 collective-permute-done.3.refs_4_
  24.1 0.0 collective-permute-done.4.refs_5_
  24.1 0.0 collective-permute-done.5.refs_6_
  24.1 0.0 collective-permute-done.6.refs_7_
  24.1 2.4 %shard_map.107 = f32[32,8,128]{2,1,0:T(8,128)} custom-call(s32[1]{0:T(128)} %bitcast.rank_ref, f32[64,256]{1,0:T(8,128)S(1)} %get-tuple-element.31.table_ref, bf16[624,128]{1,0:T(8,128)(2,1)S(1)} %get-tuple-element.34.refs_0_, bf16[624,128]{1,0:T(8,128)(2,1)S(1)} %collective-permute-done.refs_1_, bf16[624,128]{1,0:T(8,128)(2,1)S(1)} %collective-permute-done.1.refs_2_, ...), custom_call_target="tpu_custom_call" | custom-call | bytes 8388608 | tf_op jit(solution)/shard_map/pallas_call | solution.py:207
  26.6 0.0 copy-start
  26.6 0.0 copy-start.5
  26.6 0.0 all-to-all-done.1.coupling_ref
  26.6 4.6 %all-to-all-start = ((f32[32,8,128]{2,1,0:T(8,128)}), f32[32,8,128]{2,1,0:T(8,128)S(1)}, u32[]{:S(2)}, u32[]{:S(2)}) async-start(f32[32,8,128]{2,1,0:T(8,128)} %shard_map.107), calls=%async_computation | async-start | bytes 262144 | tf_op jit(solution)/shard_map/all_to_all | solution.py:589
  31.2 2.7 %shard_map.109 = (bf16[624,128]{1,0:T(8,128)(2,1)S(1)}, bf16[624,128]{1,0:T(8,128)(2,1)S(1)}, bf16[624,128]{1,0:T(8,128)(2,1)S(1)}, bf16[624,128]{1,0:T(8,128)(2,1)S(1)}) custom-call(s32[1]{0:T(128)} %bitcast.rank_ref, f32[64,256]{1,0:T(8,128)S(1)} %get-tuple-element.31.table_ref, f32[32,8,128]{2,1,0:T(8,128)S(1)} %all-to-all-done.1.coupling_ref, ...), custom_call_target="tpu_custom_call" | custom-call | bytes 8388608 | tf_op jit(solution)/shard_map/pallas_call | solution.py:207
  33.9 1.8 %collective-permute-start.10 = (bf16[624,128]{1,0:T(8,128)(2,1)S(1)}, bf16[624,128]{1,0:T(8,128)(2,1)S(1)}, u32[]{:S(2)}, u32[]{:S(2)}) collective-permute-start(bf16[624,128]{1,0:T(8,128)(2,1)S(1)} %get-tuple-element.46), channel_id=1, source_target_pairs={{0,8},{8,0},{16,24},{24,16},{1,9},{9,1},{17,25},{25,17},{2,10},{10... | collective-permute-start | bytes 479240 | tf_op jit(solution)/shard_map/ppermute | solution.py:537
  35.7 1.5 %collective-permute-start.11 = (bf16[624,128]{1,0:T(8,128)(2,1)S(1)}, bf16[624,128]{1,0:T(8,128)(2,1)S(1)}, u32[]{:S(2)}, u32[]{:S(2)}) collective-permute-start(bf16[624,128]{1,0:T(8,128)(2,1)S(1)} %get-tuple-element.47), channel_id=1, source_target_pairs={{0,16},{8,24},{16,0},{24,8},{1,17},{9,25},{17,1},{25,9},{2,18},{10... | collective-permute-start | bytes 479240 | tf_op jit(solution)/shard_map/ppermute | solution.py:537
  37.2 0.3 collective-permute-start.12
  37.4 2.3 %all-to-all-done.polar_ref = f32[32,8,128]{2,1,0:T(8,128)S(1)} async-done(((f32[32,8,128]{2,1,0:T(8,128)}), f32[32,8,128]{2,1,0:T(8,128)S(1)}, u32[]{:S(2)}, u32[]{:S(2)}) %all-to-all-start) | async-done | bytes 131104 | tf_op jit(solution)/shard_map/all_to_all | solution.py:589
  39.7 0.0 copy-done
  39.7 0.0 copy-done.5
  39.7 5.0 %shard_map.108 = bf16[2,2,384,384]{3,2,1,0:T(8,128)(2,1)} custom-call(f32[32,8,128]{2,1,0:T(8,128)S(1)} %all-to-all-done.polar_ref, bf16[2,2,384,384]{3,2,1,0:T(8,128)(2,1)S(1)} %copy-done, s32[17,128]{1,0:T(8,128)S(1)} %copy-done.5, f32[6,17,128]{2,1,0:T(8,128)S(1)} %get-tuple-element.42.pair_ref), custom_call_target="tpu_custom_call" | custom-call | bytes 20971520 | tf_op jit(solution)/shard_map/pallas_call | solution.py:207
  44.7 0.0 collective-permute-done.10.refs_1_
  44.7 0.0 collective-permute-done.11.refs_2_
  44.7 0.5 %collective-permute-done.12.refs_3_ = bf16[624,128]{1,0:T(8,128)(2,1)S(1)} collective-permute-done((bf16[624,128]{1,0:T(8,128)(2,1)S(1)}, bf16[624,128]{1,0:T(8,128)(2,1)S(1)}, u32[]{:S(2)}, u32[]{:S(2)}) %collective-permute-start.12) | collective-permute-done | bytes 159776 | tf_op jit(solution)/shard_map/ppermute | solution.py:537
  45.3 0.9 %shard_map.110 = bf16[2,1,2,144,544]{4,3,2,1,0:T(8,128)(2,1)} custom-call(s32[1]{0:T(128)} %bitcast.rank_ref, bf16[624,128]{1,0:T(8,128)(2,1)S(1)} %get-tuple-element.45.refs_0_, bf16[624,128]{1,0:T(8,128)(2,1)S(1)} %collective-permute-done.10.refs_1_, bf16[624,128]{1,0:T(8,128)(2,1)S(1)} %collective-permute-done.11.refs_2_, ...), custom_call_target="tpu_custom_call" | custom-call | bytes 4194304 | tf_op jit(solution)/shard_map/pallas_call | solution.py:207
Async XLA Ops:
  0.6 9.5 %copy-start.8 = (f32[64]{0:T(128)S(1)}, f32[64]{0:T(128)}, u32[]{:S(2)}) copy-start(f32[64]{0:T(128)} %param.17) | copy-start | bytes 772
  0.6 9.5 %copy-start.7 = (s32[64]{0:T(128)S(1)}, s32[64]{0:T(128)}, u32[]{:S(2)}) copy-start(s32[64]{0:T(128)} %param.16) | copy-start | bytes 772
  0.7 9.5 %copy-start.6 = (s32[64]{0:T(128)S(1)}, s32[64]{0:T(128)}, u32[]{:S(2)}) copy-start(s32[64]{0:T(128)} %param.15) | copy-start | bytes 772
  0.7 1.1 %copy-start.1 = (bf16[2,1,2,144,544]{4,3,2,1,0:T(8,128)(2,1)S(1)}, bf16[2,1,2,144,544]{4,3,2,1,0:T(8,128)(2,1)}, u32[]{:S(2)}) copy-start(bf16[2,1,2,144,544]{4,3,2,1,0:T(8,128)(2,1)} %source_ref.1) | copy-start | bytes 1880068
  1.8 4.7 %copy-start.2 = (bf16[2,1,2,144,544]{4,3,2,1,0:T(8,128)(2,1)S(1)}, bf16[2,1,2,144,544]{4,3,2,1,0:T(8,128)(2,1)}, u32[]{:S(2)}) copy-start(bf16[2,1,2,144,544]{4,3,2,1,0:T(8,128)(2,1)} %source_ref.2) | copy-start | bytes 1880068
  1.8 8.4 %copy-start.3 = (f32[2,2,9,17,128]{4,1,3,2,0:T(2,128)S(1)}, f32[2,2,9,17,128]{4,1,3,2,0:T(2,128)}, u32[]{:S(2)}) copy-start(f32[2,2,9,17,128]{4,1,3,2,0:T(2,128)} %param.11) | copy-start | bytes 940036
  1.8 8.4 %copy-start.4 = (f32[3,17,128]{2,0,1:T(4,128)S(1)}, f32[3,17,128]{2,0,1:T(4,128)}, u32[]{:S(2)}) copy-start(f32[3,17,128]{2,0,1:T(4,128)} %param.14) | copy-start | bytes 78340
  1.9 13.7 %collective-permute-start = (bf16[624,128]{1,0:T(8,128)(2,1)S(1)}, bf16[624,128]{1,0:T(8,128)(2,1)S(1)}, u32[]{:S(2)}, u32[]{:S(2)}) collective-permute-start(bf16[624,128]{1,0:T(8,128)(2,1)S(1)} %get-tuple-element.33), channel_id=1, source_target_pairs={{0,8},{8,0},{16,24},{24,16},{1,9},{9,1},{17,25},{25,17},{2,10},{10... | collective-permute-start | bytes 479240 | tf_op jit(solution)/shard_map/ppermute | solution.py:537
  4.9 13.4 %collective-permute-start.1 = (bf16[624,128]{1,0:T(8,128)(2,1)S(1)}, bf16[624,128]{1,0:T(8,128)(2,1)S(1)}, u32[]{:S(2)}, u32[]{:S(2)}) collective-permute-start(bf16[624,128]{1,0:T(8,128)(2,1)S(1)} %get-tuple-element.36), channel_id=1, source_target_pairs={{0,16},{8,24},{16,0},{24,8},{1,17},{9,25},{17,1},{25,9},{2,18},{10... | collective-permute-start | bytes 479240 | tf_op jit(solution)/shard_map/ppermute | solution.py:537
  6.5 11.9 %collective-permute-start.2 = (bf16[624,128]{1,0:T(8,128)(2,1)S(1)}, bf16[624,128]{1,0:T(8,128)(2,1)S(1)}, u32[]{:S(2)}, u32[]{:S(2)}) collective-permute-start(bf16[624,128]{1,0:T(8,128)(2,1)S(1)} %get-tuple-element.37), channel_id=1, source_target_pairs={{0,24},{8,16},{16,8},{24,0},{1,25},{9,17},{17,9},{25,1},{2,26},{10... | collective-permute-start | bytes 479240 | tf_op jit(solution)/shard_map/ppermute | solution.py:537
  6.6 12.2 %collective-permute-start.7 = (bf16[624,128]{1,0:T(8,128)(2,1)S(1)}, bf16[624,128]{1,0:T(8,128)(2,1)S(1)}, u32[]{:S(2)}, u32[]{:S(2)}) collective-permute-start(bf16[624,128]{1,0:T(8,128)(2,1)S(1)} %get-tuple-element.39), channel_id=1, source_target_pairs={{0,8},{8,0},{16,24},{24,16},{1,9},{9,1},{17,25},{25,17},{2,10},{10... | collective-permute-start | bytes 479240 | tf_op jit(solution)/shard_map/ppermute | solution.py:537
  8.6 10.3 %collective-permute-start.8 = (bf16[624,128]{1,0:T(8,128)(2,1)S(1)}, bf16[624,128]{1,0:T(8,128)(2,1)S(1)}, u32[]{:S(2)}, u32[]{:S(2)}) collective-permute-start(bf16[624,128]{1,0:T(8,128)(2,1)S(1)} %get-tuple-element.40), channel_id=1, source_target_pairs={{0,16},{8,24},{16,0},{24,8},{1,17},{9,25},{17,1},{25,9},{2,18},{10... | collective-permute-start | bytes 479240 | tf_op jit(solution)/shard_map/ppermute | solution.py:537
  11.6 15.0 %all-to-all-start.1 = ((f32[32,8,128]{2,1,0:T(8,128)}), f32[32,8,128]{2,1,0:T(8,128)S(1)}, u32[]{:S(2)}, u32[]{:S(2)}) async-start(f32[32,8,128]{2,1,0:T(8,128)} %get-tuple-element.43), calls=%async_computation.1 | async-start | bytes 262144 | tf_op jit(solution)/shard_map/all_to_all | solution.py:582
  15.6 8.5 %collective-permute-start.9 = (bf16[624,128]{1,0:T(8,128)(2,1)S(1)}, bf16[624,128]{1,0:T(8,128)(2,1)S(1)}, u32[]{:S(2)}, u32[]{:S(2)}) collective-permute-start(bf16[624,128]{1,0:T(8,128)(2,1)S(1)} %get-tuple-element.41), channel_id=1, source_target_pairs={{0,24},{8,16},{16,8},{24,0},{1,25},{9,17},{17,9},{25,1},{2,26},{10... | collective-permute-start | bytes 479240 | tf_op jit(solution)/shard_map/ppermute | solution.py:537
  18.3 5.8 %collective-permute-start.3 = (bf16[624,128]{1,0:T(8,128)(2,1)S(1)}, bf16[624,128]{1,0:T(8,128)(2,1)S(1)}, u32[]{:S(2)}, u32[]{:S(2)}) collective-permute-start(bf16[624,128]{1,0:T(8,128)(2,1)S(1)} %get-tuple-element.34.refs_0_), channel_id=1, source_target_pairs={{0,4},{4,0},{1,5},{5,1},{2,6},{6,2},{3,7},{7,3},{8,12},{12,8},{9,1... | collective-permute-start | bytes 479240 | tf_op jit(solution)/shard_map/ppermute | solution.py:537
  18.3 5.8 %collective-permute-start.4 = (bf16[624,128]{1,0:T(8,128)(2,1)S(1)}, bf16[624,128]{1,0:T(8,128)(2,1)S(1)}, u32[]{:S(2)}, u32[]{:S(2)}) collective-permute-start(bf16[624,128]{1,0:T(8,128)(2,1)S(1)} %collective-permute-done.refs_1_), channel_id=1, source_target_pairs={{0,4},{4,0},{1,5},{5,1},{2,6},{6,2},{3,7},{7,3},{8,12},{12,8},{9,1... | collective-permute-start | bytes 479240 | tf_op jit(solution)/shard_map/ppermute | solution.py:537
  18.8 5.3 %collective-permute-start.5 = (bf16[624,128]{1,0:T(8,128)(2,1)S(1)}, bf16[624,128]{1,0:T(8,128)(2,1)S(1)}, u32[]{:S(2)}, u32[]{:S(2)}) collective-permute-start(bf16[624,128]{1,0:T(8,128)(2,1)S(1)} %collective-permute-done.1.refs_2_), channel_id=1, source_target_pairs={{0,4},{4,0},{1,5},{5,1},{2,6},{6,2},{3,7},{7,3},{8,12},{12,8},{9,1... | collective-permute-start | bytes 479240 | tf_op jit(solution)/shard_map/ppermute | solution.py:537
  18.9 5.2 %collective-permute-start.6 = (bf16[624,128]{1,0:T(8,128)(2,1)S(1)}, bf16[624,128]{1,0:T(8,128)(2,1)S(1)}, u32[]{:S(2)}, u32[]{:S(2)}) collective-permute-start(bf16[624,128]{1,0:T(8,128)(2,1)S(1)} %collective-permute-done.2.refs_3_), channel_id=1, source_target_pairs={{0,4},{4,0},{1,5},{5,1},{2,6},{6,2},{3,7},{7,3},{8,12},{12,8},{9,1... | collective-permute-start | bytes 479240 | tf_op jit(solution)/shard_map/ppermute | solution.py:537
  26.6 13.2 %copy-start = (bf16[2,2,384,384]{3,2,1,0:T(8,128)(2,1)S(1)}, bf16[2,2,384,384]{3,2,1,0:T(8,128)(2,1)}, u32[]{:S(2)}) copy-start(bf16[2,2,384,384]{3,2,1,0:T(8,128)(2,1)} %ret_ref.1) | copy-start | bytes 3538948
  26.6 13.2 %copy-start.5 = (s32[17,128]{1,0:T(8,128)S(1)}, s32[17,128]{1,0:T(8,128)}, u32[]{:S(2)}) copy-start(s32[17,128]{1,0:T(8,128)} %near_ref.1) | copy-start | bytes 26116
  26.6 13.1 %all-to-all-start = ((f32[32,8,128]{2,1,0:T(8,128)}), f32[32,8,128]{2,1,0:T(8,128)S(1)}, u32[]{:S(2)}, u32[]{:S(2)}) async-start(f32[32,8,128]{2,1,0:T(8,128)} %shard_map.107), calls=%async_computation | async-start | bytes 262144 | tf_op jit(solution)/shard_map/all_to_all | solution.py:589
  33.9 10.8 %collective-permute-start.10 = (bf16[624,128]{1,0:T(8,128)(2,1)S(1)}, bf16[624,128]{1,0:T(8,128)(2,1)S(1)}, u32[]{:S(2)}, u32[]{:S(2)}) collective-permute-start(bf16[624,128]{1,0:T(8,128)(2,1)S(1)} %get-tuple-element.46), channel_id=1, source_target_pairs={{0,8},{8,0},{16,24},{24,16},{1,9},{9,1},{17,25},{25,17},{2,10},{10... | collective-permute-start | bytes 479240 | tf_op jit(solution)/shard_map/ppermute | solution.py:537
  35.7 9.0 %collective-permute-start.11 = (bf16[624,128]{1,0:T(8,128)(2,1)S(1)}, bf16[624,128]{1,0:T(8,128)(2,1)S(1)}, u32[]{:S(2)}, u32[]{:S(2)}) collective-permute-start(bf16[624,128]{1,0:T(8,128)(2,1)S(1)} %get-tuple-element.47), channel_id=1, source_target_pairs={{0,16},{8,24},{16,0},{24,8},{1,17},{9,25},{17,1},{25,9},{2,18},{10... | collective-permute-start | bytes 479240 | tf_op jit(solution)/shard_map/ppermute | solution.py:537
  37.2 8.1 %collective-permute-start.12 = (bf16[624,128]{1,0:T(8,128)(2,1)S(1)}, bf16[624,128]{1,0:T(8,128)(2,1)S(1)}, u32[]{:S(2)}, u32[]{:S(2)}) collective-permute-start(bf16[624,128]{1,0:T(8,128)(2,1)S(1)} %get-tuple-element.48), channel_id=1, source_target_pairs={{0,24},{8,16},{16,8},{24,0},{1,25},{9,17},{17,9},{25,1},{2,26},{10... | collective-permute-start | bytes 479240 | tf_op jit(solution)/shard_map/ppermute | solution.py:537

commit v6 on v5

--- a/solution.py
+++ b/solution.py
@@ -369,10 +369,14 @@
 def energy_kernel(plan, rank_ref, table_ref, coupling_ref, *refs):
     chips = plan.n_energy
     outs = refs[2 * chips : 3 * chips]
-    low_ref, sum_ref, weight_ref = refs[3 * chips :]
+    low_ref, sum_ref, weight_ref, mixed_ref = refs[3 * chips :]
     rank = rank_ref[0]
     flat = coupling_ref[...].reshape(plan.devices * 8, LANES)
-    weight_ref[...] = jnp.dot(table_ref[...], flat, precision=HIGH, preferred_element_type=F32)
+    weights = jnp.dot(table_ref[...], flat, precision=HIGH, preferred_element_type=F32)
+    following = pltpu.roll(weights, weights.shape[0] - 1, 0)
+    weight_ref[...] = weights
+    mixed_ref[0] = weights + following
+    mixed_ref[1] = following - weights
     stage_blocks(plan, rank, refs[:chips], low_ref, 2, 0)
     stage_blocks(plan, rank, refs[chips : 2 * chips], low_ref, 2, 1)
     count = plan.all_energies
@@ -380,28 +384,31 @@
     def run(base):
         def step(chunk, carry):
             rows = pl.ds(pl.multiple_of(chunk * 8, 8), 8)
-            re = [None] * count
-            im = [None] * count
+            both = [low_ref[2 * at, rows] + low_ref[2 * at + 1, rows] for at in range(2 * count)]
+            parts = [[None] * count for _ in range(3)]
             for energy_step in range(1, REACH + 1):
                 for q in range(2):
                     index = base + ((energy_step - 1) * 2 + q) * 2
-                    for part, sign in ((0, -1), (1, 1)):
-                        at = index + part * 2 * plan.classes
+                    for kind, sign in ((0, -1), (1, 1)):
+                        at = index + kind * 2 * plan.classes
                         w_re = jnp.broadcast_to(weight_ref[at : at + 1], (8, LANES))
-                        w_im = jnp.broadcast_to(weight_ref[at + 1 : at + 2], (8, LANES))
+                        w_sum = jnp.broadcast_to(mixed_ref[0, at : at + 1], (8, LANES))
+                        w_dif = jnp.broadcast_to(mixed_ref[1, at : at + 1], (8, LANES))
                         for energy in range(count):
                             other = energy + sign * energy_step
                             if other < 0 or other >= count:
                                 continue
-                            at = (other * 2 + q) * 2
-                            b_re, b_im = low_ref[at, rows], low_ref[at + 1, rows]
-                            t_re = w_re * b_re - w_im * b_im
-                            t_im = w_re * b_im + w_im * b_re
-                            re[energy] = t_re if re[energy] is None else re[energy] + t_re
-                            im[energy] = t_im if im[energy] is None else im[energy] + t_im
+                            at = other * 2 + q
+                            terms = (
+                                w_re * both[at],
+                                w_sum * low_ref[2 * at + 1, rows],
+                                w_dif * low_ref[2 * at, rows],
+                            )
+                            for part, term in zip(parts, terms):
+                                part[energy] = term if part[energy] is None else part[energy] + term
             for energy in range(count):
-                sum_ref[2 * energy, rows] = re[energy]
-                sum_ref[2 * energy + 1, rows] = im[energy]
+                sum_ref[2 * energy, rows] = parts[0][energy] - parts[1][energy]
+                sum_ref[2 * energy + 1, rows] = parts[0][energy] + parts[2][energy]
             return carry
 
         return step
@@ -590,7 +597,12 @@
     sums = call(
         functools.partial(energy_kernel, plan), [message] * chips,
         rank, table, coupling, *low, *low_beside,
-        scalars=1, scratch=[low_scratch, half_scratch, pltpu.VMEM((4 * lines, LANES), F32)],
+        scalars=1, scratch=[
+            low_scratch,
+            half_scratch,
+            pltpu.VMEM((4 * lines, LANES), F32),
+            pltpu.VMEM((2, 4 * lines, LANES), F32),
+        ],
         moved=8 * 2**20,
     )
     sums = to_chips(plan, sums)

time: 46.5 us -> 46.2 us (level)
  transfers between devices with their start and end apart: 15 -> 15, of which waited for: 3 -> 3; matrix products, arithmetic and copies ran while one was open for 0% -> 0% of each run, Pallas kernels for 25% -> 24%
where the time goes in v6:
time: 46.2 us; the launch traced here: 45.9 us
  starting transfers between devices  24 us (52%)
  Pallas kernels  12.3 us (27%)
  waiting for transfers between devices  7.73 us (17%)
  local copies, waits for them, and re-layouts  1.15 us (2%)
  between operations  0.76 us (2%)
    ppermute x13, starting transfers between devices, swap(): lax.ppermute(block, axis, [(i, i ^ distance) for i in range(lax.axis_size...  15.4 us
    pallas_call x7, Pallas kernels, call(): pl.pallas_call(kernel, out_shape=out_shape, in_specs=specs, out_specs=[vm...  12.3 us
    ppermute x13, waiting for transfers between devices, swap(): lax.ppermute(block, axis, [(i, i ^ distance) for i in range(lax.axis_size...  5.05 us
    all_to_all x1, starting transfers between devices, dealt(): polar = lax.all_to_all(polar, EVERY, 0, 0, tiled=True)  4.63 us
    all_to_all x1, starting transfers between devices, dealt(): coupling = lax.all_to_all(coupling, EVERY, 0, 0, tiled=True)  3.97 us
    all_to_all x1, waiting for transfers between devices, dealt(): polar = lax.all_to_all(polar, EVERY, 0, 0, tiled=True)  2.68 us
    unnamed x18, local copies, waits for them, and re-layouts  1.15 us
  transfers between devices with their start and end apart: 15, of which 3 were waited for; matrix products, arithmetic and copies ran while one was open for 0% of the time, Pallas kernels for 24%

profile of v6, /device:TPU:0, one launch (start us, length us, event | category | flops | bytes accessed | tf_op | source)
XLA Modules:
  0.0 45.9 jit_solution(8974261772365169526)
XLA Ops:
  0.6 0.0 copy-start.8
  0.6 0.0 copy-start.7
  0.7 0.0 copy-start.6
  0.7 0.0 copy-start.1
  0.7 1.1 %copy-done.1 = bf16[2,1,2,144,544]{4,3,2,1,0:T(8,128)(2,1)S(1)} copy-done((bf16[2,1,2,144,544]{4,3,2,1,0:T(8,128)(2,1)S(1)}, bf16[2,1,2,144,544]{4,3,2,1,0:T(8,128)(2,1)}, u32[]{:S(2)}) %copy-start.1) | copy-done | bytes 626712
  1.8 0.0 copy-start.2
  1.8 0.0 copy-start.3
  1.8 0.0 copy-start.4
  1.8 0.1 shard_map.104
  1.9 3.0 %collective-permute-start = (bf16[624,128]{1,0:T(8,128)(2,1)S(1)}, bf16[624,128]{1,0:T(8,128)(2,1)S(1)}, u32[]{:S(2)}, u32[]{:S(2)}) collective-permute-start(bf16[624,128]{1,0:T(8,128)(2,1)S(1)} %get-tuple-element.33), channel_id=1, source_target_pairs={{0,8},{8,0},{16,24},{24,16},{1,9},{9,1},{17,25},{25,17},{2,10},{10... | collective-permute-start | bytes 479240 | tf_op jit(solution)/shard_map/ppermute | solution.py:544
  4.9 1.5 %collective-permute-start.1 = (bf16[624,128]{1,0:T(8,128)(2,1)S(1)}, bf16[624,128]{1,0:T(8,128)(2,1)S(1)}, u32[]{:S(2)}, u32[]{:S(2)}) collective-permute-start(bf16[624,128]{1,0:T(8,128)(2,1)S(1)} %get-tuple-element.36), channel_id=1, source_target_pairs={{0,16},{8,24},{16,0},{24,8},{1,17},{9,25},{17,1},{25,9},{2,18},{10... | collective-permute-start | bytes 479240 | tf_op jit(solution)/shard_map/ppermute | solution.py:544
  6.5 0.0 collective-permute-start.2
  6.5 0.0 copy-done.2
  6.5 0.1 shard_map.105
  6.6 2.0 %collective-permute-start.7 = (bf16[624,128]{1,0:T(8,128)(2,1)S(1)}, bf16[624,128]{1,0:T(8,128)(2,1)S(1)}, u32[]{:S(2)}, u32[]{:S(2)}) collective-permute-start(bf16[624,128]{1,0:T(8,128)(2,1)S(1)} %get-tuple-element.39), channel_id=1, source_target_pairs={{0,8},{8,0},{16,24},{24,16},{1,9},{9,1},{17,25},{25,17},{2,10},{10... | collective-permute-start | bytes 479240 | tf_op jit(solution)/shard_map/ppermute | solution.py:544
  8.6 1.5 %collective-permute-start.8 = (bf16[624,128]{1,0:T(8,128)(2,1)S(1)}, bf16[624,128]{1,0:T(8,128)(2,1)S(1)}, u32[]{:S(2)}, u32[]{:S(2)}) collective-permute-start(bf16[624,128]{1,0:T(8,128)(2,1)S(1)} %get-tuple-element.40), channel_id=1, source_target_pairs={{0,16},{8,24},{16,0},{24,8},{1,17},{9,25},{17,1},{25,9},{2,18},{10... | collective-permute-start | bytes 479240 | tf_op jit(solution)/shard_map/ppermute | solution.py:544
  10.1 0.0 copy-done.8
  10.1 0.0 copy-done.7
  10.1 0.0 copy-done.6
  10.1 0.0 copy-done.3
  10.2 0.0 copy-done.4
  10.2 1.4 %shard_map.106 = (f32[32,8,128]{2,1,0:T(8,128)}, f32[64,256]{1,0:T(8,128)S(1)}, f32[6,17,128]{2,1,0:T(8,128)S(1)}) custom-call(f32[2,9,17,2,128]{4,3,2,1,0:T(2,128)S(1)} %bitcast.6, f32[17,3,128]{2,1,0:T(4,128)S(1)} %bitcast.7, s32[1,64]{1,0:T(1,128)S(1)} %bitcast.8, s32[1,64]{1,0:T(1,128)S(1)} %bitcast.9, f32[1,64]{1,0:T(1,128)S(1)} %bitcast.10), custom_call_target="tpu_custom_call" | custom-call | bytes 313344 | tf_op jit(solution)/shard_map/pallas_call | solution.py:207
  11.6 4.0 %all-to-all-start.1 = ((f32[32,8,128]{2,1,0:T(8,128)}), f32[32,8,128]{2,1,0:T(8,128)S(1)}, u32[]{:S(2)}, u32[]{:S(2)}) async-start(f32[32,8,128]{2,1,0:T(8,128)} %get-tuple-element.43), calls=%async_computation.1 | async-start | bytes 262144 | tf_op jit(solution)/shard_map/all_to_all | solution.py:589
  15.6 0.0 collective-permute-done.refs_1_
  15.6 2.7 %collective-permute-start.9 = (bf16[624,128]{1,0:T(8,128)(2,1)S(1)}, bf16[624,128]{1,0:T(8,128)(2,1)S(1)}, u32[]{:S(2)}, u32[]{:S(2)}) collective-permute-start(bf16[624,128]{1,0:T(8,128)(2,1)S(1)} %get-tuple-element.41), channel_id=1, source_target_pairs={{0,24},{8,16},{16,8},{24,0},{1,25},{9,17},{17,9},{25,1},{2,26},{10... | collective-permute-start | bytes 479240 | tf_op jit(solution)/shard_map/ppermute | solution.py:544
  18.3 0.0 collective-permute-done.1.refs_2_
  18.3 0.0 collective-permute-start.3
  18.3 0.0 collective-permute-done.2.refs_3_
  18.3 0.5 %collective-permute-start.4 = (bf16[624,128]{1,0:T(8,128)(2,1)S(1)}, bf16[624,128]{1,0:T(8,128)(2,1)S(1)}, u32[]{:S(2)}, u32[]{:S(2)}) collective-permute-start(bf16[624,128]{1,0:T(8,128)(2,1)S(1)} %collective-permute-done.refs_1_), channel_id=1, source_target_pairs={{0,4},{4,0},{1,5},{5,1},{2,6},{6,2},{3,7},{7,3},{8,12},{12,8},{9,1... | collective-permute-start | bytes 479240 | tf_op jit(solution)/shard_map/ppermute | solution.py:544
  18.8 0.0 collective-permute-done.7.refs_9_
  18.8 0.1 collective-permute-start.5
  18.9 0.0 collective-permute-done.8.refs_10_
  18.9 0.4 collective-permute-start.6
  19.4 4.8 %collective-permute-done.9.refs_11_ = bf16[624,128]{1,0:T(8,128)(2,1)S(1)} collective-permute-done((bf16[624,128]{1,0:T(8,128)(2,1)S(1)}, bf16[624,128]{1,0:T(8,128)(2,1)S(1)}, u32[]{:S(2)}, u32[]{:S(2)}) %collective-permute-start.9) | collective-permute-done | bytes 159776 | tf_op jit(solution)/shard_map/ppermute | solution.py:544
  24.1 0.0 collective-permute-done.3.refs_4_
  24.1 0.0 collective-permute-done.4.refs_5_
  24.1 0.0 collective-permute-done.5.refs_6_
  24.1 0.0 collective-permute-done.6.refs_7_
  24.1 2.4 %shard_map.107 = f32[32,8,128]{2,1,0:T(8,128)} custom-call(s32[1]{0:T(128)} %bitcast.rank_ref, f32[64,256]{1,0:T(8,128)S(1)} %get-tuple-element.31.table_ref, bf16[624,128]{1,0:T(8,128)(2,1)S(1)} %get-tuple-element.34.refs_0_, bf16[624,128]{1,0:T(8,128)(2,1)S(1)} %collective-permute-done.refs_1_, bf16[624,128]{1,0:T(8,128)(2,1)S(1)} %collective-permute-done.1.refs_2_, ...), custom_call_target="tpu_custom_call" | custom-call | bytes 8388608 | tf_op jit(solution)/shard_map/pallas_call | solution.py:207
  26.6 0.0 copy-start
  26.6 0.0 copy-start.5
  26.6 0.0 all-to-all-done.1.coupling_ref
  26.6 4.6 %all-to-all-start = ((f32[32,8,128]{2,1,0:T(8,128)}), f32[32,8,128]{2,1,0:T(8,128)S(1)}, u32[]{:S(2)}, u32[]{:S(2)}) async-start(f32[32,8,128]{2,1,0:T(8,128)} %shard_map.107), calls=%async_computation | async-start | bytes 262144 | tf_op jit(solution)/shard_map/all_to_all | solution.py:596
  31.2 2.3 %shard_map.109 = (bf16[624,128]{1,0:T(8,128)(2,1)S(1)}, bf16[624,128]{1,0:T(8,128)(2,1)S(1)}, bf16[624,128]{1,0:T(8,128)(2,1)S(1)}, bf16[624,128]{1,0:T(8,128)(2,1)S(1)}) custom-call(s32[1]{0:T(128)} %bitcast.rank_ref, f32[64,256]{1,0:T(8,128)S(1)} %get-tuple-element.31.table_ref, f32[32,8,128]{2,1,0:T(8,128)S(1)} %all-to-all-done.1.coupling_ref, ...), custom_call_target="tpu_custom_call" | custom-call | bytes 8388608 | tf_op jit(solution)/shard_map/pallas_call | solution.py:207
  33.5 1.8 %collective-permute-start.10 = (bf16[624,128]{1,0:T(8,128)(2,1)S(1)}, bf16[624,128]{1,0:T(8,128)(2,1)S(1)}, u32[]{:S(2)}, u32[]{:S(2)}) collective-permute-start(bf16[624,128]{1,0:T(8,128)(2,1)S(1)} %get-tuple-element.46), channel_id=1, source_target_pairs={{0,8},{8,0},{16,24},{24,16},{1,9},{9,1},{17,25},{25,17},{2,10},{10... | collective-permute-start | bytes 479240 | tf_op jit(solution)/shard_map/ppermute | solution.py:544
  35.3 1.5 %collective-permute-start.11 = (bf16[624,128]{1,0:T(8,128)(2,1)S(1)}, bf16[624,128]{1,0:T(8,128)(2,1)S(1)}, u32[]{:S(2)}, u32[]{:S(2)}) collective-permute-start(bf16[624,128]{1,0:T(8,128)(2,1)S(1)} %get-tuple-element.47), channel_id=1, source_target_pairs={{0,16},{8,24},{16,0},{24,8},{1,17},{9,25},{17,1},{25,9},{2,18},{10... | collective-permute-start | bytes 479240 | tf_op jit(solution)/shard_map/ppermute | solution.py:544
  36.8 0.3 collective-permute-start.12
  37.0 2.7 %all-to-all-done.polar_ref = f32[32,8,128]{2,1,0:T(8,128)S(1)} async-done(((f32[32,8,128]{2,1,0:T(8,128)}), f32[32,8,128]{2,1,0:T(8,128)S(1)}, u32[]{:S(2)}, u32[]{:S(2)}) %all-to-all-start) | async-done | bytes 131104 | tf_op jit(solution)/shard_map/all_to_all | solution.py:596
  39.7 0.0 copy-done
  39.7 0.0 copy-done.5
  39.7 5.0 %shard_map.108 = bf16[2,2,384,384]{3,2,1,0:T(8,128)(2,1)} custom-call(f32[32,8,128]{2,1,0:T(8,128)S(1)} %all-to-all-done.polar_ref, bf16[2,2,384,384]{3,2,1,0:T(8,128)(2,1)S(1)} %copy-done, s32[17,128]{1,0:T(8,128)S(1)} %copy-done.5, f32[6,17,128]{2,1,0:T(8,128)S(1)} %get-tuple-element.42.pair_ref), custom_call_target="tpu_custom_call" | custom-call | bytes 20971520 | tf_op jit(solution)/shard_map/pallas_call | solution.py:207
  44.7 0.0 collective-permute-done.10.refs_1_
  44.7 0.3 collective-permute-done.11.refs_2_
  45.0 0.0 collective-permute-done.12.refs_3_
  45.0 0.9 %shard_map.110 = bf16[2,1,2,144,544]{4,3,2,1,0:T(8,128)(2,1)} custom-call(s32[1]{0:T(128)} %bitcast.rank_ref, bf16[624,128]{1,0:T(8,128)(2,1)S(1)} %get-tuple-element.45.refs_0_, bf16[624,128]{1,0:T(8,128)(2,1)S(1)} %collective-permute-done.10.refs_1_, bf16[624,128]{1,0:T(8,128)(2,1)S(1)} %collective-permute-done.11.refs_2_, ...), custom_call_target="tpu_custom_call" | custom-call | bytes 4194304 | tf_op jit(solution)/shard_map/pallas_call | solution.py:207
Async XLA Ops:
  0.6 9.5 %copy-start.8 = (f32[64]{0:T(128)S(1)}, f32[64]{0:T(128)}, u32[]{:S(2)}) copy-start(f32[64]{0:T(128)} %param.17) | copy-start | bytes 772
  0.6 9.5 %copy-start.7 = (s32[64]{0:T(128)S(1)}, s32[64]{0:T(128)}, u32[]{:S(2)}) copy-start(s32[64]{0:T(128)} %param.16) | copy-start | bytes 772
  0.7 9.5 %copy-start.6 = (s32[64]{0:T(128)S(1)}, s32[64]{0:T(128)}, u32[]{:S(2)}) copy-start(s32[64]{0:T(128)} %param.15) | copy-start | bytes 772
  0.7 1.1 %copy-start.1 = (bf16[2,1,2,144,544]{4,3,2,1,0:T(8,128)(2,1)S(1)}, bf16[2,1,2,144,544]{4,3,2,1,0:T(8,128)(2,1)}, u32[]{:S(2)}) copy-start(bf16[2,1,2,144,544]{4,3,2,1,0:T(8,128)(2,1)} %source_ref.1) | copy-start | bytes 1880068
  1.8 4.7 %copy-start.2 = (bf16[2,1,2,144,544]{4,3,2,1,0:T(8,128)(2,1)S(1)}, bf16[2,1,2,144,544]{4,3,2,1,0:T(8,128)(2,1)}, u32[]{:S(2)}) copy-start(bf16[2,1,2,144,544]{4,3,2,1,0:T(8,128)(2,1)} %source_ref.2) | copy-start | bytes 1880068
  1.8 8.4 %copy-start.3 = (f32[2,2,9,17,128]{4,1,3,2,0:T(2,128)S(1)}, f32[2,2,9,17,128]{4,1,3,2,0:T(2,128)}, u32[]{:S(2)}) copy-start(f32[2,2,9,17,128]{4,1,3,2,0:T(2,128)} %param.11) | copy-start | bytes 940036
  1.8 8.4 %copy-start.4 = (f32[3,17,128]{2,0,1:T(4,128)S(1)}, f32[3,17,128]{2,0,1:T(4,128)}, u32[]{:S(2)}) copy-start(f32[3,17,128]{2,0,1:T(4,128)} %param.14) | copy-start | bytes 78340
  1.9 13.7 %collective-permute-start = (bf16[624,128]{1,0:T(8,128)(2,1)S(1)}, bf16[624,128]{1,0:T(8,128)(2,1)S(1)}, u32[]{:S(2)}, u32[]{:S(2)}) collective-permute-start(bf16[624,128]{1,0:T(8,128)(2,1)S(1)} %get-tuple-element.33), channel_id=1, source_target_pairs={{0,8},{8,0},{16,24},{24,16},{1,9},{9,1},{17,25},{25,17},{2,10},{10... | collective-permute-start | bytes 479240 | tf_op jit(solution)/shard_map/ppermute | solution.py:544
  4.9 13.4 %collective-permute-start.1 = (bf16[624,128]{1,0:T(8,128)(2,1)S(1)}, bf16[624,128]{1,0:T(8,128)(2,1)S(1)}, u32[]{:S(2)}, u32[]{:S(2)}) collective-permute-start(bf16[624,128]{1,0:T(8,128)(2,1)S(1)} %get-tuple-element.36), channel_id=1, source_target_pairs={{0,16},{8,24},{16,0},{24,8},{1,17},{9,25},{17,1},{25,9},{2,18},{10... | collective-permute-start | bytes 479240 | tf_op jit(solution)/shard_map/ppermute | solution.py:544
  6.5 11.9 %collective-permute-start.2 = (bf16[624,128]{1,0:T(8,128)(2,1)S(1)}, bf16[624,128]{1,0:T(8,128)(2,1)S(1)}, u32[]{:S(2)}, u32[]{:S(2)}) collective-permute-start(bf16[624,128]{1,0:T(8,128)(2,1)S(1)} %get-tuple-element.37), channel_id=1, source_target_pairs={{0,24},{8,16},{16,8},{24,0},{1,25},{9,17},{17,9},{25,1},{2,26},{10... | collective-permute-start | bytes 479240 | tf_op jit(solution)/shard_map/ppermute | solution.py:544
  6.6 12.2 %collective-permute-start.7 = (bf16[624,128]{1,0:T(8,128)(2,1)S(1)}, bf16[624,128]{1,0:T(8,128)(2,1)S(1)}, u32[]{:S(2)}, u32[]{:S(2)}) collective-permute-start(bf16[624,128]{1,0:T(8,128)(2,1)S(1)} %get-tuple-element.39), channel_id=1, source_target_pairs={{0,8},{8,0},{16,24},{24,16},{1,9},{9,1},{17,25},{25,17},{2,10},{10... | collective-permute-start | bytes 479240 | tf_op jit(solution)/shard_map/ppermute | solution.py:544
  8.6 10.3 %collective-permute-start.8 = (bf16[624,128]{1,0:T(8,128)(2,1)S(1)}, bf16[624,128]{1,0:T(8,128)(2,1)S(1)}, u32[]{:S(2)}, u32[]{:S(2)}) collective-permute-start(bf16[624,128]{1,0:T(8,128)(2,1)S(1)} %get-tuple-element.40), channel_id=1, source_target_pairs={{0,16},{8,24},{16,0},{24,8},{1,17},{9,25},{17,1},{25,9},{2,18},{10... | collective-permute-start | bytes 479240 | tf_op jit(solution)/shard_map/ppermute | solution.py:544
  11.6 15.0 %all-to-all-start.1 = ((f32[32,8,128]{2,1,0:T(8,128)}), f32[32,8,128]{2,1,0:T(8,128)S(1)}, u32[]{:S(2)}, u32[]{:S(2)}) async-start(f32[32,8,128]{2,1,0:T(8,128)} %get-tuple-element.43), calls=%async_computation.1 | async-start | bytes 262144 | tf_op jit(solution)/shard_map/all_to_all | solution.py:589
  15.6 8.5 %collective-permute-start.9 = (bf16[624,128]{1,0:T(8,128)(2,1)S(1)}, bf16[624,128]{1,0:T(8,128)(2,1)S(1)}, u32[]{:S(2)}, u32[]{:S(2)}) collective-permute-start(bf16[624,128]{1,0:T(8,128)(2,1)S(1)} %get-tuple-element.41), channel_id=1, source_target_pairs={{0,24},{8,16},{16,8},{24,0},{1,25},{9,17},{17,9},{25,1},{2,26},{10... | collective-permute-start | bytes 479240 | tf_op jit(solution)/shard_map/ppermute | solution.py:544
  18.3 5.8 %collective-permute-start.3 = (bf16[624,128]{1,0:T(8,128)(2,1)S(1)}, bf16[624,128]{1,0:T(8,128)(2,1)S(1)}, u32[]{:S(2)}, u32[]{:S(2)}) collective-permute-start(bf16[624,128]{1,0:T(8,128)(2,1)S(1)} %get-tuple-element.34.refs_0_), channel_id=1, source_target_pairs={{0,4},{4,0},{1,5},{5,1},{2,6},{6,2},{3,7},{7,3},{8,12},{12,8},{9,1... | collective-permute-start | bytes 479240 | tf_op jit(solution)/shard_map/ppermute | solution.py:544
  18.3 5.8 %collective-permute-start.4 = (bf16[624,128]{1,0:T(8,128)(2,1)S(1)}, bf16[624,128]{1,0:T(8,128)(2,1)S(1)}, u32[]{:S(2)}, u32[]{:S(2)}) collective-permute-start(bf16[624,128]{1,0:T(8,128)(2,1)S(1)} %collective-permute-done.refs_1_), channel_id=1, source_target_pairs={{0,4},{4,0},{1,5},{5,1},{2,6},{6,2},{3,7},{7,3},{8,12},{12,8},{9,1... | collective-permute-start | bytes 479240 | tf_op jit(solution)/shard_map/ppermute | solution.py:544
  18.8 5.3 %collective-permute-start.5 = (bf16[624,128]{1,0:T(8,128)(2,1)S(1)}, bf16[624,128]{1,0:T(8,128)(2,1)S(1)}, u32[]{:S(2)}, u32[]{:S(2)}) collective-permute-start(bf16[624,128]{1,0:T(8,128)(2,1)S(1)} %collective-permute-done.1.refs_2_), channel_id=1, source_target_pairs={{0,4},{4,0},{1,5},{5,1},{2,6},{6,2},{3,7},{7,3},{8,12},{12,8},{9,1... | collective-permute-start | bytes 479240 | tf_op jit(solution)/shard_map/ppermute | solution.py:544
  18.9 5.2 %collective-permute-start.6 = (bf16[624,128]{1,0:T(8,128)(2,1)S(1)}, bf16[624,128]{1,0:T(8,128)(2,1)S(1)}, u32[]{:S(2)}, u32[]{:S(2)}) collective-permute-start(bf16[624,128]{1,0:T(8,128)(2,1)S(1)} %collective-permute-done.2.refs_3_), channel_id=1, source_target_pairs={{0,4},{4,0},{1,5},{5,1},{2,6},{6,2},{3,7},{7,3},{8,12},{12,8},{9,1... | collective-permute-start | bytes 479240 | tf_op jit(solution)/shard_map/ppermute | solution.py:544
  26.6 13.2 %copy-start = (bf16[2,2,384,384]{3,2,1,0:T(8,128)(2,1)S(1)}, bf16[2,2,384,384]{3,2,1,0:T(8,128)(2,1)}, u32[]{:S(2)}) copy-start(bf16[2,2,384,384]{3,2,1,0:T(8,128)(2,1)} %ret_ref.1) | copy-start | bytes 3538948
  26.6 13.2 %copy-start.5 = (s32[17,128]{1,0:T(8,128)S(1)}, s32[17,128]{1,0:T(8,128)}, u32[]{:S(2)}) copy-start(s32[17,128]{1,0:T(8,128)} %near_ref.1) | copy-start | bytes 26116
  26.6 13.1 %all-to-all-start = ((f32[32,8,128]{2,1,0:T(8,128)}), f32[32,8,128]{2,1,0:T(8,128)S(1)}, u32[]{:S(2)}, u32[]{:S(2)}) async-start(f32[32,8,128]{2,1,0:T(8,128)} %shard_map.107), calls=%async_computation | async-start | bytes 262144 | tf_op jit(solution)/shard_map/all_to_all | solution.py:596
  33.5 11.2 %collective-permute-start.10 = (bf16[624,128]{1,0:T(8,128)(2,1)S(1)}, bf16[624,128]{1,0:T(8,128)(2,1)S(1)}, u32[]{:S(2)}, u32[]{:S(2)}) collective-permute-start(bf16[624,128]{1,0:T(8,128)(2,1)S(1)} %get-tuple-element.46), channel_id=1, source_target_pairs={{0,8},{8,0},{16,24},{24,16},{1,9},{9,1},{17,25},{25,17},{2,10},{10... | collective-permute-start | bytes 479240 | tf_op jit(solution)/shard_map/ppermute | solution.py:544
  35.3 9.7 %collective-permute-start.11 = (bf16[624,128]{1,0:T(8,128)(2,1)S(1)}, bf16[624,128]{1,0:T(8,128)(2,1)S(1)}, u32[]{:S(2)}, u32[]{:S(2)}) collective-permute-start(bf16[624,128]{1,0:T(8,128)(2,1)S(1)} %get-tuple-element.47), channel_id=1, source_target_pairs={{0,16},{8,24},{16,0},{24,8},{1,17},{9,25},{17,1},{25,9},{2,18},{10... | collective-permute-start | bytes 479240 | tf_op jit(solution)/shard_map/ppermute | solution.py:544
  36.8 8.2 %collective-permute-start.12 = (bf16[624,128]{1,0:T(8,128)(2,1)S(1)}, bf16[624,128]{1,0:T(8,128)(2,1)S(1)}, u32[]{:S(2)}, u32[]{:S(2)}) collective-permute-start(bf16[624,128]{1,0:T(8,128)(2,1)S(1)} %get-tuple-element.48), channel_id=1, source_target_pairs={{0,24},{8,16},{16,8},{24,0},{1,25},{9,17},{17,9},{25,1},{2,26},{10... | collective-permute-start | bytes 479240 | tf_op jit(solution)/shard_map/ppermute | solution.py:544

commit v7 on v6

--- a/solution.py
+++ b/solution.py
@@ -339,22 +339,29 @@
     def step(chunk, sums):
         rows = pl.ds(pl.multiple_of(chunk * 8, 8), 8)
         sums = list(sums)
-        for energy in range(count):
+        both = [low_ref[2 * at, rows] + low_ref[2 * at + 1, rows] for at in range(2 * count)]
+        for energy in range(count - 1):
             high_re, high_im = high_ref[2 * energy, rows], high_ref[2 * energy + 1, rows]
-            for energy_step in range(1, REACH + 1):
-                if energy + energy_step >= count:
-                    continue
+            high_sum, high_dif = high_re + high_im, high_re - high_im
+            for energy_step in range(1, min(REACH, count - 1 - energy) + 1):
                 for q in range(2):
-                    index = ((energy_step - 1) * 2 + q) * 2
-                    low = ((energy + energy_step) * 2 + q) * 2
-                    low_re, low_im = low_ref[low, rows], low_ref[low + 1, rows]
-                    sums[index] = sums[index] + (low_re * high_re + low_im * high_im)
-                    sums[index + 1] = sums[index + 1] + (low_im * high_re - low_re * high_im)
+                    index = ((energy_step - 1) * 2 + q) * 3
+                    at = (energy + energy_step) * 2 + q
+                    sums[index] = sums[index] + both[at] * high_re
+                    sums[index + 1] = sums[index + 1] + low_ref[2 * at + 1, rows] * high_dif
+                    sums[index + 2] = sums[index + 2] + low_ref[2 * at, rows] * high_sum
         return tuple(sums)
 
-    none = tuple(jnp.zeros((8, LANES), F32) for _ in range(2 * plan.classes))
-    main = lax.fori_loop(0, plan.entries // 8, step, none, unroll=3)
-    rest = lax.fori_loop(plan.entries // 8, plan.held // 8, step, none, unroll=5)
+    none = tuple(jnp.zeros((8, LANES), F32) for _ in range(3 * plan.classes))
+
+    def joined(sums):
+        parts = []
+        for index in range(0, 3 * plan.classes, 3):
+            parts += [sums[index] - sums[index + 1], sums[index] - sums[index + 2]]
+        return parts
+
+    main = joined(lax.fori_loop(0, plan.entries // 8, step, none, unroll=3))
+    rest = joined(lax.fori_loop(plan.entries // 8, plan.held // 8, step, none, unroll=5))
     scale = float(count * 2 * plan.entries) ** (-0.5)
     lines = [jnp.sum(part, axis=0, keepdims=True) * scale for part in main + rest]
     sums = jnp.concatenate(lines, axis=0)

time: 46.2 us -> 46 us (level)
  no operation moved by 1% of the time
where the time goes in v7:
time: 46 us; the launch traced here: 45.8 us
  starting transfers between devices  24 us (52%)
  Pallas kernels  12.1 us (26%)
  waiting for transfers between devices  7.73 us (17%)
  local copies, waits for them, and re-layouts  1.15 us (2%)
  between operations  0.76 us (2%)
    ppermute x13, starting transfers between devices, swap(): lax.ppermute(block, axis, [(i, i ^ distance) for i in range(lax.axis_size...  15.4 us
    pallas_call x7, Pallas kernels, call(): pl.pallas_call(kernel, out_shape=out_shape, in_specs=specs, out_specs=[vm...  12.1 us
    ppermute x13, waiting for transfers between devices, swap(): lax.ppermute(block, axis, [(i, i ^ distance) for i in range(lax.axis_size...  5.05 us
    all_to_all x1, starting transfers between devices, dealt(): polar = lax.all_to_all(polar, EVERY, 0, 0, tiled=True)  4.62 us
    all_to_all x1, starting transfers between devices, dealt(): coupling = lax.all_to_all(coupling, EVERY, 0, 0, tiled=True)  3.97 us
    all_to_all x1, waiting for transfers between devices, dealt(): polar = lax.all_to_all(polar, EVERY, 0, 0, tiled=True)  2.68 us
    unnamed x18, local copies, waits for them, and re-layouts  1.15 us
  transfers between devices with their start and end apart: 15, of which 3 were waited for; matrix products, arithmetic and copies ran while one was open for 0% of the time, Pallas kernels for 24%

profile of v7, /device:TPU:0, one launch (start us, length us, event | category | flops | bytes accessed | tf_op | source)
XLA Modules:
  0.0 45.8 jit_solution(1021911280472121618)
XLA Ops:
  0.6 0.0 copy-start.8
  0.6 0.0 copy-start.7
  0.7 0.0 copy-start.6
  0.7 0.0 copy-start.1
  0.7 1.1 %copy-done.1 = bf16[2,1,2,144,544]{4,3,2,1,0:T(8,128)(2,1)S(1)} copy-done((bf16[2,1,2,144,544]{4,3,2,1,0:T(8,128)(2,1)S(1)}, bf16[2,1,2,144,544]{4,3,2,1,0:T(8,128)(2,1)}, u32[]{:S(2)}) %copy-start.1) | copy-done | bytes 626712
  1.8 0.0 copy-start.2
  1.8 0.0 copy-start.3
  1.8 0.0 copy-start.4
  1.8 0.1 shard_map.104
  1.9 3.0 %collective-permute-start = (bf16[624,128]{1,0:T(8,128)(2,1)S(1)}, bf16[624,128]{1,0:T(8,128)(2,1)S(1)}, u32[]{:S(2)}, u32[]{:S(2)}) collective-permute-start(bf16[624,128]{1,0:T(8,128)(2,1)S(1)} %get-tuple-element.33), channel_id=1, source_target_pairs={{0,8},{8,0},{16,24},{24,16},{1,9},{9,1},{17,25},{25,17},{2,10},{10... | collective-permute-start | bytes 479240 | tf_op jit(solution)/shard_map/ppermute | solution.py:551
  4.9 1.5 %collective-permute-start.1 = (bf16[624,128]{1,0:T(8,128)(2,1)S(1)}, bf16[624,128]{1,0:T(8,128)(2,1)S(1)}, u32[]{:S(2)}, u32[]{:S(2)}) collective-permute-start(bf16[624,128]{1,0:T(8,128)(2,1)S(1)} %get-tuple-element.36), channel_id=1, source_target_pairs={{0,16},{8,24},{16,0},{24,8},{1,17},{9,25},{17,1},{25,9},{2,18},{10... | collective-permute-start | bytes 479240 | tf_op jit(solution)/shard_map/ppermute | solution.py:551
  6.5 0.0 collective-permute-start.2
  6.5 0.0 copy-done.2
  6.5 0.1 shard_map.105
  6.6 2.0 %collective-permute-start.7 = (bf16[624,128]{1,0:T(8,128)(2,1)S(1)}, bf16[624,128]{1,0:T(8,128)(2,1)S(1)}, u32[]{:S(2)}, u32[]{:S(2)}) collective-permute-start(bf16[624,128]{1,0:T(8,128)(2,1)S(1)} %get-tuple-element.39), channel_id=1, source_target_pairs={{0,8},{8,0},{16,24},{24,16},{1,9},{9,1},{17,25},{25,17},{2,10},{10... | collective-permute-start | bytes 479240 | tf_op jit(solution)/shard_map/ppermute | solution.py:551
  8.6 1.5 %collective-permute-start.8 = (bf16[624,128]{1,0:T(8,128)(2,1)S(1)}, bf16[624,128]{1,0:T(8,128)(2,1)S(1)}, u32[]{:S(2)}, u32[]{:S(2)}) collective-permute-start(bf16[624,128]{1,0:T(8,128)(2,1)S(1)} %get-tuple-element.40), channel_id=1, source_target_pairs={{0,16},{8,24},{16,0},{24,8},{1,17},{9,25},{17,1},{25,9},{2,18},{10... | collective-permute-start | bytes 479240 | tf_op jit(solution)/shard_map/ppermute | solution.py:551
  10.1 0.0 copy-done.8
  10.1 0.0 copy-done.7
  10.1 0.0 copy-done.6
  10.1 0.0 copy-done.3
  10.2 0.0 copy-done.4
  10.2 1.4 %shard_map.106 = (f32[32,8,128]{2,1,0:T(8,128)}, f32[64,256]{1,0:T(8,128)S(1)}, f32[6,17,128]{2,1,0:T(8,128)S(1)}) custom-call(f32[2,9,17,2,128]{4,3,2,1,0:T(2,128)S(1)} %bitcast.6, f32[17,3,128]{2,1,0:T(4,128)S(1)} %bitcast.7, s32[1,64]{1,0:T(1,128)S(1)} %bitcast.8, s32[1,64]{1,0:T(1,128)S(1)} %bitcast.9, f32[1,64]{1,0:T(1,128)S(1)} %bitcast.10), custom_call_target="tpu_custom_call" | custom-call | bytes 313344 | tf_op jit(solution)/shard_map/pallas_call | solution.py:207
  11.6 4.0 %all-to-all-start.1 = ((f32[32,8,128]{2,1,0:T(8,128)}), f32[32,8,128]{2,1,0:T(8,128)S(1)}, u32[]{:S(2)}, u32[]{:S(2)}) async-start(f32[32,8,128]{2,1,0:T(8,128)} %get-tuple-element.43), calls=%async_computation.1 | async-start | bytes 262144 | tf_op jit(solution)/shard_map/all_to_all | solution.py:596
  15.6 0.0 collective-permute-done.refs_1_
  15.6 2.7 %collective-permute-start.9 = (bf16[624,128]{1,0:T(8,128)(2,1)S(1)}, bf16[624,128]{1,0:T(8,128)(2,1)S(1)}, u32[]{:S(2)}, u32[]{:S(2)}) collective-permute-start(bf16[624,128]{1,0:T(8,128)(2,1)S(1)} %get-tuple-element.41), channel_id=1, source_target_pairs={{0,24},{8,16},{16,8},{24,0},{1,25},{9,17},{17,9},{25,1},{2,26},{10... | collective-permute-start | bytes 479240 | tf_op jit(solution)/shard_map/ppermute | solution.py:551
  18.3 0.0 collective-permute-done.1.refs_2_
  18.3 0.0 collective-permute-start.3
  18.3 0.0 collective-permute-done.2.refs_3_
  18.3 0.5 %collective-permute-start.4 = (bf16[624,128]{1,0:T(8,128)(2,1)S(1)}, bf16[624,128]{1,0:T(8,128)(2,1)S(1)}, u32[]{:S(2)}, u32[]{:S(2)}) collective-permute-start(bf16[624,128]{1,0:T(8,128)(2,1)S(1)} %collective-permute-done.refs_1_), channel_id=1, source_target_pairs={{0,4},{4,0},{1,5},{5,1},{2,6},{6,2},{3,7},{7,3},{8,12},{12,8},{9,1... | collective-permute-start | bytes 479240 | tf_op jit(solution)/shard_map/ppermute | solution.py:551
  18.8 0.0 collective-permute-done.7.refs_9_
  18.8 0.1 collective-permute-start.5
  18.9 0.0 collective-permute-done.8.refs_10_
  18.9 0.4 collective-permute-start.6
  19.4 4.8 %collective-permute-done.9.refs_11_ = bf16[624,128]{1,0:T(8,128)(2,1)S(1)} collective-permute-done((bf16[624,128]{1,0:T(8,128)(2,1)S(1)}, bf16[624,128]{1,0:T(8,128)(2,1)S(1)}, u32[]{:S(2)}, u32[]{:S(2)}) %collective-permute-start.9) | collective-permute-done | bytes 159776 | tf_op jit(solution)/shard_map/ppermute | solution.py:551
  24.1 0.0 collective-permute-done.3.refs_4_
  24.1 0.0 collective-permute-done.4.refs_5_
  24.1 0.0 collective-permute-done.5.refs_6_
  24.1 0.0 collective-permute-done.6.refs_7_
  24.1 2.3 %shard_map.107 = f32[32,8,128]{2,1,0:T(8,128)} custom-call(s32[1]{0:T(128)} %bitcast.rank_ref, f32[64,256]{1,0:T(8,128)S(1)} %get-tuple-element.31.table_ref, bf16[624,128]{1,0:T(8,128)(2,1)S(1)} %get-tuple-element.34.refs_0_, bf16[624,128]{1,0:T(8,128)(2,1)S(1)} %collective-permute-done.refs_1_, bf16[624,128]{1,0:T(8,128)(2,1)S(1)} %collective-permute-done.1.refs_2_, ...), custom_call_target="tpu_custom_call" | custom-call | bytes 8388608 | tf_op jit(solution)/shard_map/pallas_call | solution.py:207
  26.4 0.0 copy-start
  26.4 0.0 copy-start.5
  26.4 0.0 all-to-all-done.1.coupling_ref
  26.4 4.6 %all-to-all-start = ((f32[32,8,128]{2,1,0:T(8,128)}), f32[32,8,128]{2,1,0:T(8,128)S(1)}, u32[]{:S(2)}, u32[]{:S(2)}) async-start(f32[32,8,128]{2,1,0:T(8,128)} %shard_map.107), calls=%async_computation | async-start | bytes 262144 | tf_op jit(solution)/shard_map/all_to_all | solution.py:603
  31.1 2.3 %shard_map.109 = (bf16[624,128]{1,0:T(8,128)(2,1)S(1)}, bf16[624,128]{1,0:T(8,128)(2,1)S(1)}, bf16[624,128]{1,0:T(8,128)(2,1)S(1)}, bf16[624,128]{1,0:T(8,128)(2,1)S(1)}) custom-call(s32[1]{0:T(128)} %bitcast.rank_ref, f32[64,256]{1,0:T(8,128)S(1)} %get-tuple-element.31.table_ref, f32[32,8,128]{2,1,0:T(8,128)S(1)} %all-to-all-done.1.coupling_ref, ...), custom_call_target="tpu_custom_call" | custom-call | bytes 8388608 | tf_op jit(solution)/shard_map/pallas_call | solution.py:207
  33.3 1.8 %collective-permute-start.10 = (bf16[624,128]{1,0:T(8,128)(2,1)S(1)}, bf16[624,128]{1,0:T(8,128)(2,1)S(1)}, u32[]{:S(2)}, u32[]{:S(2)}) collective-permute-start(bf16[624,128]{1,0:T(8,128)(2,1)S(1)} %get-tuple-element.46), channel_id=1, source_target_pairs={{0,8},{8,0},{16,24},{24,16},{1,9},{9,1},{17,25},{25,17},{2,10},{10... | collective-permute-start | bytes 479240 | tf_op jit(solution)/shard_map/ppermute | solution.py:551
  35.2 1.5 %collective-permute-start.11 = (bf16[624,128]{1,0:T(8,128)(2,1)S(1)}, bf16[624,128]{1,0:T(8,128)(2,1)S(1)}, u32[]{:S(2)}, u32[]{:S(2)}) collective-permute-start(bf16[624,128]{1,0:T(8,128)(2,1)S(1)} %get-tuple-element.47), channel_id=1, source_target_pairs={{0,16},{8,24},{16,0},{24,8},{1,17},{9,25},{17,1},{25,9},{2,18},{10... | collective-permute-start | bytes 479240 | tf_op jit(solution)/shard_map/ppermute | solution.py:551
  36.6 0.3 collective-permute-start.12
  36.9 2.7 %all-to-all-done.polar_ref = f32[32,8,128]{2,1,0:T(8,128)S(1)} async-done(((f32[32,8,128]{2,1,0:T(8,128)}), f32[32,8,128]{2,1,0:T(8,128)S(1)}, u32[]{:S(2)}, u32[]{:S(2)}) %all-to-all-start) | async-done | bytes 131104 | tf_op jit(solution)/shard_map/all_to_all | solution.py:603
  39.6 0.0 copy-done
  39.6 0.0 copy-done.5
  39.6 5.0 %shard_map.108 = bf16[2,2,384,384]{3,2,1,0:T(8,128)(2,1)} custom-call(f32[32,8,128]{2,1,0:T(8,128)S(1)} %all-to-all-done.polar_ref, bf16[2,2,384,384]{3,2,1,0:T(8,128)(2,1)S(1)} %copy-done, s32[17,128]{1,0:T(8,128)S(1)} %copy-done.5, f32[6,17,128]{2,1,0:T(8,128)S(1)} %get-tuple-element.42.pair_ref), custom_call_target="tpu_custom_call" | custom-call | bytes 20971520 | tf_op jit(solution)/shard_map/pallas_call | solution.py:207
  44.6 0.0 collective-permute-done.10.refs_1_
  44.6 0.3 collective-permute-done.11.refs_2_
  44.8 0.0 collective-permute-done.12.refs_3_
  44.8 0.9 %shard_map.110 = bf16[2,1,2,144,544]{4,3,2,1,0:T(8,128)(2,1)} custom-call(s32[1]{0:T(128)} %bitcast.rank_ref, bf16[624,128]{1,0:T(8,128)(2,1)S(1)} %get-tuple-element.45.refs_0_, bf16[624,128]{1,0:T(8,128)(2,1)S(1)} %collective-permute-done.10.refs_1_, bf16[624,128]{1,0:T(8,128)(2,1)S(1)} %collective-permute-done.11.refs_2_, ...), custom_call_target="tpu_custom_call" | custom-call | bytes 4194304 | tf_op jit(solution)/shard_map/pallas_call | solution.py:207
Async XLA Ops:
  0.6 9.5 %copy-start.8 = (f32[64]{0:T(128)S(1)}, f32[64]{0:T(128)}, u32[]{:S(2)}) copy-start(f32[64]{0:T(128)} %param.17) | copy-start | bytes 772
  0.6 9.5 %copy-start.7 = (s32[64]{0:T(128)S(1)}, s32[64]{0:T(128)}, u32[]{:S(2)}) copy-start(s32[64]{0:T(128)} %param.16) | copy-start | bytes 772
  0.7 9.5 %copy-start.6 = (s32[64]{0:T(128)S(1)}, s32[64]{0:T(128)}, u32[]{:S(2)}) copy-start(s32[64]{0:T(128)} %param.15) | copy-start | bytes 772
  0.7 1.1 %copy-start.1 = (bf16[2,1,2,144,544]{4,3,2,1,0:T(8,128)(2,1)S(1)}, bf16[2,1,2,144,544]{4,3,2,1,0:T(8,128)(2,1)}, u32[]{:S(2)}) copy-start(bf16[2,1,2,144,544]{4,3,2,1,0:T(8,128)(2,1)} %source_ref.1) | copy-start | bytes 1880068
  1.8 4.7 %copy-start.2 = (bf16[2,1,2,144,544]{4,3,2,1,0:T(8,128)(2,1)S(1)}, bf16[2,1,2,144,544]{4,3,2,1,0:T(8,128)(2,1)}, u32[]{:S(2)}) copy-start(bf16[2,1,2,144,544]{4,3,2,1,0:T(8,128)(2,1)} %source_ref.2) | copy-start | bytes 1880068
  1.8 8.4 %copy-start.3 = (f32[2,2,9,17,128]{4,1,3,2,0:T(2,128)S(1)}, f32[2,2,9,17,128]{4,1,3,2,0:T(2,128)}, u32[]{:S(2)}) copy-start(f32[2,2,9,17,128]{4,1,3,2,0:T(2,128)} %param.11) | copy-start | bytes 940036
  1.8 8.4 %copy-start.4 = (f32[3,17,128]{2,0,1:T(4,128)S(1)}, f32[3,17,128]{2,0,1:T(4,128)}, u32[]{:S(2)}) copy-start(f32[3,17,128]{2,0,1:T(4,128)} %param.14) | copy-start | bytes 78340
  1.9 13.7 %collective-permute-start = (bf16[624,128]{1,0:T(8,128)(2,1)S(1)}, bf16[624,128]{1,0:T(8,128)(2,1)S(1)}, u32[]{:S(2)}, u32[]{:S(2)}) collective-permute-start(bf16[624,128]{1,0:T(8,128)(2,1)S(1)} %get-tuple-element.33), channel_id=1, source_target_pairs={{0,8},{8,0},{16,24},{24,16},{1,9},{9,1},{17,25},{25,17},{2,10},{10... | collective-permute-start | bytes 479240 | tf_op jit(solution)/shard_map/ppermute | solution.py:551
  4.9 13.4 %collective-permute-start.1 = (bf16[624,128]{1,0:T(8,128)(2,1)S(1)}, bf16[624,128]{1,0:T(8,128)(2,1)S(1)}, u32[]{:S(2)}, u32[]{:S(2)}) collective-permute-start(bf16[624,128]{1,0:T(8,128)(2,1)S(1)} %get-tuple-element.36), channel_id=1, source_target_pairs={{0,16},{8,24},{16,0},{24,8},{1,17},{9,25},{17,1},{25,9},{2,18},{10... | collective-permute-start | bytes 479240 | tf_op jit(solution)/shard_map/ppermute | solution.py:551
  6.5 11.9 %collective-permute-start.2 = (bf16[624,128]{1,0:T(8,128)(2,1)S(1)}, bf16[624,128]{1,0:T(8,128)(2,1)S(1)}, u32[]{:S(2)}, u32[]{:S(2)}) collective-permute-start(bf16[624,128]{1,0:T(8,128)(2,1)S(1)} %get-tuple-element.37), channel_id=1, source_target_pairs={{0,24},{8,16},{16,8},{24,0},{1,25},{9,17},{17,9},{25,1},{2,26},{10... | collective-permute-start | bytes 479240 | tf_op jit(solution)/shard_map/ppermute | solution.py:551
  6.6 12.2 %collective-permute-start.7 = (bf16[624,128]{1,0:T(8,128)(2,1)S(1)}, bf16[624,128]{1,0:T(8,128)(2,1)S(1)}, u32[]{:S(2)}, u32[]{:S(2)}) collective-permute-start(bf16[624,128]{1,0:T(8,128)(2,1)S(1)} %get-tuple-element.39), channel_id=1, source_target_pairs={{0,8},{8,0},{16,24},{24,16},{1,9},{9,1},{17,25},{25,17},{2,10},{10... | collective-permute-start | bytes 479240 | tf_op jit(solution)/shard_map/ppermute | solution.py:551
  8.6 10.3 %collective-permute-start.8 = (bf16[624,128]{1,0:T(8,128)(2,1)S(1)}, bf16[624,128]{1,0:T(8,128)(2,1)S(1)}, u32[]{:S(2)}, u32[]{:S(2)}) collective-permute-start(bf16[624,128]{1,0:T(8,128)(2,1)S(1)} %get-tuple-element.40), channel_id=1, source_target_pairs={{0,16},{8,24},{16,0},{24,8},{1,17},{9,25},{17,1},{25,9},{2,18},{10... | collective-permute-start | bytes 479240 | tf_op jit(solution)/shard_map/ppermute | solution.py:551
  11.6 14.8 %all-to-all-start.1 = ((f32[32,8,128]{2,1,0:T(8,128)}), f32[32,8,128]{2,1,0:T(8,128)S(1)}, u32[]{:S(2)}, u32[]{:S(2)}) async-start(f32[32,8,128]{2,1,0:T(8,128)} %get-tuple-element.43), calls=%async_computation.1 | async-start | bytes 262144 | tf_op jit(solution)/shard_map/all_to_all | solution.py:596
  15.6 8.5 %collective-permute-start.9 = (bf16[624,128]{1,0:T(8,128)(2,1)S(1)}, bf16[624,128]{1,0:T(8,128)(2,1)S(1)}, u32[]{:S(2)}, u32[]{:S(2)}) collective-permute-start(bf16[624,128]{1,0:T(8,128)(2,1)S(1)} %get-tuple-element.41), channel_id=1, source_target_pairs={{0,24},{8,16},{16,8},{24,0},{1,25},{9,17},{17,9},{25,1},{2,26},{10... | collective-permute-start | bytes 479240 | tf_op jit(solution)/shard_map/ppermute | solution.py:551
  18.3 5.8 %collective-permute-start.3 = (bf16[624,128]{1,0:T(8,128)(2,1)S(1)}, bf16[624,128]{1,0:T(8,128)(2,1)S(1)}, u32[]{:S(2)}, u32[]{:S(2)}) collective-permute-start(bf16[624,128]{1,0:T(8,128)(2,1)S(1)} %get-tuple-element.34.refs_0_), channel_id=1, source_target_pairs={{0,4},{4,0},{1,5},{5,1},{2,6},{6,2},{3,7},{7,3},{8,12},{12,8},{9,1... | collective-permute-start | bytes 479240 | tf_op jit(solution)/shard_map/ppermute | solution.py:551
  18.3 5.8 %collective-permute-start.4 = (bf16[624,128]{1,0:T(8,128)(2,1)S(1)}, bf16[624,128]{1,0:T(8,128)(2,1)S(1)}, u32[]{:S(2)}, u32[]{:S(2)}) collective-permute-start(bf16[624,128]{1,0:T(8,128)(2,1)S(1)} %collective-permute-done.refs_1_), channel_id=1, source_target_pairs={{0,4},{4,0},{1,5},{5,1},{2,6},{6,2},{3,7},{7,3},{8,12},{12,8},{9,1... | collective-permute-start | bytes 479240 | tf_op jit(solution)/shard_map/ppermute | solution.py:551
  18.8 5.3 %collective-permute-start.5 = (bf16[624,128]{1,0:T(8,128)(2,1)S(1)}, bf16[624,128]{1,0:T(8,128)(2,1)S(1)}, u32[]{:S(2)}, u32[]{:S(2)}) collective-permute-start(bf16[624,128]{1,0:T(8,128)(2,1)S(1)} %collective-permute-done.1.refs_2_), channel_id=1, source_target_pairs={{0,4},{4,0},{1,5},{5,1},{2,6},{6,2},{3,7},{7,3},{8,12},{12,8},{9,1... | collective-permute-start | bytes 479240 | tf_op jit(solution)/shard_map/ppermute | solution.py:551
  18.9 5.2 %collective-permute-start.6 = (bf16[624,128]{1,0:T(8,128)(2,1)S(1)}, bf16[624,128]{1,0:T(8,128)(2,1)S(1)}, u32[]{:S(2)}, u32[]{:S(2)}) collective-permute-start(bf16[624,128]{1,0:T(8,128)(2,1)S(1)} %collective-permute-done.2.refs_3_), channel_id=1, source_target_pairs={{0,4},{4,0},{1,5},{5,1},{2,6},{6,2},{3,7},{7,3},{8,12},{12,8},{9,1... | collective-permute-start | bytes 479240 | tf_op jit(solution)/shard_map/ppermute | solution.py:551
  26.4 13.2 %copy-start = (bf16[2,2,384,384]{3,2,1,0:T(8,128)(2,1)S(1)}, bf16[2,2,384,384]{3,2,1,0:T(8,128)(2,1)}, u32[]{:S(2)}) copy-start(bf16[2,2,384,384]{3,2,1,0:T(8,128)(2,1)} %ret_ref.1) | copy-start | bytes 3538948
  26.4 13.2 %copy-start.5 = (s32[17,128]{1,0:T(8,128)S(1)}, s32[17,128]{1,0:T(8,128)}, u32[]{:S(2)}) copy-start(s32[17,128]{1,0:T(8,128)} %near_ref.1) | copy-start | bytes 26116
  26.4 13.1 %all-to-all-start = ((f32[32,8,128]{2,1,0:T(8,128)}), f32[32,8,128]{2,1,0:T(8,128)S(1)}, u32[]{:S(2)}, u32[]{:S(2)}) async-start(f32[32,8,128]{2,1,0:T(8,128)} %shard_map.107), calls=%async_computation | async-start | bytes 262144 | tf_op jit(solution)/shard_map/all_to_all | solution.py:603
  33.3 11.2 %collective-permute-start.10 = (bf16[624,128]{1,0:T(8,128)(2,1)S(1)}, bf16[624,128]{1,0:T(8,128)(2,1)S(1)}, u32[]{:S(2)}, u32[]{:S(2)}) collective-permute-start(bf16[624,128]{1,0:T(8,128)(2,1)S(1)} %get-tuple-element.46), channel_id=1, source_target_pairs={{0,8},{8,0},{16,24},{24,16},{1,9},{9,1},{17,25},{25,17},{2,10},{10... | collective-permute-start | bytes 479240 | tf_op jit(solution)/shard_map/ppermute | solution.py:551
  35.2 9.7 %collective-permute-start.11 = (bf16[624,128]{1,0:T(8,128)(2,1)S(1)}, bf16[624,128]{1,0:T(8,128)(2,1)S(1)}, u32[]{:S(2)}, u32[]{:S(2)}) collective-permute-start(bf16[624,128]{1,0:T(8,128)(2,1)S(1)} %get-tuple-element.47), channel_id=1, source_target_pairs={{0,16},{8,24},{16,0},{24,8},{1,17},{9,25},{17,1},{25,9},{2,18},{10... | collective-permute-start | bytes 479240 | tf_op jit(solution)/shard_map/ppermute | solution.py:551
  36.6 8.2 %collective-permute-start.12 = (bf16[624,128]{1,0:T(8,128)(2,1)S(1)}, bf16[624,128]{1,0:T(8,128)(2,1)S(1)}, u32[]{:S(2)}, u32[]{:S(2)}) collective-permute-start(bf16[624,128]{1,0:T(8,128)(2,1)S(1)} %get-tuple-element.48), channel_id=1, source_target_pairs={{0,24},{8,16},{16,8},{24,0},{1,25},{9,17},{17,9},{25,1},{2,26},{10... | collective-permute-start | bytes 479240 | tf_op jit(solution)/shard_map/ppermute | solution.py:551
